TPU v7x, 256 devices: a whole 4x4x8 slice. The times are simulated.
256 devices in a mesh: expert: 32 (over x, y, core), tensor: 8 (over z).
Axes of the slice: x: 4, y: 4, z: 8, core: 2. Of those that a mesh axis runs over, the one named last changes fastest.
Arguments:
- tokens: bfloat16 [32768, 8192], P(('expert', 'tensor')), may hold values from -6 to 6
- routes: int32 [32768, 2], P(('expert', 'tensor')), may hold values from 0 to 63, all different within a row; in each aligned block of 128 rows (0 to 127, 128 to 255, ...) at most 8 rows name the same one
- route_weight: float32 [32768, 2], P(('expert', 'tensor')), may hold values from 0.1 to 1
- shrink_weight: bfloat16 [64, 32, 8192], P('expert'), may hold values from -0.0625 to 0.0625
- expand_weight: bfloat16 [64, 32, 8192], P('expert', None, 'tensor'), may hold values from -1 to 1
Outputs:
- adapted: bfloat16 [32768, 8192], P(('expert', 'tensor'))
Inputs may be any that keep to these rules, and one draw needn't show every extreme that they name: `routes`: in each aligned block of 128 rows (the tokens of one device) a row names two different experts and no expert is named by more than 8 rows; in every draw some expert is named by exactly 8 rows of some block.
All inputs are finite; a program needn't handle non-finite values.
Results may differ from a plain program's by a relative error of at most 0.0058.
Values may be sent and summed in bfloat16 or wider, within the bound.
No kernel may reach another device: no remote copies, remote signals or barrier semaphores. Data moves between devices by JAX's collectives and lax.ppermute only.
A program may use at most 128 MiB of HBM per device.

v0:
```python
import jax
import jax.numpy as jnp
from jax import lax
from jax.sharding import PartitionSpec as P

EXPERTS = 64
CAP = 8


def per_device(tokens, routes, route_weight, shrink_weight, expand_weight):
    tok_rows, features = tokens.shape
    owners = lax.axis_size("expert")
    local_count = shrink_weight.shape[0]
    flat_routes = routes.reshape(-1)
    one_hot = (flat_routes[:, None] == jnp.arange(EXPERTS, dtype=jnp.int32)[None, :]).astype(
        jnp.int32
    )
    slot_index = jnp.sum((jnp.cumsum(one_hot, axis=0) - one_hot) * one_hot, axis=1)
    destination = flat_routes * CAP + slot_index
    token_rows = jnp.repeat(tokens, 2, axis=0)
    outgoing = jnp.zeros((EXPERTS * CAP, features), tokens.dtype).at[destination].set(token_rows)
    outgoing = outgoing.reshape(owners, local_count * CAP, features)
    arrived = lax.all_to_all(outgoing, "expert", split_axis=0, concat_axis=0, tiled=True)
    arrived = arrived.reshape(owners, local_count, CAP, features)
    shrunk = jnp.einsum(
        "sjcd,jrd->sjcr", arrived, shrink_weight, preferred_element_type=jnp.float32
    ).astype(jnp.bfloat16)
    columns = jnp.einsum(
        "sjcr,jrd->sjcd",
        lax.all_gather(shrunk, "tensor", axis=0, tiled=True),
        expand_weight,
        preferred_element_type=jnp.float32,
    ).astype(jnp.bfloat16)
    expanded = lax.all_to_all(columns, "tensor", split_axis=0, concat_axis=3, tiled=True)
    returned = lax.all_to_all(
        expanded.reshape(owners, local_count * CAP, features),
        "expert",
        split_axis=0,
        concat_axis=0,
        tiled=True,
    )
    returned = returned.reshape(EXPERTS * CAP, features)
    picked = jnp.take(returned, destination, axis=0).reshape(tok_rows, 2, features)
    mixed = (
        picked[:, 0, :].astype(jnp.float32) * route_weight[:, 0:1]
        + picked[:, 1, :].astype(jnp.float32) * route_weight[:, 1:2]
    )
    return mixed.astype(jnp.bfloat16)


def solution(mesh):
    return jax.shard_map(
        per_device,
        mesh=mesh,
        in_specs=(
            P(("expert", "tensor"), None),
            P(("expert", "tensor"), None),
            P(("expert", "tensor"), None),
            P("expert", None, None),
            P("expert", None, "tensor"),
        ),
        out_specs=P(("expert", "tensor"), None),
        check_vma=False,
    )
```

profile of v0, /device:TPU:8, one launch (start us, length us, event | category | flops | bytes accessed | tf_op | source)
XLA Modules:
  0.0 559.1 jit_solution(2721371778995773595)
XLA Ops:
  0.0 0.9 copy.33
  0.9 0.1 eq.26
  1.0 0.1 reshape.82
  1.2 0.7 broadcast_multiply_fusion
  1.9 0.6 reduce-window.6
  2.5 0.2 slice_reduce_fusion
  2.8 0.1 mul.45
  3.0 5.8 %broadcast_in_dim.20 = bf16[128,2,8192]{2,1,0:T(2,128)(2,1)} broadcast(bf16[128,8192]{1,0:T(8,128)(2,1)} %param.5), dimensions={0,2} | broadcast | bytes 6291456 | tf_op jit(solution)/shard_map/broadcast_in_dim | solution.py:20
  8.7 7.2 %reshape.103 = bf16[256,8192]{1,0:T(8,128)(2,1)} reshape(bf16[128,2,8192]{2,1,0:T(2,128)(2,1)} %broadcast_in_dim.20) | data formatting | bytes 8388608 | tf_op jit(solution)/shard_map/reshape | solution.py:20
  16.1 12.3 %scatter_custom_fusion = bf16[512,8192]{1,0:T(8,128)(2,1)} fusion(s32[256]{0:T(256)S(1)} %bitcast.65, bf16[256,8192]{1,0:T(8,128)(2,1)} %reshape.103, bf16[]{:T(256)} %constant.25.clone.1), kind=kCustom, calls=%fused_computation.11 | custom fusion | bytes 8389120 | tf_op jit(solution)/shard_map/scatter | solution.py:21
  28.4 101.9 %all_to_all.25 = bf16[32,16,8192]{2,1,0:T(8,128)(2,1)S(1)} all-to-all(bf16[32,16,8192]{2,1,0:T(8,128)(2,1)} %bitcast.61), channel_id=1, replica_groups=mesh['expert'=32,'tensor'=8] {'expert'}, dimensions={0} | all-to-all | bytes 16777216 | tf_op jit(solution)/shard_map/all_to_all | solution.py:23
  130.3 2.3 fusion.9
  132.6 30.6 %all_gather.3 = bf16[256,2,8,32]{3,2,0,1:T(8,128)(2,1)S(1)} all-gather(bf16[32,2,8,32]{3,2,0,1:T(8,128)(2,1)S(1)} %fusion.9), channel_id=1, replica_groups=mesh['expert'=32,'tensor'=8] {'tensor'}, dimensions={0}, use_global_device_ids=true | all-gather | bytes 294912 | tf_op jit(solution)/shard_map/all_gather | solution.py:30
  163.2 5.5 convert_bitcast_fusion
  168.7 11.3 %copy.40 = bf16[256,2,8,1024]{3,2,1,0:T(8,128)(2,1)} copy(bf16[256,2,8,1024]{3,0,2,1:T(8,128)(2,1)} %convert_bitcast_fusion) | data formatting | bytes 16777216 | tf_op jit(solution)/shard_map/convert_element_type | solution.py:33
  180.0 186.3 %all_to_all.26 = bf16[256,2,8,1024]{3,2,1,0:T(8,128)(2,1)} all-to-all(bf16[256,2,8,1024]{3,2,1,0:T(8,128)(2,1)} %copy.40), channel_id=1, replica_groups=mesh['expert'=32,'tensor'=8] {'tensor'}, dimensions={0} | all-to-all | bytes 16777216 | tf_op jit(solution)/shard_map/all_to_all | solution.py:34
  366.4 16.7 %copy.57 = bf16[8,32,2,8,1024]{4,0,3,2,1:T(8,128)(2,1)} copy(bf16[8,32,2,8,1024]{4,3,2,1,0:T(8,128)(2,1)} %bitcast.62) | data formatting | bytes 16777216 | tf_op jit(solution)/shard_map/all_to_all | solution.py:34
  383.1 13.5 %reshape.87 = bf16[32,16,8192]{2,1,0:T(8,128)(2,1)} reshape(bf16[32,2,8,8,1024]{4,3,2,1,0:T(8,128)(2,1)} %bitcast.63) | data formatting | bytes 16777216 | tf_op jit(solution)/shard_map/reshape | solution.py:36
  396.6 7.6 %all-to-all-start.2 = ((bf16[32,16,8192]{2,1,0:T(8,128)(2,1)}), bf16[32,16,8192]{2,1,0:T(8,128)(2,1)}, u32[]{:S(2)}, u32[]{:S(2)}) async-start(bf16[32,16,8192]{2,1,0:T(8,128)(2,1)} %reshape.87), calls=%async_computation.2 | async-start | bytes 16777216 | tf_op jit(solution)/shard_map/all_to_all | solution.py:35
  404.5 123.4 %all-to-all-done.2 = bf16[32,16,8192]{2,1,0:T(8,128)(2,1)} async-done(((bf16[32,16,8192]{2,1,0:T(8,128)(2,1)}), bf16[32,16,8192]{2,1,0:T(8,128)(2,1)}, u32[]{:S(2)}, u32[]{:S(2)}) %all-to-all-start.2) | async-done | bytes 8388640 | tf_op jit(solution)/shard_map/all_to_all | solution.py:35
  527.9 13.4 %gather_fusion = bf16[256,8192]{1,0:T(8,128)(2,1)} fusion(bf16[512,8192]{1,0:T(8,128)(2,1)} %bitcast.13, s32[1024]{0:T(1024)S(1)} %pad_clamp_fusion), kind=kCustom, calls=%fused_computation | custom fusion | bytes 8389632 | tf_op jit(solution)/shard_map/jit(_take)/gather | solution.py:43
  541.3 7.9 %gather.7 = bf16[128,2,8192]{2,1,0:T(2,128)(2,1)} reshape(bf16[256,8192]{1,0:T(8,128)(2,1)} %gather_fusion) | data formatting | bytes 8388608 | tf_op jit(solution)/shard_map/jit(_take)/gather | solution.py:43
  549.2 7.1 %copy_select_fusion = bf16[128,2,8192]{2,0,1:T(8,128)(2,1)S(1)} fusion(bf16[128,2,8192]{2,1,0:T(2,128)(2,1)} %gather.7, pred[128,2]{0,1:T(4,128)(4,1)S(1)} %compare_and_fusion), kind=kLoop, calls=%fused_computation.10 | loop fusion | flops 2097152 | bytes 8388864 | tf_op jit(solution)/shard_map/jit(_take)/select_n | solution.py:43
  556.4 2.2 fusion.3
  (21 shorter events, 0.5 us)
Async XLA Ops:
  0.0 130.3 %copy-start = (bf16[2,32,8192]{2,1,0:T(8,128)(2,1)S(1)}, bf16[2,32,8192]{2,1,0:T(8,128)(2,1)}, u32[]{:S(2)}) copy-start(bf16[2,32,8192]{2,1,0:T(8,128)(2,1)} %param.8) | copy-start | bytes 3145732
  130.3 32.9 %copy-start.2 = (bf16[2,32,1024]{2,1,0:T(8,128)(2,1)S(1)}, bf16[2,32,1024]{2,1,0:T(8,128)(2,1)}, u32[]{:S(2)}) copy-start(bf16[2,32,1024]{2,1,0:T(8,128)(2,1)} %param.9) | copy-start | bytes 393220
  396.6 7.8 %copy-start.4 = (f32[128,2]{0,1:T(2,128)S(1)}, f32[128,2]{0,1:T(2,128)}, u32[]{:S(2)}) copy-start(f32[128,2]{0,1:T(2,128)} %param.7) | copy-start | bytes 3076
  396.6 7.8 %copy-start.3 = (s32[128,2]{0,1:T(2,128)S(1)}, s32[128,2]{0,1:T(2,128)}, u32[]{:S(2)}) copy-start(s32[128,2]{0,1:T(2,128)} %param.6) | copy-start | bytes 3076
  396.6 131.3 %all-to-all-start.2 = ((bf16[32,16,8192]{2,1,0:T(8,128)(2,1)}), bf16[32,16,8192]{2,1,0:T(8,128)(2,1)}, u32[]{:S(2)}, u32[]{:S(2)}) async-start(bf16[32,16,8192]{2,1,0:T(8,128)(2,1)} %reshape.87), calls=%async_computation.2 | async-start | bytes 16777216 | tf_op jit(solution)/shard_map/all_to_all | solution.py:35
  549.2 9.4 %copy-start.1 = (bf16[2,32,8192]{2,1,0:T(8,128)(2,1)S(1)}, bf16[2,32,8192]{2,1,0:T(8,128)(2,1)}, u32[]{:S(2)}) copy-start(bf16[2,32,8192]{2,1,0:T(8,128)(2,1)} %param.8) | copy-start | bytes 3145732
where the time goes:
time: 568 us; the launch traced here: 559 us
  blocking collectives  319 us (56%)
  waiting for transfers between devices  123 us (22%)
  local copies, waits for them, and re-layouts  90 us (16%)
  other arithmetic  10.8 us (2%)
  matrix products  7.84 us (1%)
  starting transfers between devices  7.59 us (1%)
    all_to_all x1, blocking collectives, per_device(): lax.all_to_all(columns, 'tensor', split_axis=0, concat_axis=3, tiled=True)  186 us
    all_to_all x1, waiting for transfers between devices, per_device(): lax.all_to_all(expanded.reshape(owners, local_count * CAP, features), 'ex...  123 us
    all_to_all x1, blocking collectives, per_device(): lax.all_to_all(outgoing, 'expert', split_axis=0, concat_axis=0, tiled=True)  102 us
    all_gather x1, blocking collectives, per_device(): lax.all_gather(shrunk, 'tensor', axis=0, tiled=True)  30.6 us
    gather x2, local copies, waits for them, and re-layouts, per_device(): jnp.take(returned, destination, axis=0).reshape(tok_rows, 2, features)  21.3 us
    all_to_all x1, local copies, waits for them, and re-layouts, per_device(): lax.all_to_all(columns, 'tensor', split_axis=0, concat_axis=3, tiled=True)  16.7 us
    reshape x1, local copies, waits for them, and re-layouts, per_device(): expanded.reshape(owners, local_count * CAP, features)  13.5 us
    scatter x1, local copies, waits for them, and re-layouts, per_device(): jnp.zeros((EXPERTS * CAP, features), tokens.dtype).at[destination]  12.3 us
  transfers between devices with their start and end apart: 1, of which 1 were waited for; matrix products, arithmetic and copies ran while one was open for 0% of the time, Pallas kernels for 0%

commit v1 on v0

v1 whole, which is shorter than its diff:
```python
import functools

import jax
import jax.numpy as jnp
from jax import lax
from jax.experimental import pallas as pl
from jax.experimental.pallas import tpu as pltpu
from jax.sharding import PartitionSpec as P

BF16 = jnp.bfloat16
F32 = jnp.float32
ANY = pl.BlockSpec(memory_space=pl.ANY)
NT = (((1,), (1,)), ((), ()))
TN = (((0,), (0,)), ((), ()))


def params(mib=48):
    return pltpu.CompilerParams(vmem_limit_bytes=mib * 1024 * 1024)


def pack_kernel(peers, toks, rows, width, tokens_ref, weight_ref, out_ref, sems):
    copies = []
    for p in range(peers):
        cols = pl.ds(p * width, width)
        copies.append(
            pltpu.make_async_copy(tokens_ref.at[:, cols], out_ref.at[p, pl.ds(0, toks)], sems.at[0, p])
        )
        copies.append(
            pltpu.make_async_copy(weight_ref.at[:, cols], out_ref.at[p, pl.ds(toks, rows)], sems.at[1, p])
        )
    for c in copies:
        c.start()
    for c in copies:
        c.wait()


def pack(tokens, weight, peers):
    toks, d = tokens.shape
    rows = weight.shape[0]
    width = d // peers
    return pl.pallas_call(
        functools.partial(pack_kernel, peers, toks, rows, width),
        out_shape=jax.ShapeDtypeStruct((peers, toks + rows, width), tokens.dtype),
        in_specs=[ANY, ANY],
        out_specs=ANY,
        scratch_shapes=[pltpu.SemaphoreType.DMA((2, peers))],
        name="pack",
    )(tokens, weight)


def shrink_kernel(group, rank, x_ref, w_ref, r_ref, out_ref):
    peers, wrows, width = w_ref.shape
    toks = x_ref.shape[1]
    chunk = max(1, 256 // wrows)
    per = chunk * wrows // rank

    @pl.loop(0, group // 2)
    def _(g):
        x = x_ref[pl.ds(2 * g, 2)].reshape(2 * toks, width)
        routes = [[r_ref[2 * g + b, pl.ds(k, 1), :] for k in range(2)] for b in range(2)]
        acc = [[jnp.zeros((rank, toks), F32) for _ in range(2)] for _ in range(2)]
        for c in range(peers // chunk):
            w = w_ref[c * chunk : (c + 1) * chunk].reshape(chunk * wrows, width)
            p = lax.dot_general(w, x, NT, preferred_element_type=F32)
            for j in range(per):
                e = c * per + j
                for b in range(2):
                    piece = p[j * rank : (j + 1) * rank, b * toks : (b + 1) * toks]
                    for k in range(2):
                        acc[b][k] = jnp.where(routes[b][k] == e, piece, acc[b][k])
        for b in range(2):
            for k in range(2):
                out_ref[2 * g + b, pl.ds(k * rank, rank), :] = acc[b][k].astype(out_ref.dtype)


def shrink(buf, routes, toks, rank, group):
    peers, total, width = buf.shape
    wrows = total - toks
    return pl.pallas_call(
        functools.partial(shrink_kernel, group, rank),
        grid=(peers // group,),
        out_shape=jax.ShapeDtypeStruct((peers, 2 * rank, toks), F32),
        in_specs=[
            pl.BlockSpec((group, toks, width), lambda i: (i, 0, 0)),
            pl.BlockSpec((peers, wrows, width), lambda i: (0, toks // wrows, 0)),
            pl.BlockSpec((group, 2, toks), lambda i: (i, 0, 0)),
        ],
        out_specs=pl.BlockSpec((group, 2 * rank, toks), lambda i: (i, 0, 0)),
        compiler_params=params(),
        name="shrink",
    )(buf, buf, routes)


def combine_kernel(peers, per_block, rank, toks, part_ref, gate_ref, weight_ref, out_ref, s_ref, sems):
    wrows = weight_ref.shape[1]
    width = out_ref.shape[2]
    copies = []
    for p in range(peers):
        z, q = p // per_block, p % per_block
        copies.append(
            pltpu.make_async_copy(
                weight_ref.at[z, :, pl.ds(q * width, width)], out_ref.at[p, pl.ds(0, wrows)], sems.at[0, p]
            )
        )
    for c in copies:
        c.start()
    for k in range(2):
        total = jnp.sum(part_ref[:, pl.ds(k * rank, rank), :], axis=0)
        gated = total.astype(BF16).astype(F32) * gate_ref[pl.ds(k, 1), :]
        s_ref[:, pl.ds(k * toks, toks)] = gated.astype(BF16)
    sends = []
    for p in range(peers):
        sends.append(pltpu.make_async_copy(s_ref, out_ref.at[p, pl.ds(wrows, rank)], sems.at[1, p]))
    for c in sends:
        c.start()
    for c in copies + sends:
        c.wait()


def combine(part, gates, weight):
    peers, rank2, toks = part.shape
    rank = rank2 // 2
    blocks, wrows, cols = weight.shape
    per_block = peers // blocks
    width = cols // per_block
    return pl.pallas_call(
        functools.partial(combine_kernel, peers, per_block, rank, toks),
        out_shape=jax.ShapeDtypeStruct((peers, wrows + rank, width), BF16),
        in_specs=[pl.BlockSpec(memory_space=pltpu.VMEM), pl.BlockSpec(memory_space=pltpu.VMEM), ANY],
        out_specs=ANY,
        scratch_shapes=[pltpu.VMEM((rank, 2 * toks), BF16), pltpu.SemaphoreType.DMA((2, peers))],
        compiler_params=params(),
        name="combine",
    )(part, gates, weight)


def expand_kernel(group, s_ref, w_ref, r_ref, out_ref, a_ref):
    peers, wrows, width = w_ref.shape
    rank = s_ref.shape[1]
    toks = s_ref.shape[2] // 2
    lanes = 128
    per = lanes // rank
    tiles = peers * wrows // lanes
    src = lax.broadcasted_iota(jnp.int32, (4 * rank, 4 * lanes), 0)
    dst = lax.broadcasted_iota(jnp.int32, (4 * rank, 4 * lanes), 1)
    spread = (src == (dst // lanes) * rank + dst % rank).astype(F32).astype(BF16)
    lane_expert = (lax.broadcasted_iota(jnp.int32, (toks, lanes), 1) // rank).astype(F32)
    zero = jnp.zeros((toks, lanes), BF16)

    @pl.loop(0, group)
    def _(b):
        s = s_ref[b].astype(F32)
        r = r_ref[b].astype(F32)
        rows = jnp.concatenate(
            [s[:, :toks], s[:, toks:]] + [jnp.broadcast_to(r[k : k + 1], (rank, toks)) for k in range(2)], axis=0
        ).astype(BF16)
        t = lax.dot_general(rows, spread, TN, preferred_element_type=F32)
        s0 = t[:, :lanes].astype(BF16)
        s1 = t[:, lanes : 2 * lanes].astype(BF16)
        d0 = (t[:, 2 * lanes : 3 * lanes] - lane_expert).astype(BF16)
        d1 = (t[:, 3 * lanes :] - lane_expert).astype(BF16)
        for j in range(tiles):
            e = jnp.asarray(j * per, BF16)
            a = jnp.where(d0 == e, s0, jnp.where(d1 == e, s1, zero))
            a_ref[pl.ds(pl.multiple_of(b * toks, toks), toks), j * lanes : (j + 1) * lanes] = a

    w = w_ref[...].reshape(peers * wrows, width)
    out = jnp.dot(a_ref[...], w, preferred_element_type=F32)
    out_ref[...] = out.astype(BF16).reshape(group, toks, width)


def expand(buf, routes, rank, group):
    peers, total, width = buf.shape
    wrows = total - rank
    toks = routes.shape[2]
    return pl.pallas_call(
        functools.partial(expand_kernel, group),
        grid=(peers // group,),
        out_shape=jax.ShapeDtypeStruct((peers, toks, width), BF16),
        in_specs=[
            pl.BlockSpec((group, rank, width), lambda i: (i, wrows // rank, 0)),
            pl.BlockSpec((peers, wrows, width), lambda i: (0, 0, 0)),
            pl.BlockSpec((group, 2, toks), lambda i: (i, 0, 0)),
        ],
        out_specs=pl.BlockSpec((group, toks, width), lambda i: (i, 0, 0)),
        scratch_shapes=[pltpu.VMEM((group * toks, peers * wrows), BF16)],
        compiler_params=params(),
        name="expand",
    )(buf, buf, routes)


def unpack_kernel(peers, width, in_ref, out_ref, sems):
    copies = [
        pltpu.make_async_copy(in_ref.at[p], out_ref.at[:, pl.ds(p * width, width)], sems.at[p]) for p in range(peers)
    ]
    for c in copies:
        c.start()
    for c in copies:
        c.wait()


def unpack(buf):
    peers, toks, width = buf.shape
    return pl.pallas_call(
        functools.partial(unpack_kernel, peers, width),
        out_shape=jax.ShapeDtypeStruct((toks, peers * width), buf.dtype),
        in_specs=[ANY],
        out_specs=ANY,
        scratch_shapes=[pltpu.SemaphoreType.DMA((peers,))],
        name="unpack",
    )(buf)


def swap(x):
    return lax.all_to_all(x, "expert", split_axis=0, concat_axis=0, tiled=True)


def per_device(tokens, routes, route_weight, shrink_weight, expand_weight):
    toks, _ = tokens.shape
    local, rank, _ = shrink_weight.shape
    peers = lax.axis_size("expert")
    rows = local * rank
    group = min(8, peers)
    all_routes = lax.all_gather(routes.T, "expert", axis=0)
    all_expand = lax.all_gather(expand_weight.reshape(rows, -1), "tensor", axis=0)
    arrived = swap(pack(tokens, shrink_weight.reshape(rows, -1), peers))
    partial = shrink(arrived, all_routes, toks, rank, group)
    packed = swap(combine(swap(partial), route_weight.T, all_expand))
    columns = expand(packed, all_routes, rank, group)
    return unpack(swap(columns))


def solution(mesh):
    return jax.shard_map(
        per_device,
        mesh=mesh,
        in_specs=(
            P(("expert", "tensor"), None),
            P(("expert", "tensor"), None),
            P(("expert", "tensor"), None),
            P("expert", None, None),
            P("expert", None, "tensor"),
        ),
        out_specs=P(("expert", "tensor"), None),
        check_vma=False,
    )
```

time: 568 us -> 348 us (0.61); the launches traced: 559 us -> 345 us
  blocking collectives: 319 us -> 111 us
  Pallas kernels: 0 us -> 189 us
  waiting for transfers between devices: 123 us -> 16.2 us
  local copies, waits for them, and re-layouts: 90 us -> 2.2 us
  between operations: 0.61 us -> 13.5 us
  other arithmetic: 10.8 us -> 0 us
  matrix products: 7.84 us -> 0 us
  starting transfers between devices: 7.59 us -> 13.3 us
    all_to_all x2, blocking collectives: 288 us -> 58.3 us  [swap(): return lax.all_to_all(x, 'expert', split_axis=0, concat_axis=0, tiled=True)]
    pallas_call x0 -> x5, Pallas kernels: none -> 189 us  [the longest x1 97 us: pack(): pl.pallas_call(functools.partial(pack_kernel, peers, toks, rows, width),...]
    all_to_all x1 -> x2, waiting for transfers between devices: 123 us -> 15.5 us  [swap(): return lax.all_to_all(x, 'expert', split_axis=0, concat_axis=0, tiled=True)]
    all_gather x1, blocking collectives: 30.6 us -> 53.2 us  [per_device(): all_routes = lax.all_gather(routes.T, 'expert', axis=0)]
    gather x2 -> x0, local copies, waits for them, and re-layouts: 21.3 us -> none  [per_device(): jnp.take(returned, destination, axis=0).reshape(tok_rows, 2, features)]
    reshape x3 -> x0, local copies, waits for them, and re-layouts: 20.8 us -> none  [the longest x1 13.5 us: per_device(): expanded.reshape(owners, local_count * CAP, features)]
    all_to_all x1 -> x0, local copies, waits for them, and re-layouts: 16.7 us -> none  [per_device(): lax.all_to_all(columns, 'tensor', split_axis=0, concat_axis=3, tiled=True)]
    scatter x1 -> x0, local copies, waits for them, and re-layouts: 12.3 us -> none  [per_device(): jnp.zeros((EXPERTS * CAP, features), tokens.dtype).at[destination]]
  transfers between devices with their start and end apart: 1 -> 3, of which waited for: 1 -> 1; matrix products, arithmetic and copies ran while one was open for 0% -> 0% of each run, Pallas kernels for 0% -> 3%
where the time goes in v1:
time: 348 us; the launch traced here: 345 us
  Pallas kernels  189 us (54%)
  blocking collectives  111 us (32%)
  waiting for transfers between devices  16.2 us (5%)
  between operations  13.5 us (4%)
  starting transfers between devices  13.3 us (4%)
    pallas_call x1, Pallas kernels, pack(): pl.pallas_call(functools.partial(pack_kernel, peers, toks, rows, width),...  97 us
    pallas_call x1, Pallas kernels, unpack(): pl.pallas_call(functools.partial(unpack_kernel, peers, width), out_shape=...  64.9 us
    all_to_all x2, blocking collectives, swap(): return lax.all_to_all(x, 'expert', split_axis=0, concat_axis=0, tiled=True)  58.3 us
    all_gather x1, blocking collectives, per_device(): all_routes = lax.all_gather(routes.T, 'expert', axis=0)  53.2 us
    all_to_all x2, waiting for transfers between devices, swap(): return lax.all_to_all(x, 'expert', split_axis=0, concat_axis=0, tiled=True)  15.5 us
    pallas_call x1, Pallas kernels, expand(): pl.pallas_call(functools.partial(expand_kernel, group), grid=(peers // gr...  15.2 us
    all_to_all x2, starting transfers between devices, swap(): return lax.all_to_all(x, 'expert', split_axis=0, concat_axis=0, tiled=True)  13.3 us
    pallas_call x1, Pallas kernels, shrink(): pl.pallas_call(functools.partial(shrink_kernel, group, rank), grid=(peers...  9.83 us
  transfers between devices with their start and end apart: 3, of which 1 were waited for; matrix products, arithmetic and copies ran while one was open for 0% of the time, Pallas kernels for 3%

profile of v1, /device:TPU:8, one launch (start us, length us, event | category | flops | bytes accessed | tf_op | source)
XLA Modules:
  0.0 345.2 jit_solution(6067562845040390300)
XLA Ops:
  6.5 97.0 %pack.1 = bf16[32,192,256]{2,1,0:T(8,128)(2,1)} custom-call(bf16[128,8192]{1,0:T(8,128)(2,1)} %tokens_ref.1, bf16[64,8192]{1,0:T(8,128)(2,1)} %bitcast.7), custom_call_target="tpu_custom_call" | custom-call | tf_op jit(solution)/shard_map/pack/pallas_call | solution.py:41
  103.5 0.0 copy-start.3
  103.5 7.5 %all-to-all-start = ((bf16[32,192,256]{2,1,0:T(8,128)(2,1)}), bf16[32,192,256]{2,1,0:T(8,128)(2,1)S(1)}, u32[]{:S(2)}, u32[]{:S(2)}) async-start(bf16[32,192,256]{2,1,0:T(8,128)(2,1)} %pack.1), calls=%async_computation | async-start | bytes 6291456 | tf_op jit(solution)/shard_map/all_to_all | solution.py:215
  111.1 0.0 all-gather.4.cloned.1.call-start
  111.1 0.7 all-gather.4.cloned.1.call-update
  111.8 0.0 copy-done.3
  111.8 53.2 %all-gather.1.r_ref = s32[32,2,128]{2,1,0:T(2,128)S(1)} all-gather(s32[1,2,128]{2,1,0:T(2,128)S(1)} %bitcast.9), channel_id=2, replica_groups=mesh['expert'=32,'tensor'=8] {'expert'}, dimensions={0}, use_global_device_ids=true | all-gather | bytes 33792 | tf_op jit(solution)/shard_map/all_gather | solution.py:224
  165.0 0.0 all-to-all-done.x_ref.w_ref
  165.0 9.8 %shrink.1 = f32[32,64,128]{2,1,0:T(8,128)S(1)} custom-call(bf16[32,192,256]{2,1,0:T(8,128)(2,1)S(1)} %all-to-all-done.x_ref.w_ref, bf16[32,192,256]{2,1,0:T(8,128)(2,1)S(1)} %all-to-all-done.x_ref.w_ref, s32[32,2,128]{2,1,0:T(2,128)S(1)} %all-gather.1.r_ref), custom_call_target="tpu_custom_call" | custom-call | tf_op jit(solution)/shard_map/shrink/pallas_call | solution.py:79
  174.8 0.0 copy-start
  174.8 1.0 copy-done
  175.8 0.0 copy-start.2
  175.8 5.7 %all-to-all-start.1 = ((f32[32,64,128]{2,1,0:T(8,128)}), f32[32,64,128]{2,1,0:T(8,128)S(1)}, u32[]{:S(2)}, u32[]{:S(2)}) async-start(f32[32,64,128]{2,1,0:T(8,128)} %copy-done), calls=%async_computation.1 | async-start | bytes 2097152 | tf_op jit(solution)/shard_map/all_to_all | solution.py:215
  181.5 0.0 all-gather.4.cloned.1.call-done.weight_ref
  181.5 15.5 %all-to-all-done.1.part_ref = f32[32,64,128]{2,1,0:T(8,128)S(1)} async-done(((f32[32,64,128]{2,1,0:T(8,128)}), f32[32,64,128]{2,1,0:T(8,128)S(1)}, u32[]{:S(2)}, u32[]{:S(2)}) %all-to-all-start.1) | async-done | bytes 1048608 | tf_op jit(solution)/shard_map/all_to_all | solution.py:215
  197.1 0.0 copy-done.2
  197.1 0.0 copy-start.1
  197.1 1.2 copy-done.1
  198.3 1.6 combine.1
  199.9 26.5 %all_to_all.20.s_ref.w_ref = bf16[32,96,256]{2,1,0:T(8,128)(2,1)S(1)} all-to-all(bf16[32,96,256]{2,1,0:T(8,128)(2,1)S(1)} %combine.1), channel_id=1, replica_groups=mesh['expert'=32,'tensor'=8] {'expert'}, dimensions={0} | all-to-all | bytes 3145728 | tf_op jit(solution)/shard_map/all_to_all | solution.py:215
  226.4 15.2 %expand.1 = bf16[32,128,256]{2,1,0:T(8,128)(2,1)S(1)} custom-call(bf16[32,96,256]{2,1,0:T(8,128)(2,1)S(1)} %all_to_all.20.s_ref.w_ref, bf16[32,96,256]{2,1,0:T(8,128)(2,1)S(1)} %all_to_all.20.s_ref.w_ref, s32[32,2,128]{2,1,0:T(2,128)S(1)} %all-gather.1.r_ref), custom_call_target="tpu_custom_call" | custom-call | tf_op jit(solution)/shard_map/expand/pallas_call | solution.py:176
  241.6 31.8 %all_to_all.21.in_ref = bf16[32,128,256]{2,1,0:T(8,128)(2,1)} all-to-all(bf16[32,128,256]{2,1,0:T(8,128)(2,1)S(1)} %expand.1), channel_id=1, replica_groups=mesh['expert'=32,'tensor'=8] {'expert'}, dimensions={0} | all-to-all | bytes 4194304 | tf_op jit(solution)/shard_map/all_to_all | solution.py:215
  273.4 64.9 %unpack.1 = bf16[128,8192]{1,0:T(8,128)(2,1)} custom-call(bf16[32,128,256]{2,1,0:T(8,128)(2,1)} %all_to_all.21.in_ref), custom_call_target="tpu_custom_call" | custom-call | tf_op jit(solution)/shard_map/unpack/pallas_call | solution.py:204
Async XLA Ops:
  103.5 8.3 %copy-start.3 = (s32[128,2]{0,1:T(2,128)S(1)}, s32[128,2]{0,1:T(2,128)}, u32[]{:S(2)}) copy-start(s32[128,2]{0,1:T(2,128)} %param.6) | copy-start | bytes 3076
  103.5 61.5 %all-to-all-start = ((bf16[32,192,256]{2,1,0:T(8,128)(2,1)}), bf16[32,192,256]{2,1,0:T(8,128)(2,1)S(1)}, u32[]{:S(2)}, u32[]{:S(2)}) async-start(bf16[32,192,256]{2,1,0:T(8,128)(2,1)} %pack.1), calls=%async_computation | async-start | bytes 6291456 | tf_op jit(solution)/shard_map/all_to_all | solution.py:215
  111.1 70.5 %all-gather.4.cloned.1.call-start = ((), (), s32[]{:S(2)}) async-start(), calls=%async_computation.4 | async-start | bytes 1179648 | tf_op jit(solution)/shard_map/all_gather | solution.py:225
  174.8 1.0 copy-start
  175.8 21.3 %copy-start.2 = (f32[128,2]{0,1:T(2,128)S(1)}, f32[128,2]{0,1:T(2,128)}, u32[]{:S(2)}) copy-start(f32[128,2]{0,1:T(2,128)} %param.7) | copy-start | bytes 3076
  175.8 21.3 %all-to-all-start.1 = ((f32[32,64,128]{2,1,0:T(8,128)}), f32[32,64,128]{2,1,0:T(8,128)S(1)}, u32[]{:S(2)}, u32[]{:S(2)}) async-start(f32[32,64,128]{2,1,0:T(8,128)} %copy-done), calls=%async_computation.1 | async-start | bytes 2097152 | tf_op jit(solution)/shard_map/all_to_all | solution.py:215
  197.1 1.2 copy-start.1
Sparse Core Ops, SparseCore 0:
  113.7 41.2 all-gather.3

commit v2 on v1

--- a/solution.py
+++ b/solution.py
@@ -10,6 +10,7 @@
 BF16 = jnp.bfloat16
 F32 = jnp.float32
 ANY = pl.BlockSpec(memory_space=pl.ANY)
+VM = pl.BlockSpec(memory_space=pltpu.VMEM)
 NT = (((1,), (1,)), ((), ()))
 TN = (((0,), (0,)), ((), ()))
 
@@ -18,7 +19,7 @@
     return pltpu.CompilerParams(vmem_limit_bytes=mib * 1024 * 1024)
 
 
-def pack_kernel(peers, toks, rows, width, tokens_ref, weight_ref, out_ref, sems):
+def pack_kernel(peers, toks, rows, width, tokens_ref, weight_ref, routes_ref, out_ref, sems):
     copies = []
     for p in range(peers):
         cols = pl.ds(p * width, width)
@@ -30,22 +31,25 @@
         )
     for c in copies:
         c.start()
+    for p in range(peers):
+        out_ref[p, pl.ds(toks + rows, 16), :] = routes_ref[...]
     for c in copies:
         c.wait()
 
 
-def pack(tokens, weight, peers):
+def pack(tokens, weight, routes, peers):
     toks, d = tokens.shape
     rows = weight.shape[0]
     width = d // peers
     return pl.pallas_call(
         functools.partial(pack_kernel, peers, toks, rows, width),
-        out_shape=jax.ShapeDtypeStruct((peers, toks + rows, width), tokens.dtype),
-        in_specs=[ANY, ANY],
-        out_specs=ANY,
+        out_shape=jax.ShapeDtypeStruct((peers, toks + rows + 16, width), tokens.dtype),
+        in_specs=[ANY, ANY, VM],
+        out_specs=VM,
         scratch_shapes=[pltpu.SemaphoreType.DMA((2, peers))],
+        compiler_params=params(16),
         name="pack",
-    )(tokens, weight)
+    )(tokens, weight, routes)
 
 
 def shrink_kernel(group, rank, x_ref, w_ref, r_ref, out_ref):
@@ -57,7 +61,8 @@
     @pl.loop(0, group // 2)
     def _(g):
         x = x_ref[pl.ds(2 * g, 2)].reshape(2 * toks, width)
-        routes = [[r_ref[2 * g + b, pl.ds(k, 1), :] for k in range(2)] for b in range(2)]
+        rows = [r_ref[2 * g + b].astype(F32)[0:1] for b in range(2)]
+        routes = [[r[:, :toks], r[:, toks:]] for r in rows]
         acc = [[jnp.zeros((rank, toks), F32) for _ in range(2)] for _ in range(2)]
         for c in range(peers // chunk):
             w = w_ref[c * chunk : (c + 1) * chunk].reshape(chunk * wrows, width)
@@ -73,9 +78,9 @@
                 out_ref[2 * g + b, pl.ds(k * rank, rank), :] = acc[b][k].astype(out_ref.dtype)
 
 
-def shrink(buf, routes, toks, rank, group):
+def shrink(buf, toks, rank, group):
     peers, total, width = buf.shape
-    wrows = total - toks
+    wrows = total - toks - 16
     return pl.pallas_call(
         functools.partial(shrink_kernel, group, rank),
         grid=(peers // group,),
@@ -83,12 +88,12 @@
         in_specs=[
             pl.BlockSpec((group, toks, width), lambda i: (i, 0, 0)),
             pl.BlockSpec((peers, wrows, width), lambda i: (0, toks // wrows, 0)),
-            pl.BlockSpec((group, 2, toks), lambda i: (i, 0, 0)),
+            pl.BlockSpec((group, 16, width), lambda i: (i, (toks + wrows) // 16, 0)),
         ],
         out_specs=pl.BlockSpec((group, 2 * rank, toks), lambda i: (i, 0, 0)),
         compiler_params=params(),
         name="shrink",
-    )(buf, buf, routes)
+    )(buf, buf, buf)
 
 
 def combine_kernel(peers, per_block, rank, toks, part_ref, gate_ref, weight_ref, out_ref, s_ref, sems):
@@ -126,7 +131,7 @@
     return pl.pallas_call(
         functools.partial(combine_kernel, peers, per_block, rank, toks),
         out_shape=jax.ShapeDtypeStruct((peers, wrows + rank, width), BF16),
-        in_specs=[pl.BlockSpec(memory_space=pltpu.VMEM), pl.BlockSpec(memory_space=pltpu.VMEM), ANY],
+        in_specs=[VM, VM, ANY],
         out_specs=ANY,
         scratch_shapes=[pltpu.VMEM((rank, 2 * toks), BF16), pltpu.SemaphoreType.DMA((2, peers))],
         compiler_params=params(),
@@ -150,9 +155,9 @@
     @pl.loop(0, group)
     def _(b):
         s = s_ref[b].astype(F32)
-        r = r_ref[b].astype(F32)
+        r = r_ref[b].astype(F32)[0:1]
         rows = jnp.concatenate(
-            [s[:, :toks], s[:, toks:]] + [jnp.broadcast_to(r[k : k + 1], (rank, toks)) for k in range(2)], axis=0
+            [s[:, :toks], s[:, toks:]] + [jnp.broadcast_to(t, (rank, toks)) for t in (r[:, :toks], r[:, toks:])], axis=0
         ).astype(BF16)
         t = lax.dot_general(rows, spread, TN, preferred_element_type=F32)
         s0 = t[:, :lanes].astype(BF16)
@@ -169,10 +174,11 @@
     out_ref[...] = out.astype(BF16).reshape(group, toks, width)
 
 
-def expand(buf, routes, rank, group):
+def expand(buf, arrived, rank, group):
     peers, total, width = buf.shape
     wrows = total - rank
-    toks = routes.shape[2]
+    toks = width // 2
+    route_block = arrived.shape[1] // 16 - 1
     return pl.pallas_call(
         functools.partial(expand_kernel, group),
         grid=(peers // group,),
@@ -180,13 +186,13 @@
         in_specs=[
             pl.BlockSpec((group, rank, width), lambda i: (i, wrows // rank, 0)),
             pl.BlockSpec((peers, wrows, width), lambda i: (0, 0, 0)),
-            pl.BlockSpec((group, 2, toks), lambda i: (i, 0, 0)),
+            pl.BlockSpec((group, 16, width), lambda i: (i, route_block, 0)),
         ],
         out_specs=pl.BlockSpec((group, toks, width), lambda i: (i, 0, 0)),
         scratch_shapes=[pltpu.VMEM((group * toks, peers * wrows), BF16)],
         compiler_params=params(),
         name="expand",
-    )(buf, buf, routes)
+    )(buf, buf, arrived)
 
 
 def unpack_kernel(peers, width, in_ref, out_ref, sems):
@@ -204,9 +210,10 @@
     return pl.pallas_call(
         functools.partial(unpack_kernel, peers, width),
         out_shape=jax.ShapeDtypeStruct((toks, peers * width), buf.dtype),
-        in_specs=[ANY],
+        in_specs=[VM],
         out_specs=ANY,
         scratch_shapes=[pltpu.SemaphoreType.DMA((peers,))],
+        compiler_params=params(16),
         name="unpack",
     )(buf)
 
@@ -221,12 +228,12 @@
     peers = lax.axis_size("expert")
     rows = local * rank
     group = min(8, peers)
-    all_routes = lax.all_gather(routes.T, "expert", axis=0)
+    route_rows = jnp.broadcast_to(routes.T.astype(BF16).reshape(1, 2 * toks), (16, 2 * toks))
     all_expand = lax.all_gather(expand_weight.reshape(rows, -1), "tensor", axis=0)
-    arrived = swap(pack(tokens, shrink_weight.reshape(rows, -1), peers))
-    partial = shrink(arrived, all_routes, toks, rank, group)
+    arrived = swap(pack(tokens, shrink_weight.reshape(rows, -1), route_rows, peers))
+    partial = shrink(arrived, toks, rank, group)
     packed = swap(combine(swap(partial), route_weight.T, all_expand))
-    columns = expand(packed, all_routes, rank, group)
+    columns = expand(packed, arrived, rank, group)
     return unpack(swap(columns))
 
 

time: 348 us -> 184 us (0.53)
  Pallas kernels: 189 us -> 30.3 us
  blocking collectives: 111 us -> 58.2 us
  waiting for transfers between devices: 16.2 us -> 58.6 us
  local copies, waits for them, and re-layouts: 2.2 us -> 6.72 us
    pallas_call x1, Pallas kernels: 97 us -> 1.21 us  [pack(): pl.pallas_call(functools.partial(pack_kernel, peers, toks, rows, width),...]
    pallas_call x1, Pallas kernels: 64.9 us -> 1.57 us  [unpack(): pl.pallas_call(functools.partial(unpack_kernel, peers, width), out_shape=...]
    all_gather x1 -> x0, blocking collectives: 53.2 us -> none  [per_device(): all_routes = lax.all_gather(routes.T, 'expert', axis=0)]
    all_to_all x2, waiting for transfers between devices: 15.5 us -> 57.9 us  [swap(): return lax.all_to_all(x, 'expert', split_axis=0, concat_axis=0, tiled=True)]
    unnamed x8 -> x14, local copies, waits for them, and re-layouts: 2.2 us -> 6.71 us
  transfers between devices with their start and end apart: 3 -> 3, of which waited for: 1 -> 2; matrix products, arithmetic and copies ran while one was open for 0% -> 0% of each run, Pallas kernels for 3% -> 5%
where the time goes in v2:
time: 184 us; the launch traced here: 181 us
  waiting for transfers between devices  58.6 us (32%)
  blocking collectives  58.2 us (32%)
  Pallas kernels  30.3 us (16%)
  starting transfers between devices  13.5 us (7%)
  between operations  13.5 us (7%)
  local copies, waits for them, and re-layouts  6.72 us (4%)
    all_to_all x2, blocking collectives, swap(): return lax.all_to_all(x, 'expert', split_axis=0, concat_axis=0, tiled=True)  58.2 us
    all_to_all x2, waiting for transfers between devices, swap(): return lax.all_to_all(x, 'expert', split_axis=0, concat_axis=0, tiled=True)  57.9 us
    pallas_call x1, Pallas kernels, expand(): pl.pallas_call(functools.partial(expand_kernel, group), grid=(peers // gr...  15.9 us
    all_to_all x2, starting transfers between devices, swap(): return lax.all_to_all(x, 'expert', split_axis=0, concat_axis=0, tiled=True)  13.4 us
    pallas_call x1, Pallas kernels, shrink(): pl.pallas_call(functools.partial(shrink_kernel, group, rank), grid=(peers...  9.93 us
    unnamed x14, local copies, waits for them, and re-layouts  6.71 us
  transfers between devices with their start and end apart: 3, of which 2 were waited for; matrix products, arithmetic and copies ran while one was open for 0% of the time, Pallas kernels for 5%

profile of v2, /device:TPU:8, one launch (start us, length us, event | category | flops | bytes accessed | tf_op | source)
XLA Modules:
  0.0 181.5 jit_solution(16522016228961182952)
XLA Ops:
  6.5 0.7 convert_bitcast_fusion
  7.2 1.6 copy-done.3
  8.8 1.2 copy-done.4
  10.0 1.2 pack.1
  11.3 0.0 copy-start.1
  11.3 1.7 copy-done.1
  13.0 7.5 %all-to-all-start = ((bf16[32,208,256]{2,1,0:T(8,128)(2,1)}), bf16[32,208,256]{2,1,0:T(8,128)(2,1)S(1)}, u32[]{:S(2)}, u32[]{:S(2)}) async-start(bf16[32,208,256]{2,1,0:T(8,128)(2,1)} %copy-done.1), calls=%async_computation | async-start | bytes 6815744 | tf_op jit(solution)/shard_map/all_to_all | solution.py:222
  20.5 0.0 all-gather.2.cloned.1.call-start
  20.6 0.7 all-gather.2.cloned.1.call-update
  21.2 42.4 %all-to-all-done.x_ref.w_ref.r_ref = bf16[32,208,256]{2,1,0:T(8,128)(2,1)S(1)} async-done(((bf16[32,208,256]{2,1,0:T(8,128)(2,1)}), bf16[32,208,256]{2,1,0:T(8,128)(2,1)S(1)}, u32[]{:S(2)}, u32[]{:S(2)}) %all-to-all-start) | async-done | bytes 3407904 | tf_op jit(solution)/shard_map/all_to_all | solution.py:222
  63.7 9.9 %shrink.1 = f32[32,64,128]{2,1,0:T(8,128)S(1)} custom-call(bf16[32,208,256]{2,1,0:T(8,128)(2,1)S(1)} %all-to-all-done.x_ref.w_ref.r_ref, bf16[32,208,256]{2,1,0:T(8,128)(2,1)S(1)} %all-to-all-done.x_ref.w_ref.r_ref, bf16[32,208,256]{2,1,0:T(8,128)(2,1)S(1)} %all-to-all-done.x_ref.w_ref.r_ref), custom_call_target="tpu_custom_call" | custom-call | tf_op jit(solution)/shard_map/shrink/pallas_call | solution.py:84
  73.6 0.0 copy-done
  73.6 0.0 copy-start.2
  73.6 1.0 copy-done.2
  74.6 5.9 %all-to-all-start.1 = ((f32[32,64,128]{2,1,0:T(8,128)}), f32[32,64,128]{2,1,0:T(8,128)S(1)}, u32[]{:S(2)}, u32[]{:S(2)}) async-start(f32[32,64,128]{2,1,0:T(8,128)} %copy-done.2), calls=%async_computation.1 | async-start | bytes 2097152 | tf_op jit(solution)/shard_map/all_to_all | solution.py:222
  80.5 0.0 all-gather.2.cloned.1.call-done.weight_ref
  80.5 15.5 %all-to-all-done.1.part_ref = f32[32,64,128]{2,1,0:T(8,128)S(1)} async-done(((f32[32,64,128]{2,1,0:T(8,128)}), f32[32,64,128]{2,1,0:T(8,128)S(1)}, u32[]{:S(2)}, u32[]{:S(2)}) %all-to-all-start.1) | async-done | bytes 1048608 | tf_op jit(solution)/shard_map/all_to_all | solution.py:222
  96.0 0.0 copy-done.6
  96.1 1.2 copy-done.5
  97.3 1.6 combine.1
  98.9 26.5 %all_to_all.20.s_ref.w_ref = bf16[32,96,256]{2,1,0:T(8,128)(2,1)S(1)} all-to-all(bf16[32,96,256]{2,1,0:T(8,128)(2,1)S(1)} %combine.1), channel_id=1, replica_groups=mesh['expert'=32,'tensor'=8] {'expert'}, dimensions={0} | all-to-all | bytes 3145728 | tf_op jit(solution)/shard_map/all_to_all | solution.py:222
  125.4 15.9 %expand.1 = bf16[32,128,256]{2,1,0:T(8,128)(2,1)S(1)} custom-call(bf16[32,96,256]{2,1,0:T(8,128)(2,1)S(1)} %all_to_all.20.s_ref.w_ref, bf16[32,96,256]{2,1,0:T(8,128)(2,1)S(1)} %all_to_all.20.s_ref.w_ref, bf16[32,208,256]{2,1,0:T(8,128)(2,1)} %copy-done), custom_call_target="tpu_custom_call" | custom-call | tf_op jit(solution)/shard_map/expand/pallas_call | solution.py:182
  141.3 31.7 %all_to_all.21.in_ref = bf16[32,128,256]{2,1,0:T(8,128)(2,1)S(1)} all-to-all(bf16[32,128,256]{2,1,0:T(8,128)(2,1)S(1)} %expand.1), channel_id=1, replica_groups=mesh['expert'=32,'tensor'=8] {'expert'}, dimensions={0} | all-to-all | bytes 4194304 | tf_op jit(solution)/shard_map/all_to_all | solution.py:222
  173.0 1.6 unpack.1
  (6 shorter events, 0.0 us)
Async XLA Ops:
  7.2 1.6 copy-start.3
  8.8 1.2 copy-start.4
  11.3 1.7 copy-start.1
  13.0 50.7 %all-to-all-start = ((bf16[32,208,256]{2,1,0:T(8,128)(2,1)}), bf16[32,208,256]{2,1,0:T(8,128)(2,1)S(1)}, u32[]{:S(2)}, u32[]{:S(2)}) async-start(bf16[32,208,256]{2,1,0:T(8,128)(2,1)} %copy-done.1), calls=%async_computation | async-start | bytes 6815744 | tf_op jit(solution)/shard_map/all_to_all | solution.py:222
  20.5 60.0 %all-gather.2.cloned.1.call-start = ((), (), s32[]{:S(2)}) async-start(), calls=%async_computation.4 | async-start | bytes 1179648 | tf_op jit(solution)/shard_map/all_gather | solution.py:232
  63.7 9.9 %copy-start = (bf16[32,208,256]{2,1,0:T(8,128)(2,1)}, bf16[32,208,256]{2,1,0:T(8,128)(2,1)S(1)}, u32[]{:S(2)}) copy-start(bf16[32,208,256]{2,1,0:T(8,128)(2,1)S(1)} %all-to-all-done.x_ref.w_ref.r_ref) | copy-start | bytes 10223620
  73.6 1.0 copy-start.2
  74.6 21.5 %copy-start.6 = (f32[128,2]{0,1:T(2,128)S(1)}, f32[128,2]{0,1:T(2,128)}, u32[]{:S(2)}) copy-start(f32[128,2]{0,1:T(2,128)} %param.7) | copy-start | bytes 3076
  74.6 21.4 %all-to-all-start.1 = ((f32[32,64,128]{2,1,0:T(8,128)}), f32[32,64,128]{2,1,0:T(8,128)S(1)}, u32[]{:S(2)}, u32[]{:S(2)}) async-start(f32[32,64,128]{2,1,0:T(8,128)} %copy-done.2), calls=%async_computation.1 | async-start | bytes 2097152 | tf_op jit(solution)/shard_map/all_to_all | solution.py:222
  96.0 1.2 copy-start.5
Sparse Core Ops, SparseCore 0:
  23.1 41.2 all-gather.1

commit v3 on v0

v3 whole, which is shorter than its diff:
```python
import functools

import jax
import jax.numpy as jnp
from jax import lax
from jax.experimental import pallas as pl
from jax.experimental.pallas import tpu as pltpu
from jax.sharding import PartitionSpec as P

BF16 = jnp.bfloat16
F32 = jnp.float32
ANY = pl.BlockSpec(memory_space=pl.ANY)
HBM = pl.BlockSpec(memory_space=pltpu.HBM)
VM = pl.BlockSpec(memory_space=pltpu.VMEM)
NT = (((1,), (1,)), ((), ()))
TILE = 16
LANES = 128


def params(mib):
    return pltpu.CompilerParams(vmem_limit_bytes=mib * 1024 * 1024)


def pack_kernel(peers, toks, rows, width, tokens_ref, weight_ref, expand_ref, routes_ref, out_ref, sems):
    copies = []
    for p in range(peers):
        cols = pl.ds(p * width, width)
        copies.append(
            pltpu.make_async_copy(tokens_ref.at[:, cols], out_ref.at[p, pl.ds(0, toks)], sems.at[0, p])
        )
        copies.append(
            pltpu.make_async_copy(weight_ref.at[:, cols], out_ref.at[p, pl.ds(toks, rows)], sems.at[1, p])
        )
    for c in copies:
        c.start()
    tail = pl.ds(toks + rows, TILE)
    names = routes_ref[...].astype(F32)
    names = jnp.concatenate([names, jnp.zeros((TILE - 2, toks), F32)], axis=0).astype(BF16)
    feats = expand_ref.shape[1] // peers
    for t in range(expand_ref.shape[1] // LANES):
        block = expand_ref[:, t * LANES : (t + 1) * LANES].astype(F32).T
        for j in range(LANES // feats):
            p = t * (LANES // feats) + j
            piece = block[j * feats : (j + 1) * feats]
            piece = jnp.concatenate([piece[:TILE], piece[TILE:]], axis=1)
            out_ref[p, tail, pl.ds(0, LANES)] = piece.astype(BF16)
            out_ref[p, tail, pl.ds(LANES, toks)] = names
    for c in copies:
        c.wait()


def pack(tokens, weight, expand_weight, routes, peers):
    toks, d = tokens.shape
    rows = weight.shape[0]
    width = d // peers
    return pl.pallas_call(
        functools.partial(pack_kernel, peers, toks, rows, width),
        out_shape=jax.ShapeDtypeStruct((peers, toks + rows + TILE, width), tokens.dtype),
        in_specs=[HBM, HBM, VM, VM],
        out_specs=VM,
        scratch_shapes=[pltpu.SemaphoreType.DMA((2, peers))],
        compiler_params=params(16),
        name="pack",
    )(tokens, weight, expand_weight, routes)


def shrink_kernel(group, rank, x_ref, w_ref, r_ref, out_ref):
    peers, wrows, width = w_ref.shape
    toks = x_ref.shape[1]
    chunk = max(1, 256 // wrows)
    per = chunk * wrows // rank
    x = x_ref[...].reshape(group * toks, width)
    names = [r_ref[b].astype(F32) for b in range(group)]
    acc = [[jnp.zeros((rank, toks), F32) for _ in range(2)] for _ in range(group)]
    for c in range(peers // chunk):
        w = w_ref[c * chunk : (c + 1) * chunk].reshape(chunk * wrows, width)
        p = lax.dot_general(w, x, NT, preferred_element_type=F32)
        for j in range(per):
            e = c * per + j
            for b in range(group):
                piece = p[j * rank : (j + 1) * rank, b * toks : (b + 1) * toks]
                for k in range(2):
                    acc[b][k] = jnp.where(names[b][k : k + 1] == e, piece, acc[b][k])
    for b in range(group):
        for k in range(2):
            out_ref[b, pl.ds(k * rank, rank), :] = acc[b][k].astype(out_ref.dtype)


def shrink(buf, toks, rows, rank, group):
    peers, _, width = buf.shape
    tail = (toks + rows) // TILE
    return pl.pallas_call(
        functools.partial(shrink_kernel, group, rank),
        grid=(peers // group,),
        out_shape=jax.ShapeDtypeStruct((peers, 2 * rank, toks), BF16),
        in_specs=[
            pl.BlockSpec((group, toks, width), lambda i: (i, 0, 0)),
            pl.BlockSpec((peers, rows, width), lambda i: (0, toks // rows, 0)),
            pl.BlockSpec((group, TILE, LANES), lambda i: (i, tail, 1)),
        ],
        out_specs=pl.BlockSpec((group, 2 * rank, toks), lambda i: (i, 0, 0)),
        compiler_params=params(32),
        name="shrink",
    )(buf, buf, buf)


def combine_kernel(peers, rank, part_ref, gate_ref, out_ref):
    gated = []
    for k in range(2):
        total = part_ref[0, pl.ds(k * rank, rank), :].astype(F32)
        for p in range(1, peers):
            total = total + part_ref[p, pl.ds(k * rank, rank), :].astype(F32)
        gated.append((total.astype(BF16).astype(F32) * gate_ref[pl.ds(k, 1), :]).astype(BF16))
    both = jnp.concatenate(gated, axis=1)
    for p in range(peers):
        out_ref[p] = both


def combine(part, gates):
    peers, rank2, toks = part.shape
    rank = rank2 // 2
    return pl.pallas_call(
        functools.partial(combine_kernel, peers, rank),
        out_shape=jax.ShapeDtypeStruct((peers, rank, 2 * toks), BF16),
        in_specs=[VM, VM],
        out_specs=VM,
        compiler_params=params(16),
        name="combine",
    )(part, gates)


def expand_kernel(group, experts, order, s_ref, r_ref, *refs):
    *piece_refs, out_ref, w_ref = refs
    rank = s_ref.shape[1]
    toks = s_ref.shape[2] // 2

    @pl.when(pl.program_id(0) == 0)
    def _():
        me = lax.axis_index("tensor")
        low = lax.broadcasted_iota(jnp.int32, (TILE, LANES), 1) < LANES // 2
        blocks = []
        for ref in piece_refs:
            blocks += [ref.at[m] for m in range(ref.shape[0])]
        for offset, ref in zip(order, blocks):
            row = pl.multiple_of((me ^ offset) * (2 * TILE), 2 * TILE)
            for t in range(ref.shape[0] // 2):
                a = ref[2 * t].astype(F32)
                b = ref[2 * t + 1].astype(F32)
                first = jnp.where(low, a, pltpu.roll(b, LANES // 2, 1))
                second = jnp.where(low, pltpu.roll(a, LANES // 2, 1), b)
                both = jnp.concatenate([first, second], axis=0).astype(BF16)
                w_ref[pl.ds(row, 2 * TILE), t * LANES : (t + 1) * LANES] = both

    spread = []
    for b in range(group):
        s = s_ref[b]
        names = r_ref[b]
        s0, s1 = s[:, :toks], s[:, toks:]
        r0, r1 = (jnp.broadcast_to(names[k : k + 1], (rank, toks)) for k in range(2))
        zero = jnp.zeros((rank, toks), BF16)
        rows = []
        for e in range(experts):
            name = jnp.asarray(e, BF16)
            rows.append(jnp.where(r0 == name, s0, jnp.where(r1 == name, s1, zero)))
        spread.append(jnp.concatenate(rows, axis=0))
    out = jnp.dot(w_ref[...], jnp.concatenate(spread, axis=1), preferred_element_type=F32)
    for b in range(group):
        out_ref[b] = out[:, b * toks : (b + 1) * toks].astype(BF16)


def expand(vectors, arrived, pieces, order, experts, group):
    peers, rank, toks2 = vectors.shape
    toks = toks2 // 2
    tail = arrived.shape[1] // TILE - 1
    feats = len(order) * 2 * TILE
    return pl.pallas_call(
        functools.partial(expand_kernel, group, experts, order),
        grid=(peers // group,),
        out_shape=jax.ShapeDtypeStruct((peers, feats, toks), BF16),
        in_specs=[
            pl.BlockSpec((group, rank, toks2), lambda i: (i, 0, 0)),
            pl.BlockSpec((group, TILE, LANES), lambda i: (i, tail, 1)),
        ]
        + [pl.BlockSpec(p.shape, lambda i: (0, 0, 0, 0)) for p in pieces],
        out_specs=pl.BlockSpec((group, feats, toks), lambda i: (i, 0, 0)),
        scratch_shapes=[pltpu.VMEM((feats, experts * rank), BF16)],
        compiler_params=params(32),
        name="expand",
    )(vectors, arrived, *pieces)


def unpack_kernel(blocks, in_ref, out_ref, buf, sems):
    peers, feats, toks = in_ref.shape
    piece = feats // blocks
    per = LANES // piece
    cols = peers * piece
    copies = []
    for z in range(blocks):
        for q in range(peers // per):
            parts = [in_ref[per * q + k, z * piece : (z + 1) * piece, :] for k in range(per)]
            buf[z, q] = jnp.concatenate(parts, axis=0).T
            copy = pltpu.make_async_copy(
                buf.at[z, q], out_ref.at[:, pl.ds(z * cols + q * LANES, LANES)], sems.at[z, q]
            )
            copy.start()
            copies.append(copy)
    for copy in copies:
        copy.wait()


def unpack(buf, blocks):
    peers, feats, toks = buf.shape
    quads = peers * (feats // blocks) // LANES
    return pl.pallas_call(
        functools.partial(unpack_kernel, blocks),
        out_shape=jax.ShapeDtypeStruct((toks, peers * feats), buf.dtype),
        in_specs=[VM],
        out_specs=ANY,
        scratch_shapes=[
            pltpu.VMEM((blocks, quads, toks, LANES), buf.dtype),
            pltpu.SemaphoreType.DMA((blocks, quads)),
        ],
        compiler_params=params(16),
        name="unpack",
    )(buf)


def swap(x):
    return lax.all_to_all(x, "expert", split_axis=0, concat_axis=0, tiled=True)


def across(x, blocks, offset):
    return lax.ppermute(x, "tensor", [(i, i ^ offset) for i in range(blocks)])


def per_device(tokens, routes, route_weight, shrink_weight, expand_weight):
    toks, _ = tokens.shape
    local, rank, _ = shrink_weight.shape
    peers = lax.axis_size("expert")
    blocks = lax.axis_size("tensor")
    rows = local * rank
    group = min(8, peers)
    arrived = swap(
        pack(tokens, shrink_weight.reshape(rows, -1), expand_weight.reshape(rows, -1), routes.T, peers)
    )
    pieces = [arrived[None, :, toks + rows :, :LANES]]
    order = [0]
    offset = blocks // 2
    while offset:
        held = pieces[0] if len(pieces) == 1 else jnp.concatenate(pieces, axis=0)
        pieces.append(across(held, blocks, offset))
        order += [o ^ offset for o in order]
        offset //= 2
    partial = shrink(arrived, toks, rows, rank, group)
    vectors = swap(combine(swap(partial), route_weight.T))
    columns = expand(vectors, arrived, pieces, tuple(order), peers * local, group)
    return unpack(swap(columns), blocks)


def solution(mesh):
    return jax.shard_map(
        per_device,
        mesh=mesh,
        in_specs=(
            P(("expert", "tensor"), None),
            P(("expert", "tensor"), None),
            P(("expert", "tensor"), None),
            P("expert", None, None),
            P("expert", None, "tensor"),
        ),
        out_specs=P(("expert", "tensor"), None),
        check_vma=False,
    )
```

time: 568 us -> 157 us (0.28); the launches traced: 559 us -> 154 us
  blocking collectives: 319 us -> 80.1 us
  waiting for transfers between devices: 123 us -> 23.6 us
  local copies, waits for them, and re-layouts: 90 us -> 7.66 us
  Pallas kernels: 0 us -> 17.8 us
  starting transfers between devices: 7.59 us -> 22.5 us
  other arithmetic: 10.8 us -> 2.72 us
  matrix products: 7.84 us -> 0 us
    all_to_all x2, blocking collectives: 288 us -> 80.1 us  [swap(): return lax.all_to_all(x, 'expert', split_axis=0, concat_axis=0, tiled=True)]
    all_to_all x1 -> x2, waiting for transfers between devices: 123 us -> 6 us  [swap(): return lax.all_to_all(x, 'expert', split_axis=0, concat_axis=0, tiled=True)]
    all_gather x1 -> x0, blocking collectives: 30.6 us -> none  [per_device(): lax.all_gather(shrunk, 'tensor', axis=0, tiled=True)]
    gather x2 -> x0, local copies, waits for them, and re-layouts: 21.3 us -> none  [per_device(): jnp.take(returned, destination, axis=0).reshape(tok_rows, 2, features)]
    reshape x3 -> x0, local copies, waits for them, and re-layouts: 20.8 us -> none  [the longest x1 13.5 us: per_device(): expanded.reshape(owners, local_count * CAP, features)]
    pallas_call x0 -> x5, Pallas kernels: none -> 17.8 us  [the longest x1 6.7 us: expand(): pl.pallas_call(functools.partial(expand_kernel, group, experts, order), g...]
    ppermute x0 -> x3, waiting for transfers between devices: none -> 17.6 us  [across(): return lax.ppermute(x, 'tensor', [(i, i ^ offset) for i in range(blocks)])]
    all_to_all x1 -> x0, local copies, waits for them, and re-layouts: 16.7 us -> none  [per_device(): lax.all_to_all(columns, 'tensor', split_axis=0, concat_axis=3, tiled=True)]
  transfers between devices with their start and end apart: 1 -> 5, of which waited for: 1 -> 3; matrix products, arithmetic and copies ran while one was open for 0% -> 2% of each run, Pallas kernels for 0% -> 5%
where the time goes in v3:
time: 157 us; the launch traced here: 154 us
  blocking collectives  80.1 us (51%)
  waiting for transfers between devices  23.6 us (15%)
  starting transfers between devices  22.5 us (14%)
  Pallas kernels  17.8 us (11%)
  local copies, waits for them, and re-layouts  7.66 us (5%)
  other arithmetic  2.72 us (2%)
    all_to_all x2, blocking collectives, swap(): return lax.all_to_all(x, 'expert', split_axis=0, concat_axis=0, tiled=True)  80.1 us
    ppermute x3, waiting for transfers between devices, across(): return lax.ppermute(x, 'tensor', [(i, i ^ offset) for i in range(blocks)])  17.6 us
    all_to_all x2, starting transfers between devices, swap(): return lax.all_to_all(x, 'expert', split_axis=0, concat_axis=0, tiled=True)  13.7 us
    ppermute x3, starting transfers between devices, across(): return lax.ppermute(x, 'tensor', [(i, i ^ offset) for i in range(blocks)])  8.84 us
    unnamed x18, local copies, waits for them, and re-layouts  7.64 us
    pallas_call x1, Pallas kernels, expand(): pl.pallas_call(functools.partial(expand_kernel, group, experts, order), g...  6.7 us
    pallas_call x1, Pallas kernels, shrink(): pl.pallas_call(functools.partial(shrink_kernel, group, rank), grid=(peers...  6.51 us
    all_to_all x2, waiting for transfers between devices, swap(): return lax.all_to_all(x, 'expert', split_axis=0, concat_axis=0, tiled=True)  6 us
  transfers between devices with their start and end apart: 5, of which 3 were waited for; matrix products, arithmetic and copies ran while one was open for 2% of the time, Pallas kernels for 5%

profile of v3, /device:TPU:8, one launch (start us, length us, event | category | flops | bytes accessed | tf_op | source)
XLA Modules:
  0.0 154.5 jit_solution(14806357546644806206)
XLA Ops:
  0.0 1.6 %copy-done.1 = bf16[128,8192]{1,0:T(8,128)(2,1)S(1)} copy-done((bf16[128,8192]{1,0:T(8,128)(2,1)S(1)}, bf16[128,8192]{1,0:T(8,128)(2,1)}, u32[]{:S(2)}) %copy-start.1) | copy-done | bytes 2097176
  1.6 1.2 copy-done.5
  2.8 0.9 copy-done.6
  3.7 0.7 copy-done.8
  4.4 1.5 pack.1
  5.9 48.4 %all_to_all.20.x_ref.w_ref.r_ref = bf16[32,208,256]{2,1,0:T(8,128)(2,1)S(1)} all-to-all(bf16[32,208,256]{2,1,0:T(8,128)(2,1)S(1)} %pack.1), channel_id=1, replica_groups=mesh['expert'=32,'tensor'=8] {'expert'}, dimensions={0} | all-to-all | bytes 6815744 | tf_op jit(solution)/shard_map/all_to_all | solution.py:229
  54.3 7.3 %collective-permute-start = (bf16[1,32,16,128]{3,2,1,0:T(8,128)(2,1)S(1)}, bf16[1,32,16,128]{3,2,1,0:T(8,128)(2,1)}, u32[]{:S(2)}, u32[]{:S(2)}) collective-permute-start(bf16[1,32,16,128]{3,2,1,0:T(8,128)(2,1)S(1)} %slice_bitcast_fusion.refs_0_), channel_id=1, source_target_pairs={{0,4},{1,5},{2,6},{3,7},{4,0},{5,1},{6,2},{7,3},{8,12},{9,13},{10,... | collective-permute-start | bytes 393224 | tf_op jit(solution)/shard_map/ppermute | solution.py:233
  61.6 6.5 %shrink.1 = bf16[32,64,128]{2,1,0:T(8,128)(2,1)S(1)} custom-call(bf16[32,208,256]{2,1,0:T(8,128)(2,1)S(1)} %all_to_all.20.x_ref.w_ref.r_ref, bf16[32,208,256]{2,1,0:T(8,128)(2,1)S(1)} %all_to_all.20.x_ref.w_ref.r_ref, bf16[32,208,256]{2,1,0:T(8,128)(2,1)S(1)} %all_to_all.20.x_ref.w_ref.r_ref), custom_call_target="tpu_custom_call" | custom-call | tf_op jit(solution)/shard_map/shrink/pallas_call | solution.py:92
  68.1 0.8 copy-done.2
  68.9 6.2 %all-to-all-start.1 = ((bf16[32,64,128]{2,1,0:T(8,128)(2,1)}), bf16[32,64,128]{2,1,0:T(8,128)(2,1)}, u32[]{:S(2)}, u32[]{:S(2)}) async-start(bf16[32,64,128]{2,1,0:T(8,128)(2,1)} %copy-done.2), calls=%async_computation.1 | async-start | bytes 1048576 | tf_op jit(solution)/shard_map/all_to_all | solution.py:229
  75.1 0.9 pad_maximum_fusion.1
  76.0 1.6 %collective-permute-start.1 = (bf16[2,32,16,128]{3,2,1,0:T(8,128)(2,1)S(1)}, bf16[2,32,16,128]{3,2,1,0:T(8,128)(2,1)S(1)}, u32[]{:S(2)}, u32[]{:S(2)}) collective-permute-start(bf16[2,32,16,128]{3,2,1,0:T(8,128)(2,1)S(1)} %pad_maximum_fusion.1), channel_id=1, source_target_pairs={{0,2},{1,3},{2,0},{3,1},{4,6},{5,7},{6,4},{7,5},{8,10},{9,11},{10,... | collective-permute-start | bytes 786440 | tf_op jit(solution)/shard_map/ppermute | solution.py:233
  77.6 13.4 %collective-permute-done.1.refs_2_ = bf16[2,32,16,128]{3,2,1,0:T(8,128)(2,1)S(1)} collective-permute-done((bf16[2,32,16,128]{3,2,1,0:T(8,128)(2,1)S(1)}, bf16[2,32,16,128]{3,2,1,0:T(8,128)(2,1)S(1)}, u32[]{:S(2)}, u32[]{:S(2)}) %collective-permute-start.1) | collective-permute-done | bytes 262176 | tf_op jit(solution)/shard_map/ppermute | solution.py:233
  91.0 1.8 %pad_maximum_fusion = bf16[4,32,16,128]{3,2,1,0:T(8,128)(2,1)} fusion(bf16[2,32,16,128]{3,2,1,0:T(8,128)(2,1)S(1)} %collective-permute-done.1.refs_2_, bf16[1,32,16,128]{3,2,1,0:T(8,128)(2,1)} %collective-permute-done.refs_1_, bf16[1,32,16,128]{3,2,1,0:T(8,128)(2,1)S(1)} %slice_bitcast_fusion.refs_0_), kind=kLoop, calls=%fused_computation | loop fusion | flops 524288 | bytes 1048576 | tf_op jit(solution)/shard_map/concatenate | solution.py:250
  92.8 0.7 copy-done.3
  93.5 1.2 combine.1
  94.7 0.8 copy-done
  95.5 7.5 %all-to-all-start.2 = ((bf16[32,32,256]{2,1,0:T(8,128)(2,1)}), bf16[32,32,256]{2,1,0:T(8,128)(2,1)}, u32[]{:S(2)}, u32[]{:S(2)}) async-start(bf16[32,32,256]{2,1,0:T(8,128)(2,1)} %copy-done), calls=%async_computation.2 | async-start | bytes 1048576 | tf_op jit(solution)/shard_map/all_to_all | solution.py:229
  103.0 4.2 %collective-permute-done.2.refs_3_ = bf16[4,32,16,128]{3,2,1,0:T(8,128)(2,1)} collective-permute-done((bf16[4,32,16,128]{3,2,1,0:T(8,128)(2,1)}, bf16[4,32,16,128]{3,2,1,0:T(8,128)(2,1)}, u32[]{:S(2)}, u32[]{:S(2)}) %collective-permute-start.2) | collective-permute-done | bytes 524320 | tf_op jit(solution)/shard_map/ppermute | solution.py:233
  107.2 6.0 %all-to-all-done.2.s_ref = bf16[32,32,256]{2,1,0:T(8,128)(2,1)} async-done(((bf16[32,32,256]{2,1,0:T(8,128)(2,1)}), bf16[32,32,256]{2,1,0:T(8,128)(2,1)}, u32[]{:S(2)}, u32[]{:S(2)}) %all-to-all-start.2) | async-done | bytes 524320 | tf_op jit(solution)/shard_map/all_to_all | solution.py:229
  113.2 0.9 copy-done.4
  114.2 6.7 %expand.1 = bf16[32,256,128]{2,1,0:T(8,128)(2,1)S(1)} custom-call(bf16[32,32,256]{2,1,0:T(8,128)(2,1)} %all-to-all-done.2.s_ref, bf16[32,208,256]{2,1,0:T(8,128)(2,1)S(1)} %all_to_all.20.x_ref.w_ref.r_ref, bf16[1,32,16,128]{3,2,1,0:T(8,128)(2,1)S(1)} %slice_bitcast_fusion.refs_0_, bf16[1,32,16,128]{3,2,1,0:T(8,128)(2,1)} %collective-permute-done.refs_1_, ...), custom_call_target="tpu_custom_call" | custom-call | tf_op jit(solution)/shard_map/expand/pallas_call | solution.py:176
  120.9 31.7 %all_to_all.21.in_ref = bf16[32,256,128]{2,1,0:T(8,128)(2,1)S(1)} all-to-all(bf16[32,256,128]{2,1,0:T(8,128)(2,1)S(1)} %expand.1), channel_id=1, replica_groups=mesh['expert'=32,'tensor'=8] {'expert'}, dimensions={0} | all-to-all | bytes 4194304 | tf_op jit(solution)/shard_map/all_to_all | solution.py:229
  152.6 1.9 %unpack.1 = bf16[128,8192]{1,0:T(8,128)(2,1)} custom-call(bf16[32,256,128]{2,1,0:T(8,128)(2,1)S(1)} %all_to_all.21.in_ref), custom_call_target="tpu_custom_call" | custom-call | tf_op jit(solution)/shard_map/unpack/pallas_call | solution.py:214
  (14 shorter events, 0.1 us)
Async XLA Ops:
  0.0 1.6 %copy-start.1 = (bf16[128,8192]{1,0:T(8,128)(2,1)S(1)}, bf16[128,8192]{1,0:T(8,128)(2,1)}, u32[]{:S(2)}) copy-start(bf16[128,8192]{1,0:T(8,128)(2,1)} %tokens_ref.1) | copy-start | bytes 6291460
  1.6 1.2 copy-start.5
  2.8 0.9 copy-start.6
  3.7 0.7 copy-start.8
  54.3 20.8 %collective-permute-start = (bf16[1,32,16,128]{3,2,1,0:T(8,128)(2,1)S(1)}, bf16[1,32,16,128]{3,2,1,0:T(8,128)(2,1)}, u32[]{:S(2)}, u32[]{:S(2)}) collective-permute-start(bf16[1,32,16,128]{3,2,1,0:T(8,128)(2,1)S(1)} %slice_bitcast_fusion.refs_0_), channel_id=1, source_target_pairs={{0,4},{1,5},{2,6},{3,7},{4,0},{5,1},{6,2},{7,3},{8,12},{9,13},{10,... | collective-permute-start | bytes 393224 | tf_op jit(solution)/shard_map/ppermute | solution.py:233
  68.1 0.8 copy-start.2
  68.9 24.6 %copy-start.7 = (f32[128,2]{0,1:T(2,128)S(1)}, f32[128,2]{0,1:T(2,128)}, u32[]{:S(2)}) copy-start(f32[128,2]{0,1:T(2,128)} %param.7) | copy-start | bytes 3076
  68.9 24.6 %all-to-all-start.1 = ((bf16[32,64,128]{2,1,0:T(8,128)(2,1)}), bf16[32,64,128]{2,1,0:T(8,128)(2,1)}, u32[]{:S(2)}, u32[]{:S(2)}) async-start(bf16[32,64,128]{2,1,0:T(8,128)(2,1)} %copy-done.2), calls=%async_computation.1 | async-start | bytes 1048576 | tf_op jit(solution)/shard_map/all_to_all | solution.py:229
  76.0 15.0 %collective-permute-start.1 = (bf16[2,32,16,128]{3,2,1,0:T(8,128)(2,1)S(1)}, bf16[2,32,16,128]{3,2,1,0:T(8,128)(2,1)S(1)}, u32[]{:S(2)}, u32[]{:S(2)}) collective-permute-start(bf16[2,32,16,128]{3,2,1,0:T(8,128)(2,1)S(1)} %pad_maximum_fusion.1), channel_id=1, source_target_pairs={{0,2},{1,3},{2,0},{3,1},{4,6},{5,7},{6,4},{7,5},{8,10},{9,11},{10,... | collective-permute-start | bytes 786440 | tf_op jit(solution)/shard_map/ppermute | solution.py:233
  92.8 0.7 copy-start.3
  93.5 13.7 %collective-permute-start.2 = (bf16[4,32,16,128]{3,2,1,0:T(8,128)(2,1)}, bf16[4,32,16,128]{3,2,1,0:T(8,128)(2,1)}, u32[]{:S(2)}, u32[]{:S(2)}) collective-permute-start(bf16[4,32,16,128]{3,2,1,0:T(8,128)(2,1)} %pad_maximum_fusion), channel_id=1, source_target_pairs={{0,1},{1,0},{2,3},{3,2},{4,5},{5,4},{6,7},{7,6},{8,9},{9,8},{10,11... | collective-permute-start | bytes 1572872 | tf_op jit(solution)/shard_map/ppermute | solution.py:233
  94.7 0.8 copy-start
  95.5 17.7 %all-to-all-start.2 = ((bf16[32,32,256]{2,1,0:T(8,128)(2,1)}), bf16[32,32,256]{2,1,0:T(8,128)(2,1)}, u32[]{:S(2)}, u32[]{:S(2)}) async-start(bf16[32,32,256]{2,1,0:T(8,128)(2,1)} %copy-done), calls=%async_computation.2 | async-start | bytes 1048576 | tf_op jit(solution)/shard_map/all_to_all | solution.py:229
  113.2 1.0 copy-start.4

commit v4 on v0

v4 whole, which is shorter than its diff:
```python
import functools

import jax
import jax.numpy as jnp
from jax import lax
from jax.experimental import pallas as pl
from jax.experimental.pallas import tpu as pltpu
from jax.sharding import PartitionSpec as P

BF16 = jnp.bfloat16
F32 = jnp.float32
ANY = pl.BlockSpec(memory_space=pl.ANY)
HBM = pl.BlockSpec(memory_space=pltpu.HBM)
VM = pl.BlockSpec(memory_space=pltpu.VMEM)
NT = (((1,), (1,)), ((), ()))
TILE = 16
LANES = 128


def params(mib):
    return pltpu.CompilerParams(vmem_limit_bytes=mib * 1024 * 1024)


def pack_kernel(peers, toks, rows, width, tokens_ref, weight_ref, routes_ref, out_ref, buf, sems):
    copies = []
    for p in range(peers):
        cols = pl.ds(p * width, width)
        first = pltpu.make_async_copy(tokens_ref.at[:, cols], buf.at[p, pl.ds(0, toks)], sems.at[0, p])
        second = pltpu.make_async_copy(weight_ref.at[:, cols], buf.at[p, pl.ds(toks, rows)], sems.at[1, p])
        first.start()
        second.start()
        copies.append((first, second))
    names = jnp.broadcast_to(routes_ref[pl.ds(0, 1), :], (TILE, width)).astype(F32).astype(BF16)
    for p in range(peers):
        buf[p, pl.ds(toks + rows, TILE), :] = names
    sends = []
    for p in range(peers):
        for copy in copies[p]:
            copy.wait()
        send = pltpu.make_async_copy(buf.at[p], out_ref.at[p], sems.at[2, p])
        send.start()
        sends.append(send)
    for send in sends:
        send.wait()


def pack(tokens, weight, routes, peers):
    toks, d = tokens.shape
    rows = weight.shape[0]
    width = d // peers
    shape = (peers, toks + rows + TILE, width)
    return pl.pallas_call(
        functools.partial(pack_kernel, peers, toks, rows, width),
        out_shape=jax.ShapeDtypeStruct(shape, tokens.dtype),
        in_specs=[HBM, HBM, VM],
        out_specs=HBM,
        scratch_shapes=[pltpu.VMEM(shape, tokens.dtype), pltpu.SemaphoreType.DMA((3, peers))],
        compiler_params=params(56),
        name="pack",
    )(tokens, weight, routes)


def shrink_kernel(group, rank, x_ref, w_ref, r_ref, out_ref):
    peers, wrows, width = w_ref.shape
    toks = x_ref.shape[1]
    chunk = max(1, 256 // wrows)
    per = chunk * wrows // rank
    x = x_ref[...].reshape(group * toks, width)
    names = [r_ref[b].astype(F32)[0:1] for b in range(group)]
    acc = [[jnp.zeros((rank, toks), F32) for _ in range(2)] for _ in range(group)]
    for c in range(peers // chunk):
        w = w_ref[c * chunk : (c + 1) * chunk].reshape(chunk * wrows, width)
        p = lax.dot_general(w, x, NT, preferred_element_type=F32)
        for j in range(per):
            e = c * per + j
            for b in range(group):
                piece = p[j * rank : (j + 1) * rank, b * toks : (b + 1) * toks]
                for k in range(2):
                    acc[b][k] = jnp.where(names[b][:, k * toks : (k + 1) * toks] == e, piece, acc[b][k])
    for b in range(group):
        for k in range(2):
            out_ref[b, pl.ds(k * rank, rank), :] = acc[b][k].astype(out_ref.dtype)


def shrink(buf, toks, rows, rank, group):
    peers, _, width = buf.shape
    tail = (toks + rows) // TILE
    return pl.pallas_call(
        functools.partial(shrink_kernel, group, rank),
        grid=(peers // group,),
        out_shape=jax.ShapeDtypeStruct((peers, 2 * rank, toks), BF16),
        in_specs=[
            pl.BlockSpec((group, toks, width), lambda i: (i, 0, 0)),
            pl.BlockSpec((peers, rows, width), lambda i: (0, toks // rows, 0)),
            pl.BlockSpec((group, TILE, width), lambda i: (i, tail, 0)),
        ],
        out_specs=pl.BlockSpec((group, 2 * rank, toks), lambda i: (i, 0, 0)),
        compiler_params=params(32),
        name="shrink",
    )(buf, buf, buf)


def place_kernel(blocks, width, *refs):
    *block_refs, out_ref, sems = refs
    rows = block_refs[0].shape[0]
    per = block_refs[0].shape[1] // width
    me = lax.axis_index("tensor")
    copies = []
    for offset, ref in enumerate(block_refs):
        owner = lax.rem(me + offset, blocks)
        for q in range(per):
            copy = pltpu.make_async_copy(
                ref.at[:, pl.ds(q * width, width)], out_ref.at[owner * per + q, pl.ds(0, rows)], sems.at[offset, q]
            )
            copy.start()
            copies.append(copy)
    for copy in copies:
        copy.wait()


def place(held, peers, rank):
    blocks = len(held)
    rows, cols = held[0].shape
    width = blocks * cols // peers
    return pl.pallas_call(
        functools.partial(place_kernel, blocks, width),
        out_shape=jax.ShapeDtypeStruct((peers, rows + rank, width), BF16),
        in_specs=[VM] * blocks,
        out_specs=VM,
        scratch_shapes=[pltpu.SemaphoreType.DMA((blocks, peers // blocks))],
        compiler_params=params(16),
        name="place",
    )(*held)


def combine_kernel(peers, rank, part_ref, gate_ref, _, out_ref, both_ref, sems):
    rows = out_ref.shape[1] - rank
    toks = part_ref.shape[2]
    for k in range(2):
        total = part_ref[0, pl.ds(k * rank, rank), :].astype(F32)
        for p in range(1, peers):
            total = total + part_ref[p, pl.ds(k * rank, rank), :].astype(F32)
        gated = total.astype(BF16).astype(F32) * gate_ref[pl.ds(k, 1), :]
        both_ref[:, k * toks : (k + 1) * toks] = gated.astype(BF16)
    copies = [pltpu.make_async_copy(both_ref, out_ref.at[p, pl.ds(rows, rank)], sems.at[p]) for p in range(peers)]
    for copy in copies:
        copy.start()
    for copy in copies:
        copy.wait()


def combine(part, gates, placed):
    peers, rank2, toks = part.shape
    return pl.pallas_call(
        functools.partial(combine_kernel, peers, rank2 // 2),
        out_shape=jax.ShapeDtypeStruct(placed.shape, BF16),
        in_specs=[VM, VM, ANY],
        out_specs=ANY,
        scratch_shapes=[pltpu.VMEM((rank2 // 2, 2 * toks), BF16), pltpu.SemaphoreType.DMA((peers,))],
        input_output_aliases={2: 0},
        compiler_params=params(16),
        name="combine",
    )(part, gates, placed)


def expand_kernel(group, rank, s_ref, r_ref, w_ref, out_ref, t_ref):
    toks = s_ref.shape[2] // 2
    peers, rows, _ = w_ref.shape
    experts = peers * rows // rank
    per = LANES // rows

    @pl.when(pl.program_id(0) == 0)
    def _():
        for t in range(peers // per):
            block = jnp.concatenate([w_ref[t * per + j] for j in range(per)], axis=0)
            t_ref[:, t * LANES : (t + 1) * LANES] = block.T

    spread = []
    for b in range(group):
        s = s_ref[b]
        names = r_ref[b]
        s0, s1 = s[:, :toks], s[:, toks:]
        r0, r1 = (jnp.broadcast_to(names[:1, k * toks : (k + 1) * toks], (rank, toks)) for k in range(2))
        zero = jnp.zeros((rank, toks), BF16)
        pieces = []
        for e in range(experts):
            name = jnp.asarray(e, BF16)
            pieces.append(jnp.where(r0 == name, s0, jnp.where(r1 == name, s1, zero)))
        spread.append(jnp.concatenate(pieces, axis=0))
    out = jnp.dot(t_ref[...], jnp.concatenate(spread, axis=1), preferred_element_type=F32)
    for b in range(group):
        out_ref[b] = out[:, b * toks : (b + 1) * toks].astype(BF16)


def expand(vectors, arrived, rank, group):
    peers, total, width = vectors.shape
    rows = total - rank
    toks = width // 2
    tail = arrived.shape[1] // TILE - 1
    return pl.pallas_call(
        functools.partial(expand_kernel, group, rank),
        grid=(peers // group,),
        out_shape=jax.ShapeDtypeStruct((peers, width, toks), BF16),
        in_specs=[
            pl.BlockSpec((group, rank, width), lambda i: (i, rows // rank, 0)),
            pl.BlockSpec((group, TILE, width), lambda i: (i, tail, 0)),
            pl.BlockSpec((peers, rows, width), lambda i: (0, 0, 0)),
        ],
        out_specs=pl.BlockSpec((group, width, toks), lambda i: (i, 0, 0)),
        scratch_shapes=[pltpu.VMEM((width, peers * rows), BF16)],
        compiler_params=params(32),
        name="expand",
    )(vectors, arrived, vectors)


def unpack_kernel(in_ref, out_ref, buf, sems):
    peers, width, _ = in_ref.shape
    copies = []
    for p in range(peers):
        for q in range(width // LANES):
            buf[p, :, q * LANES : (q + 1) * LANES] = in_ref[p, q * LANES : (q + 1) * LANES, :].T
        copy = pltpu.make_async_copy(buf.at[p], out_ref.at[:, pl.ds(p * width, width)], sems.at[p])
        copy.start()
        copies.append(copy)
    for copy in copies:
        copy.wait()


def unpack(buf):
    peers, width, toks = buf.shape
    return pl.pallas_call(
        unpack_kernel,
        out_shape=jax.ShapeDtypeStruct((toks, peers * width), buf.dtype),
        in_specs=[VM],
        out_specs=ANY,
        scratch_shapes=[pltpu.VMEM((peers, toks, width), buf.dtype), pltpu.SemaphoreType.DMA((peers,))],
        compiler_params=params(16),
        name="unpack",
    )(buf)


def swap(x):
    return lax.all_to_all(x, "expert", split_axis=0, concat_axis=0, tiled=True)


def ring(x, blocks):
    ahead = [(i, (i - 1) % blocks) for i in range(blocks)]
    behind = [(i, (i + 1) % blocks) for i in range(blocks)]
    held = {0: x}
    for step in range(1, blocks // 2 + 1):
        held[step] = lax.ppermute(held[step - 1], "tensor", ahead)
        if 2 * step < blocks:
            held[blocks - step] = lax.ppermute(held[(blocks - step + 1) % blocks], "tensor", behind)
    return [held[k] for k in range(blocks)]


def per_device(tokens, routes, route_weight, shrink_weight, expand_weight):
    toks, _ = tokens.shape
    local, rank, _ = shrink_weight.shape
    peers = lax.axis_size("expert")
    blocks = lax.axis_size("tensor")
    rows = local * rank
    group = min(8, peers)
    packed = pack(tokens, shrink_weight.reshape(rows, -1), routes.T.reshape(1, -1), peers)
    packed, block = lax.optimization_barrier((packed, expand_weight.reshape(rows, -1)))
    arrived = swap(packed)
    placed = place(ring(block, blocks), peers, rank)
    arrived, placed = lax.optimization_barrier((arrived, placed))
    partial = shrink(arrived, toks, rows, rank, group)
    vectors = swap(combine(swap(partial), route_weight.T, placed))
    return unpack(swap(expand(vectors, arrived, rank, group)))


def solution(mesh):
    return jax.shard_map(
        per_device,
        mesh=mesh,
        in_specs=(
            P(("expert", "tensor"), None),
            P(("expert", "tensor"), None),
            P(("expert", "tensor"), None),
            P("expert", None, None),
            P("expert", None, "tensor"),
        ),
        out_specs=P(("expert", "tensor"), None),
        check_vma=False,
    )
```

time: 568 us -> 148 us (0.26); the launches traced: 559 us -> 145 us
  blocking collectives: 319 us -> 73.7 us
  waiting for transfers between devices: 123 us -> 24.5 us
  local copies, waits for them, and re-layouts: 90 us -> 1.15 us
  Pallas kernels: 0 us -> 21.1 us
  starting transfers between devices: 7.59 us -> 24.6 us
  other arithmetic: 10.8 us -> 0 us
  matrix products: 7.84 us -> 0 us
    all_to_all x2 -> x3, blocking collectives: 288 us -> 73.7 us  [swap(): return lax.all_to_all(x, 'expert', split_axis=0, concat_axis=0, tiled=True)]
    all_to_all x1, waiting for transfers between devices: 123 us -> 13.9 us  [swap(): return lax.all_to_all(x, 'expert', split_axis=0, concat_axis=0, tiled=True)]
    all_gather x1 -> x0, blocking collectives: 30.6 us -> none  [per_device(): lax.all_gather(shrunk, 'tensor', axis=0, tiled=True)]
    gather x2 -> x0, local copies, waits for them, and re-layouts: 21.3 us -> none  [per_device(): jnp.take(returned, destination, axis=0).reshape(tok_rows, 2, features)]
    pallas_call x0 -> x6, Pallas kernels: none -> 21.1 us  [the longest x1 7.54 us: shrink(): pl.pallas_call(functools.partial(shrink_kernel, group, rank), grid=(peers...]
    reshape x3 -> x0, local copies, waits for them, and re-layouts: 20.8 us -> none  [the longest x1 13.5 us: per_device(): expanded.reshape(owners, local_count * CAP, features)]
    ppermute x0 -> x7, starting transfers between devices: none -> 16.9 us  [the longest x4 16.9 us: ring(): held[step] = lax.ppermute(held[step - 1], 'tensor', ahead)]
    all_to_all x1 -> x0, local copies, waits for them, and re-layouts: 16.7 us -> none  [per_device(): lax.all_to_all(columns, 'tensor', split_axis=0, concat_axis=3, tiled=True)]
  transfers between devices with their start and end apart: 1 -> 8, of which waited for: 1 -> 5; matrix products, arithmetic and copies ran while one was open for 0% -> 0% of each run, Pallas kernels for 0% -> 0%
where the time goes in v4:
time: 148 us; the launch traced here: 145 us
  blocking collectives  73.7 us (50%)
  starting transfers between devices  24.6 us (17%)
  waiting for transfers between devices  24.5 us (17%)
  Pallas kernels  21.1 us (14%)
    all_to_all x3, blocking collectives, swap(): return lax.all_to_all(x, 'expert', split_axis=0, concat_axis=0, tiled=True)  73.7 us
    ppermute x4, starting transfers between devices, ring(): held[step] = lax.ppermute(held[step - 1], 'tensor', ahead)  16.9 us
    all_to_all x1, waiting for transfers between devices, swap(): return lax.all_to_all(x, 'expert', split_axis=0, concat_axis=0, tiled=True)  13.9 us
    ppermute x4, waiting for transfers between devices, ring(): held[step] = lax.ppermute(held[step - 1], 'tensor', ahead)  10.6 us
    all_to_all x1, starting transfers between devices, swap(): return lax.all_to_all(x, 'expert', split_axis=0, concat_axis=0, tiled=True)  7.68 us
    pallas_call x1, Pallas kernels, shrink(): pl.pallas_call(functools.partial(shrink_kernel, group, rank), grid=(peers...  7.54 us
    pallas_call x1, Pallas kernels, expand(): pl.pallas_call(functools.partial(expand_kernel, group, rank), grid=(peers...  5.61 us
    pallas_call x1, Pallas kernels, pack(): pl.pallas_call(functools.partial(pack_kernel, peers, toks, rows, width),...  4.61 us
  transfers between devices with their start and end apart: 8, of which 5 were waited for; matrix products, arithmetic and copies ran while one was open for 0% of the time, Pallas kernels for 0%

profile of v4, /device:TPU:8, one launch (start us, length us, event | category | flops | bytes accessed | tf_op | source)
XLA Modules:
  0.0 145.1 jit_solution(15548230565965269861)
XLA Ops:
  0.0 4.6 %pack.1 = bf16[32,208,256]{2,1,0:T(8,128)(2,1)} custom-call(bf16[128,8192]{1,0:T(8,128)(2,1)} %tokens_ref.1, bf16[64,8192]{1,0:T(8,128)(2,1)} %bitcast.10, s32[1,256]{1,0:T(1,128)} %bitcast.11), custom_call_target="tpu_custom_call" | custom-call | tf_op jit(solution)/shard_map/pack/pallas_call | solution.py:52
  4.6 0.0 copy-start.2
  4.6 7.7 %all-to-all-start = ((bf16[32,208,256]{2,1,0:T(8,128)(2,1)}), bf16[32,208,256]{2,1,0:T(8,128)(2,1)S(1)}, u32[]{:S(2)}, u32[]{:S(2)}) async-start(bf16[32,208,256]{2,1,0:T(8,128)(2,1)} %pack.1), calls=%async_computation | async-start | bytes 6815744 | tf_op jit(solution)/shard_map/all_to_all | solution.py:243
  12.3 5.9 %collective-permute-start = (bf16[64,1024]{1,0:T(8,128)(2,1)S(1)}, bf16[64,1024]{1,0:T(8,128)(2,1)S(1)}, u32[]{:S(2)}, u32[]{:S(2)}) collective-permute-start(bf16[64,1024]{1,0:T(8,128)(2,1)S(1)} %bitcast.6), channel_id=1, source_target_pairs={{0,7},{1,0},{2,1},{3,2},{4,3},{5,4},{6,5},{7,6},{8,15},{9,8},{10,9... | collective-permute-start | bytes 393224 | tf_op jit(solution)/shard_map/ppermute | solution.py:251
  18.3 3.1 %collective-permute-done.refs_1_ = bf16[64,1024]{1,0:T(8,128)(2,1)S(1)} collective-permute-done((bf16[64,1024]{1,0:T(8,128)(2,1)S(1)}, bf16[64,1024]{1,0:T(8,128)(2,1)S(1)}, u32[]{:S(2)}, u32[]{:S(2)}) %collective-permute-start) | collective-permute-done | bytes 131104 | tf_op jit(solution)/shard_map/ppermute | solution.py:251
  21.3 3.7 %collective-permute-start.1 = (bf16[64,1024]{1,0:T(8,128)(2,1)S(1)}, bf16[64,1024]{1,0:T(8,128)(2,1)S(1)}, u32[]{:S(2)}, u32[]{:S(2)}) collective-permute-start(bf16[64,1024]{1,0:T(8,128)(2,1)S(1)} %collective-permute-done.refs_1_), channel_id=1, source_target_pairs={{0,7},{1,0},{2,1},{3,2},{4,3},{5,4},{6,5},{7,6},{8,15},{9,8},{10,9... | collective-permute-start | bytes 393224 | tf_op jit(solution)/shard_map/ppermute | solution.py:251
  25.0 2.5 %collective-permute-done.1.refs_2_ = bf16[64,1024]{1,0:T(8,128)(2,1)S(1)} collective-permute-done((bf16[64,1024]{1,0:T(8,128)(2,1)S(1)}, bf16[64,1024]{1,0:T(8,128)(2,1)S(1)}, u32[]{:S(2)}, u32[]{:S(2)}) %collective-permute-start.1) | collective-permute-done | bytes 131104 | tf_op jit(solution)/shard_map/ppermute | solution.py:251
  27.5 3.7 %collective-permute-start.2 = (bf16[64,1024]{1,0:T(8,128)(2,1)S(1)}, bf16[64,1024]{1,0:T(8,128)(2,1)S(1)}, u32[]{:S(2)}, u32[]{:S(2)}) collective-permute-start(bf16[64,1024]{1,0:T(8,128)(2,1)S(1)} %collective-permute-done.1.refs_2_), channel_id=1, source_target_pairs={{0,7},{1,0},{2,1},{3,2},{4,3},{5,4},{6,5},{7,6},{8,15},{9,8},{10,9... | collective-permute-start | bytes 393224 | tf_op jit(solution)/shard_map/ppermute | solution.py:251
  31.2 0.0 collective-permute-done.5.refs_6_
  31.2 2.5 %collective-permute-done.2.refs_3_ = bf16[64,1024]{1,0:T(8,128)(2,1)S(1)} collective-permute-done((bf16[64,1024]{1,0:T(8,128)(2,1)S(1)}, bf16[64,1024]{1,0:T(8,128)(2,1)S(1)}, u32[]{:S(2)}, u32[]{:S(2)}) %collective-permute-start.2) | collective-permute-done | bytes 131104 | tf_op jit(solution)/shard_map/ppermute | solution.py:251
  33.7 3.7 %collective-permute-start.3 = (bf16[64,1024]{1,0:T(8,128)(2,1)S(1)}, bf16[64,1024]{1,0:T(8,128)(2,1)S(1)}, u32[]{:S(2)}, u32[]{:S(2)}) collective-permute-start(bf16[64,1024]{1,0:T(8,128)(2,1)S(1)} %collective-permute-done.2.refs_3_), channel_id=1, source_target_pairs={{0,7},{1,0},{2,1},{3,2},{4,3},{5,4},{6,5},{7,6},{8,15},{9,8},{10,9... | collective-permute-start | bytes 393224 | tf_op jit(solution)/shard_map/ppermute | solution.py:251
  37.4 0.0 collective-permute-done.6.refs_5_
  37.4 2.5 %collective-permute-done.3.refs_4_ = bf16[64,1024]{1,0:T(8,128)(2,1)S(1)} collective-permute-done((bf16[64,1024]{1,0:T(8,128)(2,1)S(1)}, bf16[64,1024]{1,0:T(8,128)(2,1)S(1)}, u32[]{:S(2)}, u32[]{:S(2)}) %collective-permute-start.3) | collective-permute-done | bytes 131104 | tf_op jit(solution)/shard_map/ppermute | solution.py:251
  39.9 0.6 place.1._
  40.5 0.0 copy-start
  40.5 1.1 copy-done
  41.6 13.9 %all-to-all-done.x_ref.w_ref.r_ref = bf16[32,208,256]{2,1,0:T(8,128)(2,1)S(1)} async-done(((bf16[32,208,256]{2,1,0:T(8,128)(2,1)}), bf16[32,208,256]{2,1,0:T(8,128)(2,1)S(1)}, u32[]{:S(2)}, u32[]{:S(2)}) %all-to-all-start) | async-done | bytes 3407904 | tf_op jit(solution)/shard_map/all_to_all | solution.py:243
  55.5 7.5 %shrink.1 = bf16[32,64,128]{2,1,0:T(8,128)(2,1)S(1)} custom-call(bf16[32,208,256]{2,1,0:T(8,128)(2,1)S(1)} %all-to-all-done.x_ref.w_ref.r_ref, bf16[32,208,256]{2,1,0:T(8,128)(2,1)S(1)} %all-to-all-done.x_ref.w_ref.r_ref, bf16[32,208,256]{2,1,0:T(8,128)(2,1)S(1)} %all-to-all-done.x_ref.w_ref.r_ref), custom_call_target="tpu_custom_call" | custom-call | tf_op jit(solution)/shard_map/shrink/pallas_call | solution.py:88
  63.0 15.7 %all_to_all.20.part_ref = bf16[32,64,128]{2,1,0:T(8,128)(2,1)S(1)} all-to-all(bf16[32,64,128]{2,1,0:T(8,128)(2,1)S(1)} %shrink.1), channel_id=1, replica_groups=mesh['expert'=32,'tensor'=8] {'expert'}, dimensions={0} | all-to-all | bytes 1048576 | tf_op jit(solution)/shard_map/all_to_all | solution.py:243
  78.8 1.1 combine.1
  79.9 26.2 %all_to_all.21.s_ref.w_ref = bf16[32,96,256]{2,1,0:T(8,128)(2,1)S(1)} all-to-all(bf16[32,96,256]{2,1,0:T(8,128)(2,1)S(1)} %combine.1), channel_id=1, replica_groups=mesh['expert'=32,'tensor'=8] {'expert'}, dimensions={0} | all-to-all | bytes 3145728 | tf_op jit(solution)/shard_map/all_to_all | solution.py:243
  106.1 5.6 %expand.1 = bf16[32,256,128]{2,1,0:T(8,128)(2,1)S(1)} custom-call(bf16[32,96,256]{2,1,0:T(8,128)(2,1)S(1)} %all_to_all.21.s_ref.w_ref, bf16[32,208,256]{2,1,0:T(8,128)(2,1)S(1)} %all-to-all-done.x_ref.w_ref.r_ref, bf16[32,96,256]{2,1,0:T(8,128)(2,1)S(1)} %all_to_all.21.s_ref.w_ref), custom_call_target="tpu_custom_call" | custom-call | tf_op jit(solution)/shard_map/expand/pallas_call | solution.py:200
  111.7 31.7 %all_to_all.22.in_ref = bf16[32,256,128]{2,1,0:T(8,128)(2,1)S(1)} all-to-all(bf16[32,256,128]{2,1,0:T(8,128)(2,1)S(1)} %expand.1), channel_id=1, replica_groups=mesh['expert'=32,'tensor'=8] {'expert'}, dimensions={0} | all-to-all | bytes 4194304 | tf_op jit(solution)/shard_map/all_to_all | solution.py:243
  143.5 1.6 %unpack.1 = bf16[128,8192]{1,0:T(8,128)(2,1)} custom-call(bf16[32,256,128]{2,1,0:T(8,128)(2,1)S(1)} %all_to_all.22.in_ref), custom_call_target="tpu_custom_call" | custom-call | tf_op jit(solution)/shard_map/unpack/pallas_call | solution.py:231
  (9 shorter events, 0.0 us)
Async XLA Ops:
  4.6 7.7 %copy-start.2 = (bf16[2,32,1024]{2,1,0:T(8,128)(2,1)S(1)}, bf16[2,32,1024]{2,1,0:T(8,128)(2,1)}, u32[]{:S(2)}) copy-start(bf16[2,32,1024]{2,1,0:T(8,128)(2,1)} %param.9) | copy-start | bytes 393220
  4.6 50.8 %all-to-all-start = ((bf16[32,208,256]{2,1,0:T(8,128)(2,1)}), bf16[32,208,256]{2,1,0:T(8,128)(2,1)S(1)}, u32[]{:S(2)}, u32[]{:S(2)}) async-start(bf16[32,208,256]{2,1,0:T(8,128)(2,1)} %pack.1), calls=%async_computation | async-start | bytes 6815744 | tf_op jit(solution)/shard_map/all_to_all | solution.py:243
  12.3 9.0 %collective-permute-start = (bf16[64,1024]{1,0:T(8,128)(2,1)S(1)}, bf16[64,1024]{1,0:T(8,128)(2,1)S(1)}, u32[]{:S(2)}, u32[]{:S(2)}) collective-permute-start(bf16[64,1024]{1,0:T(8,128)(2,1)S(1)} %bitcast.6), channel_id=1, source_target_pairs={{0,7},{1,0},{2,1},{3,2},{4,3},{5,4},{6,5},{7,6},{8,15},{9,8},{10,9... | collective-permute-start | bytes 393224 | tf_op jit(solution)/shard_map/ppermute | solution.py:251
  18.3 6.8 %collective-permute-start.4 = (bf16[64,1024]{1,0:T(8,128)(2,1)S(1)}, bf16[64,1024]{1,0:T(8,128)(2,1)S(1)}, u32[]{:S(2)}, u32[]{:S(2)}) collective-permute-start(bf16[64,1024]{1,0:T(8,128)(2,1)S(1)} %bitcast.7), channel_id=1, source_target_pairs={{0,1},{1,2},{2,3},{3,4},{4,5},{5,6},{6,7},{7,0},{8,9},{9,10},{10,1... | collective-permute-start | bytes 393224 | tf_op jit(solution)/shard_map/ppermute | solution.py:253
  21.3 6.2 %collective-permute-start.1 = (bf16[64,1024]{1,0:T(8,128)(2,1)S(1)}, bf16[64,1024]{1,0:T(8,128)(2,1)S(1)}, u32[]{:S(2)}, u32[]{:S(2)}) collective-permute-start(bf16[64,1024]{1,0:T(8,128)(2,1)S(1)} %collective-permute-done.refs_1_), channel_id=1, source_target_pairs={{0,7},{1,0},{2,1},{3,2},{4,3},{5,4},{6,5},{7,6},{8,15},{9,8},{10,9... | collective-permute-start | bytes 393224 | tf_op jit(solution)/shard_map/ppermute | solution.py:251
  25.0 6.2 %collective-permute-start.5 = (bf16[64,1024]{1,0:T(8,128)(2,1)S(1)}, bf16[64,1024]{1,0:T(8,128)(2,1)S(1)}, u32[]{:S(2)}, u32[]{:S(2)}) collective-permute-start(bf16[64,1024]{1,0:T(8,128)(2,1)S(1)} %collective-permute-done.4.refs_7_), channel_id=1, source_target_pairs={{0,1},{1,2},{2,3},{3,4},{4,5},{5,6},{6,7},{7,0},{8,9},{9,10},{10,1... | collective-permute-start | bytes 393224 | tf_op jit(solution)/shard_map/ppermute | solution.py:253
  27.5 6.2 %collective-permute-start.2 = (bf16[64,1024]{1,0:T(8,128)(2,1)S(1)}, bf16[64,1024]{1,0:T(8,128)(2,1)S(1)}, u32[]{:S(2)}, u32[]{:S(2)}) collective-permute-start(bf16[64,1024]{1,0:T(8,128)(2,1)S(1)} %collective-permute-done.1.refs_2_), channel_id=1, source_target_pairs={{0,7},{1,0},{2,1},{3,2},{4,3},{5,4},{6,5},{7,6},{8,15},{9,8},{10,9... | collective-permute-start | bytes 393224 | tf_op jit(solution)/shard_map/ppermute | solution.py:251
  31.2 6.2 %collective-permute-start.6 = (bf16[64,1024]{1,0:T(8,128)(2,1)S(1)}, bf16[64,1024]{1,0:T(8,128)(2,1)S(1)}, u32[]{:S(2)}, u32[]{:S(2)}) collective-permute-start(bf16[64,1024]{1,0:T(8,128)(2,1)S(1)} %collective-permute-done.5.refs_6_), channel_id=1, source_target_pairs={{0,1},{1,2},{2,3},{3,4},{4,5},{5,6},{6,7},{7,0},{8,9},{9,10},{10,1... | collective-permute-start | bytes 393224 | tf_op jit(solution)/shard_map/ppermute | solution.py:253
  33.7 6.2 %collective-permute-start.3 = (bf16[64,1024]{1,0:T(8,128)(2,1)S(1)}, bf16[64,1024]{1,0:T(8,128)(2,1)S(1)}, u32[]{:S(2)}, u32[]{:S(2)}) collective-permute-start(bf16[64,1024]{1,0:T(8,128)(2,1)S(1)} %collective-permute-done.2.refs_3_), channel_id=1, source_target_pairs={{0,7},{1,0},{2,1},{3,2},{4,3},{5,4},{6,5},{7,6},{8,15},{9,8},{10,9... | collective-permute-start | bytes 393224 | tf_op jit(solution)/shard_map/ppermute | solution.py:251
  40.5 1.1 copy-start
  41.6 37.2 %copy-start.3 = (f32[128,2]{0,1:T(2,128)S(1)}, f32[128,2]{0,1:T(2,128)}, u32[]{:S(2)}) copy-start(f32[128,2]{0,1:T(2,128)} %param.7) | copy-start | bytes 3076
  55.5 23.3 %copy-start.1 = (bf16[32,96,256]{2,1,0:T(8,128)(2,1)S(1)}, bf16[32,96,256]{2,1,0:T(8,128)(2,1)}, u32[]{:S(2)}) copy-start(bf16[32,96,256]{2,1,0:T(8,128)(2,1)} %copy-done) | copy-start | bytes 4718596

commit v5 on v3

--- a/solution.py
+++ b/solution.py
@@ -21,19 +21,18 @@
     return pltpu.CompilerParams(vmem_limit_bytes=mib * 1024 * 1024)
 
 
-def pack_kernel(peers, toks, rows, width, tokens_ref, weight_ref, expand_ref, routes_ref, out_ref, sems):
+def first_kernel(peers, blocks, toks, width, weight_ref, expand_ref, routes_ref, out_ref, sems):
+    me = lax.axis_index("tensor")
+    halves = width // LANES
+    row = pl.multiple_of((me // halves) * TILE, TILE)
     copies = []
     for p in range(peers):
-        cols = pl.ds(p * width, width)
-        copies.append(
-            pltpu.make_async_copy(tokens_ref.at[:, cols], out_ref.at[p, pl.ds(0, toks)], sems.at[0, p])
+        col = pl.multiple_of(p * width + lax.rem(me, halves) * LANES, LANES)
+        copy = pltpu.make_async_copy(
+            weight_ref.at[pl.ds(row, TILE), pl.ds(col, LANES)], out_ref.at[p, pl.ds(0, TILE)], sems.at[p]
         )
-        copies.append(
-            pltpu.make_async_copy(weight_ref.at[:, cols], out_ref.at[p, pl.ds(toks, rows)], sems.at[1, p])
-        )
-    for c in copies:
-        c.start()
-    tail = pl.ds(toks + rows, TILE)
+        copy.start()
+        copies.append(copy)
     names = routes_ref[...].astype(F32)
     names = jnp.concatenate([names, jnp.zeros((TILE - 2, toks), F32)], axis=0).astype(BF16)
     feats = expand_ref.shape[1] // peers
@@ -43,25 +42,100 @@
             p = t * (LANES // feats) + j
             piece = block[j * feats : (j + 1) * feats]
             piece = jnp.concatenate([piece[:TILE], piece[TILE:]], axis=1)
-            out_ref[p, tail, pl.ds(0, LANES)] = piece.astype(BF16)
-            out_ref[p, tail, pl.ds(LANES, toks)] = names
-    for c in copies:
-        c.wait()
-
-
-def pack(tokens, weight, expand_weight, routes, peers):
+            out_ref[p, pl.ds(TILE, TILE), :] = piece.astype(BF16)
+            out_ref[p, pl.ds(2 * TILE, TILE), :] = names
+    for copy in copies:
+        copy.wait()
+
+
+def pack_first(weight, expand_weight, routes, peers, blocks):
+    width = weight.shape[1] // peers
+    toks = routes.shape[1]
+    return pl.pallas_call(
+        functools.partial(first_kernel, peers, blocks, toks, width),
+        out_shape=jax.ShapeDtypeStruct((peers, 3 * TILE, LANES), BF16),
+        in_specs=[HBM, VM, VM],
+        out_specs=VM,
+        scratch_shapes=[pltpu.SemaphoreType.DMA((peers,))],
+        compiler_params=params(56),
+        name="pack_first",
+    )(weight, expand_weight, routes)
+
+
+def pack_kernel(peers, width, tokens_ref, out_ref, buf, sems):
+    copies = []
+    for p in range(peers):
+        copy = pltpu.make_async_copy(tokens_ref.at[:, pl.ds(p * width, width)], buf.at[p], sems.at[0, p])
+        copy.start()
+        copies.append(copy)
+    sends = []
+    for p in range(peers):
+        copies[p].wait()
+        send = pltpu.make_async_copy(buf.at[p], out_ref.at[p], sems.at[1, p])
+        send.start()
+        sends.append(send)
+    for send in sends:
+        send.wait()
+
+
+def pack(tokens, peers):
     toks, d = tokens.shape
-    rows = weight.shape[0]
     width = d // peers
-    return pl.pallas_call(
-        functools.partial(pack_kernel, peers, toks, rows, width),
-        out_shape=jax.ShapeDtypeStruct((peers, toks + rows + TILE, width), tokens.dtype),
-        in_specs=[HBM, HBM, VM, VM],
-        out_specs=VM,
-        scratch_shapes=[pltpu.SemaphoreType.DMA((2, peers))],
+    shape = (peers, toks, width)
+    return pl.pallas_call(
+        functools.partial(pack_kernel, peers, width),
+        out_shape=jax.ShapeDtypeStruct(shape, tokens.dtype),
+        in_specs=[HBM],
+        out_specs=HBM,
+        scratch_shapes=[pltpu.VMEM(shape, tokens.dtype), pltpu.SemaphoreType.DMA((2, peers))],
+        compiler_params=params(56),
+        name="pack",
+    )(tokens)
+
+
+def place_kernel(blocks, *refs):
+    *held_refs, down_ref, up_ref, sems = refs
+    halves = down_ref.shape[2] // LANES
+    me = lax.axis_index("tensor")
+    copies = []
+    for k, ref in enumerate(held_refs):
+        owner = lax.rem(me + k, blocks)
+        row = pl.multiple_of((owner // halves) * TILE, TILE)
+        col = pl.multiple_of(lax.rem(owner, halves) * LANES, LANES)
+        copy = pltpu.make_async_copy(
+            ref.at[:, pl.ds(0, TILE), :], down_ref.at[:, pl.ds(row, TILE), pl.ds(col, LANES)], sems.at[k]
+        )
+        copy.start()
+        copies.append(copy)
+    low = lax.broadcasted_iota(jnp.int32, (TILE, LANES), 1) < LANES // 2
+    for k, ref in enumerate(held_refs):
+        row = pl.multiple_of(lax.rem(me + k, blocks) * (2 * TILE), 2 * TILE)
+        for t in range(ref.shape[0] // 2):
+            a = ref[2 * t, pl.ds(TILE, TILE), :].astype(F32)
+            b = ref[2 * t + 1, pl.ds(TILE, TILE), :].astype(F32)
+            first = jnp.where(low, a, pltpu.roll(b, LANES // 2, 1))
+            second = jnp.where(low, pltpu.roll(a, LANES // 2, 1), b)
+            both = jnp.concatenate([first, second], axis=0).astype(BF16)
+            up_ref[pl.ds(row, 2 * TILE), t * LANES : (t + 1) * LANES] = both
+    for copy in copies:
+        copy.wait()
+
+
+def place(held, rows, width):
+    peers = held[0].shape[0]
+    blocks = len(held)
+    return pl.pallas_call(
+        functools.partial(place_kernel, blocks),
+        out_shape=(
+            jax.ShapeDtypeStruct((peers, rows, width), BF16),
+            jax.ShapeDtypeStruct((blocks * 2 * TILE, peers * rows), BF16),
+        ),
+        in_specs=[VM] * blocks,
+        out_specs=(VM, VM),
+        scratch_shapes=[pltpu.SemaphoreType.DMA((blocks,))],
         compiler_params=params(16),
-        name="pack",
-    )(tokens, weight, expand_weight, routes)
+        name="place",
+    )(*held)
 
 
 def shrink_kernel(group, rank, x_ref, w_ref, r_ref, out_ref):
@@ -86,22 +160,21 @@
             out_ref[b, pl.ds(k * rank, rank), :] = acc[b][k].astype(out_ref.dtype)
 
 
-def shrink(buf, toks, rows, rank, group):
-    peers, _, width = buf.shape
-    tail = (toks + rows) // TILE
+def shrink(tokens, weight, first, rank, group):
+    peers, toks, width = tokens.shape
     return pl.pallas_call(
         functools.partial(shrink_kernel, group, rank),
         grid=(peers // group,),
         out_shape=jax.ShapeDtypeStruct((peers, 2 * rank, toks), BF16),
         in_specs=[
             pl.BlockSpec((group, toks, width), lambda i: (i, 0, 0)),
-            pl.BlockSpec((peers, rows, width), lambda i: (0, toks // rows, 0)),
-            pl.BlockSpec((group, TILE, LANES), lambda i: (i, tail, 1)),
+            pl.BlockSpec(weight.shape, lambda i: (0, 0, 0)),
+            pl.BlockSpec((group, TILE, LANES), lambda i: (i, 2, 0)),
         ],
         out_specs=pl.BlockSpec((group, 2 * rank, toks), lambda i: (i, 0, 0)),
-        compiler_params=params(32),
+        compiler_params=params(14),
         name="shrink",
-    )(buf, buf, buf)
+    )(tokens, weight, first)
 
 
 def combine_kernel(peers, rank, part_ref, gate_ref, out_ref):
@@ -129,28 +202,9 @@
     )(part, gates)
 
 
-def expand_kernel(group, experts, order, s_ref, r_ref, *refs):
-    *piece_refs, out_ref, w_ref = refs
+def expand_kernel(group, experts, s_ref, r_ref, w_ref, out_ref):
     rank = s_ref.shape[1]
     toks = s_ref.shape[2] // 2
-
-    @pl.when(pl.program_id(0) == 0)
-    def _():
-        me = lax.axis_index("tensor")
-        low = lax.broadcasted_iota(jnp.int32, (TILE, LANES), 1) < LANES // 2
-        blocks = []
-        for ref in piece_refs:
-            blocks += [ref.at[m] for m in range(ref.shape[0])]
-        for offset, ref in zip(order, blocks):
-            row = pl.multiple_of((me ^ offset) * (2 * TILE), 2 * TILE)
-            for t in range(ref.shape[0] // 2):
-                a = ref[2 * t].astype(F32)
-                b = ref[2 * t + 1].astype(F32)
-                first = jnp.where(low, a, pltpu.roll(b, LANES // 2, 1))
-                second = jnp.where(low, pltpu.roll(a, LANES // 2, 1), b)
-                both = jnp.concatenate([first, second], axis=0).astype(BF16)
-                w_ref[pl.ds(row, 2 * TILE), t * LANES : (t + 1) * LANES] = both
-
     spread = []
     for b in range(group):
         s = s_ref[b]
@@ -168,25 +222,23 @@
         out_ref[b] = out[:, b * toks : (b + 1) * toks].astype(BF16)
 
 
-def expand(vectors, arrived, pieces, order, experts, group):
-    peers, rank, toks2 = vectors.shape
+def expand(vectors, first, weight, rank, group):
+    peers, _, toks2 = vectors.shape
     toks = toks2 // 2
-    tail = arrived.shape[1] // TILE - 1
-    feats = len(order) * 2 * TILE
-    return pl.pallas_call(
-        functools.partial(expand_kernel, group, experts, order),
+    feats, cols = weight.shape
+    return pl.pallas_call(
+        functools.partial(expand_kernel, group, cols // rank),
         grid=(peers // group,),
         out_shape=jax.ShapeDtypeStruct((peers, feats, toks), BF16),
         in_specs=[
             pl.BlockSpec((group, rank, toks2), lambda i: (i, 0, 0)),
-            pl.BlockSpec((group, TILE, LANES), lambda i: (i, tail, 1)),
-        ]
-        + [pl.BlockSpec(p.shape, lambda i: (0, 0, 0, 0)) for p in pieces],
+            pl.BlockSpec((group, TILE, LANES), lambda i: (i, 2, 0)),
+            pl.BlockSpec(weight.shape, lambda i: (0, 0)),
+        ],
         out_specs=pl.BlockSpec((group, feats, toks), lambda i: (i, 0, 0)),
-        scratch_shapes=[pltpu.VMEM((feats, experts * rank), BF16)],
-        compiler_params=params(32),
+        compiler_params=params(20),
         name="expand",
-    )(vectors, arrived, *pieces)
+    )(vectors, first, weight)
 
 
 def unpack_kernel(blocks, in_ref, out_ref, buf, sems):
@@ -229,32 +281,32 @@
     return lax.all_to_all(x, "expert", split_axis=0, concat_axis=0, tiled=True)
 
 
-def across(x, blocks, offset):
-    return lax.ppermute(x, "tensor", [(i, i ^ offset) for i in range(blocks)])
+def ring(x, blocks):
+    ahead = [(i, (i - 1) % blocks) for i in range(blocks)]
+    behind = [(i, (i + 1) % blocks) for i in range(blocks)]
+    held = {0: x}
+    for step in range(1, blocks // 2 + 1):
+        held[step] = lax.ppermute(held[step - 1], "tensor", ahead)
+        if 2 * step < blocks:
+            held[blocks - step] = lax.ppermute(held[(blocks - step + 1) % blocks], "tensor", behind)
+    return [held[k] for k in range(blocks)]
 
 
 def per_device(tokens, routes, route_weight, shrink_weight, expand_weight):
-    toks, _ = tokens.shape
-    local, rank, _ = shrink_weight.shape
+    local, rank, features = shrink_weight.shape
     peers = lax.axis_size("expert")
     blocks = lax.axis_size("tensor")
     rows = local * rank
     group = min(8, peers)
-    arrived = swap(
-        pack(tokens, shrink_weight.reshape(rows, -1), expand_weight.reshape(rows, -1), routes.T, peers)
+    first = swap(
+        pack_first(shrink_weight.reshape(rows, -1), expand_weight.reshape(rows, -1), routes.T, peers, blocks)
     )
-    pieces = [arrived[None, :, toks + rows :, :LANES]]
-    order = [0]
-    offset = blocks // 2
-    while offset:
-        held = pieces[0] if len(pieces) == 1 else jnp.concatenate(pieces, axis=0)
-        pieces.append(across(held, blocks, offset))
-        order += [o ^ offset for o in order]
-        offset //= 2
-    partial = shrink(arrived, toks, rows, rank, group)
+    arrived = swap(pack(tokens, peers))
+    held = ring(first[:, : 2 * TILE], blocks)
+    arrived, (down, up) = lax.optimization_barrier((arrived, place(held, rows, features // peers)))
+    partial = shrink(arrived, down, first, rank, group)
     vectors = swap(combine(swap(partial), route_weight.T))
-    columns = expand(vectors, arrived, pieces, tuple(order), peers * local, group)
-    return unpack(swap(columns), blocks)
+    return unpack(swap(expand(vectors, first, up, rank, group)), blocks)
 
 
 def solution(mesh):

time: 157 us -> 144 us (0.917)
  the two profiles are of different devices: /device:TPU:8 before, /device:TPU:1 now
where the time goes in v5:
time: 144 us; the launch traced here: 143 us
  blocking collectives  67.8 us (47%)
  starting transfers between devices  28.3 us (20%)
  waiting for transfers between devices  25 us (17%)
  Pallas kernels  19.8 us (14%)
  local copies, waits for them, and re-layouts  2.22 us (2%)
    all_to_all x3, blocking collectives, swap(): return lax.all_to_all(x, 'expert', split_axis=0, concat_axis=0, tiled=True)  67.8 us
    ppermute x4, waiting for transfers between devices, ring(): held[step] = lax.ppermute(held[step - 1], 'tensor', ahead)  17.5 us
    ppermute x4, starting transfers between devices, ring(): held[step] = lax.ppermute(held[step - 1], 'tensor', ahead)  15.9 us
    all_to_all x2, starting transfers between devices, swap(): return lax.all_to_all(x, 'expert', split_axis=0, concat_axis=0, tiled=True)  12.4 us
    all_to_all x2, waiting for transfers between devices, swap(): return lax.all_to_all(x, 'expert', split_axis=0, concat_axis=0, tiled=True)  7.51 us
    pallas_call x1, Pallas kernels, shrink(): pl.pallas_call(functools.partial(shrink_kernel, group, rank), grid=(peers...  6.26 us
    pallas_call x1, Pallas kernels, expand(): pl.pallas_call(functools.partial(expand_kernel, group, cols // rank), gri...  5.09 us
  transfers between devices with their start and end apart: 9, of which 5 were waited for; matrix products, arithmetic and copies ran while one was open for 0% of the time, Pallas kernels for 2%

profile of v5, /device:TPU:1, one launch (start us, length us, event | category | flops | bytes accessed | tf_op | source)
XLA Modules:
  0.0 143.2 jit_solution(7899181803005737330)
XLA Ops:
  0.0 2.9 %pack_first.1 = bf16[32,48,128]{2,1,0:T(8,128)(2,1)} custom-call(bf16[64,8192]{1,0:T(8,128)(2,1)} %bitcast.5, bf16[64,1024]{1,0:T(8,128)(2,1)} %bitcast.6, s32[2,128]{1,0:T(2,128)} %bitcast.7), custom_call_target="tpu_custom_call" | custom-call | tf_op jit(solution)/shard_map/pack_first/pallas_call | solution.py:54
  2.9 8.6 %all-to-all-start.1 = ((bf16[32,48,128]{2,1,0:T(8,128)(2,1)}), bf16[32,48,128]{2,1,0:T(8,128)(2,1)S(1)}, u32[]{:S(2)}, u32[]{:S(2)}) async-start(bf16[32,48,128]{2,1,0:T(8,128)(2,1)} %pack_first.1), calls=%async_computation.1 | async-start | bytes 786432 | tf_op jit(solution)/shard_map/all_to_all | solution.py:281
  11.5 2.8 %pack.1 = bf16[32,128,256]{2,1,0:T(8,128)(2,1)} custom-call(bf16[128,8192]{1,0:T(8,128)(2,1)} %tokens_ref.1), custom_call_target="tpu_custom_call" | custom-call | tf_op jit(solution)/shard_map/pack/pallas_call | solution.py:85
  14.3 7.5 %all-to-all-done.1.r_ref = bf16[32,48,128]{2,1,0:T(8,128)(2,1)S(1)} async-done(((bf16[32,48,128]{2,1,0:T(8,128)(2,1)}), bf16[32,48,128]{2,1,0:T(8,128)(2,1)S(1)}, u32[]{:S(2)}, u32[]{:S(2)}) %all-to-all-start.1) | async-done | bytes 393248 | tf_op jit(solution)/shard_map/all_to_all | solution.py:281
  21.8 3.8 %all-to-all-start = ((bf16[32,128,256]{2,1,0:T(8,128)(2,1)}), bf16[32,128,256]{2,1,0:T(8,128)(2,1)S(1)}, u32[]{:S(2)}, u32[]{:S(2)}) async-start(bf16[32,128,256]{2,1,0:T(8,128)(2,1)} %pack.1), calls=%async_computation | async-start | bytes 4194304 | tf_op jit(solution)/shard_map/all_to_all | solution.py:281
  25.6 5.7 %collective-permute-start = (bf16[32,32,128]{2,1,0:T(8,128)(2,1)S(1)}, bf16[32,32,128]{2,1,0:T(8,128)(2,1)S(1)}, u32[]{:S(2)}, u32[]{:S(2)}) collective-permute-start(bf16[32,32,128]{2,1,0:T(8,128)(2,1)S(1)} %slice.4.refs_0_), channel_id=1, source_target_pairs={{0,7},{1,0},{2,1},{3,2},{4,3},{5,4},{6,5},{7,6},{8,15},{9,8},{10,9... | collective-permute-start | bytes 786440 | tf_op jit(solution)/shard_map/ppermute | solution.py:289
  31.3 5.6 %collective-permute-done.refs_1_ = bf16[32,32,128]{2,1,0:T(8,128)(2,1)S(1)} collective-permute-done((bf16[32,32,128]{2,1,0:T(8,128)(2,1)S(1)}, bf16[32,32,128]{2,1,0:T(8,128)(2,1)S(1)}, u32[]{:S(2)}, u32[]{:S(2)}) %collective-permute-start) | collective-permute-done | bytes 262176 | tf_op jit(solution)/shard_map/ppermute | solution.py:289
  36.9 3.4 %collective-permute-start.1 = (bf16[32,32,128]{2,1,0:T(8,128)(2,1)S(1)}, bf16[32,32,128]{2,1,0:T(8,128)(2,1)S(1)}, u32[]{:S(2)}, u32[]{:S(2)}) collective-permute-start(bf16[32,32,128]{2,1,0:T(8,128)(2,1)S(1)} %collective-permute-done.refs_1_), channel_id=1, source_target_pairs={{0,7},{1,0},{2,1},{3,2},{4,3},{5,4},{6,5},{7,6},{8,15},{9,8},{10,9... | collective-permute-start | bytes 786440 | tf_op jit(solution)/shard_map/ppermute | solution.py:289
  40.3 4.7 %collective-permute-done.1.refs_2_ = bf16[32,32,128]{2,1,0:T(8,128)(2,1)S(1)} collective-permute-done((bf16[32,32,128]{2,1,0:T(8,128)(2,1)S(1)}, bf16[32,32,128]{2,1,0:T(8,128)(2,1)S(1)}, u32[]{:S(2)}, u32[]{:S(2)}) %collective-permute-start.1) | collective-permute-done | bytes 262176 | tf_op jit(solution)/shard_map/ppermute | solution.py:289
  45.1 3.4 %collective-permute-start.2 = (bf16[32,32,128]{2,1,0:T(8,128)(2,1)S(1)}, bf16[32,32,128]{2,1,0:T(8,128)(2,1)S(1)}, u32[]{:S(2)}, u32[]{:S(2)}) collective-permute-start(bf16[32,32,128]{2,1,0:T(8,128)(2,1)S(1)} %collective-permute-done.1.refs_2_), channel_id=1, source_target_pairs={{0,7},{1,0},{2,1},{3,2},{4,3},{5,4},{6,5},{7,6},{8,15},{9,8},{10,9... | collective-permute-start | bytes 786440 | tf_op jit(solution)/shard_map/ppermute | solution.py:289
  48.5 0.0 collective-permute-done.5.refs_6_
  48.5 3.8 %collective-permute-done.2.refs_3_ = bf16[32,32,128]{2,1,0:T(8,128)(2,1)S(1)} collective-permute-done((bf16[32,32,128]{2,1,0:T(8,128)(2,1)S(1)}, bf16[32,32,128]{2,1,0:T(8,128)(2,1)S(1)}, u32[]{:S(2)}, u32[]{:S(2)}) %collective-permute-start.2) | collective-permute-done | bytes 262176 | tf_op jit(solution)/shard_map/ppermute | solution.py:289
  52.3 3.4 %collective-permute-start.3 = (bf16[32,32,128]{2,1,0:T(8,128)(2,1)S(1)}, bf16[32,32,128]{2,1,0:T(8,128)(2,1)S(1)}, u32[]{:S(2)}, u32[]{:S(2)}) collective-permute-start(bf16[32,32,128]{2,1,0:T(8,128)(2,1)S(1)} %collective-permute-done.2.refs_3_), channel_id=1, source_target_pairs={{0,7},{1,0},{2,1},{3,2},{4,3},{5,4},{6,5},{7,6},{8,15},{9,8},{10,9... | collective-permute-start | bytes 786440 | tf_op jit(solution)/shard_map/ppermute | solution.py:289
  55.7 3.3 %collective-permute-done.3.refs_4_ = bf16[32,32,128]{2,1,0:T(8,128)(2,1)S(1)} collective-permute-done((bf16[32,32,128]{2,1,0:T(8,128)(2,1)S(1)}, bf16[32,32,128]{2,1,0:T(8,128)(2,1)S(1)}, u32[]{:S(2)}, u32[]{:S(2)}) %collective-permute-start.3) | collective-permute-done | bytes 262176 | tf_op jit(solution)/shard_map/ppermute | solution.py:289
  59.1 0.8 place.1
  59.8 1.0 copy-done
  60.8 1.2 copy-done.1
  62.0 6.3 %shrink.1 = bf16[32,64,128]{2,1,0:T(8,128)(2,1)S(1)} custom-call(bf16[32,128,256]{2,1,0:T(8,128)(2,1)S(1)} %all-to-all-done.x_ref, bf16[32,64,256]{2,1,0:T(8,128)(2,1)S(1)} %copy-done.1, bf16[32,48,128]{2,1,0:T(8,128)(2,1)S(1)} %all-to-all-done.1.r_ref), custom_call_target="tpu_custom_call" | custom-call | tf_op jit(solution)/shard_map/shrink/pallas_call | solution.py:165
  68.3 21.2 %all_to_all.25.part_ref = bf16[32,64,128]{2,1,0:T(8,128)(2,1)S(1)} all-to-all(bf16[32,64,128]{2,1,0:T(8,128)(2,1)S(1)} %shrink.1), channel_id=1, replica_groups=mesh['expert'=32,'tensor'=8] {'expert'}, dimensions={0} | all-to-all | bytes 1048576 | tf_op jit(solution)/shard_map/all_to_all | solution.py:281
  89.5 0.1 combine.1
  89.6 15.0 %all_to_all.26.s_ref = bf16[32,32,256]{2,1,0:T(8,128)(2,1)S(1)} all-to-all(bf16[32,32,256]{2,1,0:T(8,128)(2,1)S(1)} %combine.1), channel_id=1, replica_groups=mesh['expert'=32,'tensor'=8] {'expert'}, dimensions={0} | all-to-all | bytes 1048576 | tf_op jit(solution)/shard_map/all_to_all | solution.py:281
  104.6 5.1 %expand.1 = bf16[32,256,128]{2,1,0:T(8,128)(2,1)S(1)} custom-call(bf16[32,32,256]{2,1,0:T(8,128)(2,1)S(1)} %all_to_all.26.s_ref, bf16[32,48,128]{2,1,0:T(8,128)(2,1)S(1)} %all-to-all-done.1.r_ref, bf16[256,2048]{1,0:T(8,128)(2,1)S(1)} %get-tuple-element.14.w_ref), custom_call_target="tpu_custom_call" | custom-call | tf_op jit(solution)/shard_map/expand/pallas_call | solution.py:229
  109.7 31.6 %all_to_all.27.in_ref = bf16[32,256,128]{2,1,0:T(8,128)(2,1)S(1)} all-to-all(bf16[32,256,128]{2,1,0:T(8,128)(2,1)S(1)} %expand.1), channel_id=1, replica_groups=mesh['expert'=32,'tensor'=8] {'expert'}, dimensions={0} | all-to-all | bytes 4194304 | tf_op jit(solution)/shard_map/all_to_all | solution.py:281
  141.3 1.9 %unpack.1 = bf16[128,8192]{1,0:T(8,128)(2,1)} custom-call(bf16[32,256,128]{2,1,0:T(8,128)(2,1)S(1)} %all_to_all.27.in_ref), custom_call_target="tpu_custom_call" | custom-call | tf_op jit(solution)/shard_map/unpack/pallas_call | solution.py:266
  (11 shorter events, 0.0 us)
Async XLA Ops:
  2.9 18.9 %all-to-all-start.1 = ((bf16[32,48,128]{2,1,0:T(8,128)(2,1)}), bf16[32,48,128]{2,1,0:T(8,128)(2,1)S(1)}, u32[]{:S(2)}, u32[]{:S(2)}) async-start(bf16[32,48,128]{2,1,0:T(8,128)(2,1)} %pack_first.1), calls=%async_computation.1 | async-start | bytes 786432 | tf_op jit(solution)/shard_map/all_to_all | solution.py:281
  21.8 39.0 %all-to-all-start = ((bf16[32,128,256]{2,1,0:T(8,128)(2,1)}), bf16[32,128,256]{2,1,0:T(8,128)(2,1)S(1)}, u32[]{:S(2)}, u32[]{:S(2)}) async-start(bf16[32,128,256]{2,1,0:T(8,128)(2,1)} %pack.1), calls=%async_computation | async-start | bytes 4194304 | tf_op jit(solution)/shard_map/all_to_all | solution.py:281
  25.6 11.3 %collective-permute-start = (bf16[32,32,128]{2,1,0:T(8,128)(2,1)S(1)}, bf16[32,32,128]{2,1,0:T(8,128)(2,1)S(1)}, u32[]{:S(2)}, u32[]{:S(2)}) collective-permute-start(bf16[32,32,128]{2,1,0:T(8,128)(2,1)S(1)} %slice.4.refs_0_), channel_id=1, source_target_pairs={{0,7},{1,0},{2,1},{3,2},{4,3},{5,4},{6,5},{7,6},{8,15},{9,8},{10,9... | collective-permute-start | bytes 786440 | tf_op jit(solution)/shard_map/ppermute | solution.py:289
  31.3 9.1 %collective-permute-start.4 = (bf16[32,32,128]{2,1,0:T(8,128)(2,1)S(1)}, bf16[32,32,128]{2,1,0:T(8,128)(2,1)S(1)}, u32[]{:S(2)}, u32[]{:S(2)}) collective-permute-start(bf16[32,32,128]{2,1,0:T(8,128)(2,1)S(1)} %slice.4.refs_0_), channel_id=1, source_target_pairs={{0,1},{1,2},{2,3},{3,4},{4,5},{5,6},{6,7},{7,0},{8,9},{9,10},{10,1... | collective-permute-start | bytes 786440 | tf_op jit(solution)/shard_map/ppermute | solution.py:291
  36.9 8.2 %collective-permute-start.1 = (bf16[32,32,128]{2,1,0:T(8,128)(2,1)S(1)}, bf16[32,32,128]{2,1,0:T(8,128)(2,1)S(1)}, u32[]{:S(2)}, u32[]{:S(2)}) collective-permute-start(bf16[32,32,128]{2,1,0:T(8,128)(2,1)S(1)} %collective-permute-done.refs_1_), channel_id=1, source_target_pairs={{0,7},{1,0},{2,1},{3,2},{4,3},{5,4},{6,5},{7,6},{8,15},{9,8},{10,9... | collective-permute-start | bytes 786440 | tf_op jit(solution)/shard_map/ppermute | solution.py:289
  40.3 8.2 %collective-permute-start.5 = (bf16[32,32,128]{2,1,0:T(8,128)(2,1)S(1)}, bf16[32,32,128]{2,1,0:T(8,128)(2,1)S(1)}, u32[]{:S(2)}, u32[]{:S(2)}) collective-permute-start(bf16[32,32,128]{2,1,0:T(8,128)(2,1)S(1)} %collective-permute-done.4.refs_7_), channel_id=1, source_target_pairs={{0,1},{1,2},{2,3},{3,4},{4,5},{5,6},{6,7},{7,0},{8,9},{9,10},{10,1... | collective-permute-start | bytes 786440 | tf_op jit(solution)/shard_map/ppermute | solution.py:291
  45.1 7.2 %collective-permute-start.2 = (bf16[32,32,128]{2,1,0:T(8,128)(2,1)S(1)}, bf16[32,32,128]{2,1,0:T(8,128)(2,1)S(1)}, u32[]{:S(2)}, u32[]{:S(2)}) collective-permute-start(bf16[32,32,128]{2,1,0:T(8,128)(2,1)S(1)} %collective-permute-done.1.refs_2_), channel_id=1, source_target_pairs={{0,7},{1,0},{2,1},{3,2},{4,3},{5,4},{6,5},{7,6},{8,15},{9,8},{10,9... | collective-permute-start | bytes 786440 | tf_op jit(solution)/shard_map/ppermute | solution.py:289
  48.5 7.2 %collective-permute-start.6 = (bf16[32,32,128]{2,1,0:T(8,128)(2,1)S(1)}, bf16[32,32,128]{2,1,0:T(8,128)(2,1)S(1)}, u32[]{:S(2)}, u32[]{:S(2)}) collective-permute-start(bf16[32,32,128]{2,1,0:T(8,128)(2,1)S(1)} %collective-permute-done.5.refs_6_), channel_id=1, source_target_pairs={{0,1},{1,2},{2,3},{3,4},{4,5},{5,6},{6,7},{7,0},{8,9},{9,10},{10,1... | collective-permute-start | bytes 786440 | tf_op jit(solution)/shard_map/ppermute | solution.py:291
  52.3 6.7 %collective-permute-start.3 = (bf16[32,32,128]{2,1,0:T(8,128)(2,1)S(1)}, bf16[32,32,128]{2,1,0:T(8,128)(2,1)S(1)}, u32[]{:S(2)}, u32[]{:S(2)}) collective-permute-start(bf16[32,32,128]{2,1,0:T(8,128)(2,1)S(1)} %collective-permute-done.2.refs_3_), channel_id=1, source_target_pairs={{0,7},{1,0},{2,1},{3,2},{4,3},{5,4},{6,5},{7,6},{8,15},{9,8},{10,9... | collective-permute-start | bytes 786440 | tf_op jit(solution)/shard_map/ppermute | solution.py:289
  59.8 1.0 copy-start
  60.8 1.2 copy-start.1
  62.0 27.4 %copy-start.2 = (f32[128,2]{0,1:T(2,128)S(1)}, f32[128,2]{0,1:T(2,128)}, u32[]{:S(2)}) copy-start(f32[128,2]{0,1:T(2,128)} %param.7) | copy-start | bytes 3076

commit v6 on v5

--- a/solution.py
+++ b/solution.py
@@ -21,10 +21,16 @@
     return pltpu.CompilerParams(vmem_limit_bytes=mib * 1024 * 1024)
 
 
-def first_kernel(peers, blocks, toks, width, weight_ref, expand_ref, routes_ref, out_ref, sems):
+def first_kernel(peers, blocks, toks, width, weight_ref, expand_hbm, routes_hbm, out_ref, expand_ref, routes_ref, sems):
     me = lax.axis_index("tensor")
     halves = width // LANES
     row = pl.multiple_of((me // halves) * TILE, TILE)
+    reads = [
+        pltpu.make_async_copy(expand_hbm, expand_ref, sems.at[peers]),
+        pltpu.make_async_copy(routes_hbm, routes_ref, sems.at[peers + 1]),
+    ]
+    for read in reads:
+        read.start()
     copies = []
     for p in range(peers):
         col = pl.multiple_of(p * width + lax.rem(me, halves) * LANES, LANES)
@@ -33,6 +39,8 @@
         )
         copy.start()
         copies.append(copy)
+    for read in reads:
+        read.wait()
     names = routes_ref[...].astype(F32)
     names = jnp.concatenate([names, jnp.zeros((TILE - 2, toks), F32)], axis=0).astype(BF16)
     feats = expand_ref.shape[1] // peers
@@ -54,9 +62,13 @@
     return pl.pallas_call(
         functools.partial(first_kernel, peers, blocks, toks, width),
         out_shape=jax.ShapeDtypeStruct((peers, 3 * TILE, LANES), BF16),
-        in_specs=[HBM, VM, VM],
+        in_specs=[HBM, HBM, HBM],
         out_specs=VM,
-        scratch_shapes=[pltpu.SemaphoreType.DMA((peers,))],
+        scratch_shapes=[
+            pltpu.VMEM(expand_weight.shape, BF16),
+            pltpu.VMEM(routes.shape, routes.dtype),
+            pltpu.SemaphoreType.DMA((peers + 2,)),
+        ],
         compiler_params=params(56),
         name="pack_first",
     )(weight, expand_weight, routes)
@@ -95,6 +107,7 @@
 
 def place_kernel(blocks, *refs):
     *held_refs, down_ref, up_ref, sems = refs
+    held_refs, more_refs = held_refs[:blocks], held_refs[blocks:]
     halves = down_ref.shape[2] // LANES
     me = lax.axis_index("tensor")
     copies = []
@@ -103,16 +116,16 @@
         row = pl.multiple_of((owner // halves) * TILE, TILE)
         col = pl.multiple_of(lax.rem(owner, halves) * LANES, LANES)
         copy = pltpu.make_async_copy(
-            ref.at[:, pl.ds(0, TILE), :], down_ref.at[:, pl.ds(row, TILE), pl.ds(col, LANES)], sems.at[k]
+            ref, down_ref.at[:, pl.ds(row, TILE), pl.ds(col, LANES)], sems.at[k]
         )
         copy.start()
         copies.append(copy)
     low = lax.broadcasted_iota(jnp.int32, (TILE, LANES), 1) < LANES // 2
-    for k, ref in enumerate(held_refs):
+    for k, ref in enumerate(more_refs):
         row = pl.multiple_of(lax.rem(me + k, blocks) * (2 * TILE), 2 * TILE)
         for t in range(ref.shape[0] // 2):
-            a = ref[2 * t, pl.ds(TILE, TILE), :].astype(F32)
-            b = ref[2 * t + 1, pl.ds(TILE, TILE), :].astype(F32)
+            a = ref[2 * t].astype(F32)
+            b = ref[2 * t + 1].astype(F32)
             first = jnp.where(low, a, pltpu.roll(b, LANES // 2, 1))
             second = jnp.where(low, pltpu.roll(a, LANES // 2, 1), b)
             both = jnp.concatenate([first, second], axis=0).astype(BF16)
@@ -121,7 +134,7 @@
         copy.wait()
 
 
-def place(held, rows, width):
+def place(held, more, rows, width):
     peers = held[0].shape[0]
     blocks = len(held)
     return pl.pallas_call(
@@ -130,12 +143,12 @@
             jax.ShapeDtypeStruct((peers, rows, width), BF16),
             jax.ShapeDtypeStruct((blocks * 2 * TILE, peers * rows), BF16),
         ),
-        in_specs=[VM] * blocks,
+        in_specs=[VM] * (2 * blocks),
         out_specs=(VM, VM),
         scratch_shapes=[pltpu.SemaphoreType.DMA((blocks,))],
         compiler_params=params(16),
         name="place",
-    )(*held)
+    )(*held, *more)
 
 
 def shrink_kernel(group, rank, x_ref, w_ref, r_ref, out_ref):
@@ -302,8 +315,9 @@
         pack_first(shrink_weight.reshape(rows, -1), expand_weight.reshape(rows, -1), routes.T, peers, blocks)
     )
     arrived = swap(pack(tokens, peers))
-    held = ring(first[:, : 2 * TILE], blocks)
-    arrived, (down, up) = lax.optimization_barrier((arrived, place(held, rows, features // peers)))
+    downs, ups = ring(first[:, :TILE], blocks), ring(first[:, TILE : 2 * TILE], blocks)
+    arrived, last = lax.optimization_barrier((arrived, downs[-1]))
+    down, up = place(downs[:-1] + [last], ups, rows, features // peers)
     partial = shrink(arrived, down, first, rank, group)
     vectors = swap(combine(swap(partial), route_weight.T))
     return unpack(swap(expand(vectors, first, up, rank, group)), blocks)

time: 144 us -> 140 us (0.972)
  waiting for transfers between devices: 25 us -> 14.8 us
  starting transfers between devices: 28.3 us -> 36.1 us
  local copies, waits for them, and re-layouts: 2.22 us -> 0.03 us
    ppermute x4 -> x8, waiting for transfers between devices: 17.5 us -> 3.83 us  [ring(): held[step] = lax.ppermute(held[step - 1], 'tensor', ahead)]
    ppermute x4 -> x8, starting transfers between devices: 15.9 us -> 23 us  [ring(): held[step] = lax.ppermute(held[step - 1], 'tensor', ahead)]
    ppermute x3 -> x6, waiting for transfers between devices: 0.01 us -> 2.4 us  [ring(): lax.ppermute(held[(blocks - step + 1) % blocks], 'tensor', behind)]
    unnamed x6 -> x2, local copies, waits for them, and re-layouts: 2.2 us -> 0.01 us
  transfers between devices with their start and end apart: 9 -> 16, of which waited for: 5 -> 7; matrix products, arithmetic and copies ran while one was open for 0% -> 0% of each run, Pallas kernels for 2% -> 2%
where the time goes in v6:
time: 140 us; the launch traced here: 139 us
  blocking collectives  67.7 us (48%)
  starting transfers between devices  36.1 us (26%)
  Pallas kernels  20.6 us (15%)
  waiting for transfers between devices  14.8 us (11%)
    all_to_all x3, blocking collectives, swap(): return lax.all_to_all(x, 'expert', split_axis=0, concat_axis=0, tiled=True)  67.7 us
    ppermute x8, starting transfers between devices, ring(): held[step] = lax.ppermute(held[step - 1], 'tensor', ahead)  23 us
    all_to_all x2, starting transfers between devices, swap(): return lax.all_to_all(x, 'expert', split_axis=0, concat_axis=0, tiled=True)  12.4 us
    all_to_all x2, waiting for transfers between devices, swap(): return lax.all_to_all(x, 'expert', split_axis=0, concat_axis=0, tiled=True)  8.58 us
    pallas_call x1, Pallas kernels, shrink(): pl.pallas_call(functools.partial(shrink_kernel, group, rank), grid=(peers...  6.3 us
    pallas_call x1, Pallas kernels, expand(): pl.pallas_call(functools.partial(expand_kernel, group, cols // rank), gri...  5.09 us
    ppermute x8, waiting for transfers between devices, ring(): held[step] = lax.ppermute(held[step - 1], 'tensor', ahead)  3.83 us
  transfers between devices with their start and end apart: 16, of which 7 were waited for; matrix products, arithmetic and copies ran while one was open for 0% of the time, Pallas kernels for 2%

profile of v6, /device:TPU:1, one launch (start us, length us, event | category | flops | bytes accessed | tf_op | source)
XLA Modules:
  0.0 139.5 jit_solution(3563659263359083728)
XLA Ops:
  0.0 2.3 %pack_first.1 = bf16[32,48,128]{2,1,0:T(8,128)(2,1)} custom-call(bf16[64,8192]{1,0:T(8,128)(2,1)} %bitcast.5, bf16[64,1024]{1,0:T(8,128)(2,1)} %bitcast.6, s32[2,128]{1,0:T(2,128)} %bitcast.7), custom_call_target="tpu_custom_call" | custom-call | tf_op jit(solution)/shard_map/pack_first/pallas_call | solution.py:62
  2.3 8.6 %all-to-all-start.1 = ((bf16[32,48,128]{2,1,0:T(8,128)(2,1)}), bf16[32,48,128]{2,1,0:T(8,128)(2,1)S(1)}, u32[]{:S(2)}, u32[]{:S(2)}) async-start(bf16[32,48,128]{2,1,0:T(8,128)(2,1)} %pack_first.1), calls=%async_computation.1 | async-start | bytes 786432 | tf_op jit(solution)/shard_map/all_to_all | solution.py:294
  10.9 2.8 %pack.1 = bf16[32,128,256]{2,1,0:T(8,128)(2,1)} custom-call(bf16[128,8192]{1,0:T(8,128)(2,1)} %tokens_ref.1), custom_call_target="tpu_custom_call" | custom-call | tf_op jit(solution)/shard_map/pack/pallas_call | solution.py:97
  13.7 7.5 %all-to-all-done.1.r_ref = bf16[32,48,128]{2,1,0:T(8,128)(2,1)S(1)} async-done(((bf16[32,48,128]{2,1,0:T(8,128)(2,1)}), bf16[32,48,128]{2,1,0:T(8,128)(2,1)S(1)}, u32[]{:S(2)}, u32[]{:S(2)}) %all-to-all-start.1) | async-done | bytes 393248 | tf_op jit(solution)/shard_map/all_to_all | solution.py:294
  21.2 3.8 %all-to-all-start = ((bf16[32,128,256]{2,1,0:T(8,128)(2,1)}), bf16[32,128,256]{2,1,0:T(8,128)(2,1)S(1)}, u32[]{:S(2)}, u32[]{:S(2)}) async-start(bf16[32,128,256]{2,1,0:T(8,128)(2,1)} %pack.1), calls=%async_computation | async-start | bytes 4194304 | tf_op jit(solution)/shard_map/all_to_all | solution.py:294
  25.1 5.7 %collective-permute-start.1 = (bf16[32,16,128]{2,1,0:T(8,128)(2,1)S(1)}, bf16[32,16,128]{2,1,0:T(8,128)(2,1)S(1)}, u32[]{:S(2)}, u32[]{:S(2)}) collective-permute-start(bf16[32,16,128]{2,1,0:T(8,128)(2,1)S(1)} %get-tuple-element.14.refs_0_), channel_id=1, source_target_pairs={{0,7},{1,0},{2,1},{3,2},{4,3},{5,4},{6,5},{7,6},{8,15},{9,8},{10,9... | collective-permute-start | bytes 393224 | tf_op jit(solution)/shard_map/ppermute | solution.py:302
  31.5 0.7 collective-permute-start
  32.2 1.3 collective-permute-done.1.refs_1_
  33.6 3.4 %collective-permute-start.2 = (bf16[32,16,128]{2,1,0:T(8,128)(2,1)S(1)}, bf16[32,16,128]{2,1,0:T(8,128)(2,1)S(1)}, u32[]{:S(2)}, u32[]{:S(2)}) collective-permute-start(bf16[32,16,128]{2,1,0:T(8,128)(2,1)S(1)} %collective-permute-done.1.refs_1_), channel_id=1, source_target_pairs={{0,7},{1,0},{2,1},{3,2},{4,3},{5,4},{6,5},{7,6},{8,15},{9,8},{10,9... | collective-permute-start | bytes 393224 | tf_op jit(solution)/shard_map/ppermute | solution.py:302
  37.0 2.8 %collective-permute-start.8 = (bf16[32,16,128]{2,1,0:T(8,128)(2,1)S(1)}, bf16[32,16,128]{2,1,0:T(8,128)(2,1)S(1)}, u32[]{:S(2)}, u32[]{:S(2)}) collective-permute-start(bf16[32,16,128]{2,1,0:T(8,128)(2,1)S(1)} %collective-permute-done.7.refs_9_), channel_id=1, source_target_pairs={{0,7},{1,0},{2,1},{3,2},{4,3},{5,4},{6,5},{7,6},{8,15},{9,8},{10,9... | collective-permute-start | bytes 393224 | tf_op jit(solution)/shard_map/ppermute | solution.py:302
  39.9 2.7 %collective-permute-start.3 = (bf16[32,16,128]{2,1,0:T(8,128)(2,1)S(1)}, bf16[32,16,128]{2,1,0:T(8,128)(2,1)}, u32[]{:S(2)}, u32[]{:S(2)}) collective-permute-start(bf16[32,16,128]{2,1,0:T(8,128)(2,1)S(1)} %collective-permute-done.2.refs_2_), channel_id=1, source_target_pairs={{0,7},{1,0},{2,1},{3,2},{4,3},{5,4},{6,5},{7,6},{8,15},{9,8},{10,9... | collective-permute-start | bytes 393224 | tf_op jit(solution)/shard_map/ppermute | solution.py:302
  42.6 3.4 %collective-permute-start.9 = (bf16[32,16,128]{2,1,0:T(8,128)(2,1)S(1)}, bf16[32,16,128]{2,1,0:T(8,128)(2,1)}, u32[]{:S(2)}, u32[]{:S(2)}) collective-permute-start(bf16[32,16,128]{2,1,0:T(8,128)(2,1)S(1)} %collective-permute-done.8.refs_10_), channel_id=1, source_target_pairs={{0,7},{1,0},{2,1},{3,2},{4,3},{5,4},{6,5},{7,6},{8,15},{9,8},{10,9... | collective-permute-start | bytes 393224 | tf_op jit(solution)/shard_map/ppermute | solution.py:302
  46.0 1.8 %collective-permute-done.12.refs_14_ = bf16[32,16,128]{2,1,0:T(8,128)(2,1)} collective-permute-done((bf16[32,16,128]{2,1,0:T(8,128)(2,1)S(1)}, bf16[32,16,128]{2,1,0:T(8,128)(2,1)}, u32[]{:S(2)}, u32[]{:S(2)}) %collective-permute-start.12) | collective-permute-done | bytes 131104 | tf_op jit(solution)/shard_map/ppermute | solution.py:304
  47.8 2.7 %collective-permute-start.4 = (bf16[32,16,128]{2,1,0:T(8,128)(2,1)}, bf16[32,16,128]{2,1,0:T(8,128)(2,1)}, u32[]{:S(2)}, u32[]{:S(2)}) collective-permute-start(bf16[32,16,128]{2,1,0:T(8,128)(2,1)} %collective-permute-done.3.refs_3_), channel_id=1, source_target_pairs={{0,7},{1,0},{2,1},{3,2},{4,3},{5,4},{6,5},{7,6},{8,15},{9,8},{10,9... | collective-permute-start | bytes 393224 | tf_op jit(solution)/shard_map/ppermute | solution.py:302
  50.5 1.6 %collective-permute-start.10 = (bf16[32,16,128]{2,1,0:T(8,128)(2,1)}, bf16[32,16,128]{2,1,0:T(8,128)(2,1)}, u32[]{:S(2)}, u32[]{:S(2)}) collective-permute-start(bf16[32,16,128]{2,1,0:T(8,128)(2,1)} %collective-permute-done.9.refs_11_), channel_id=1, source_target_pairs={{0,7},{1,0},{2,1},{3,2},{4,3},{5,4},{6,5},{7,6},{8,15},{9,8},{10,9... | collective-permute-start | bytes 393224 | tf_op jit(solution)/shard_map/ppermute | solution.py:302
  52.1 1.1 all-to-all-done.x_ref
  53.7 2.5 %collective-permute-done.10.refs_12_ = bf16[32,16,128]{2,1,0:T(8,128)(2,1)} collective-permute-done((bf16[32,16,128]{2,1,0:T(8,128)(2,1)}, bf16[32,16,128]{2,1,0:T(8,128)(2,1)}, u32[]{:S(2)}, u32[]{:S(2)}) %collective-permute-start.10) | collective-permute-done | bytes 131104 | tf_op jit(solution)/shard_map/ppermute | solution.py:302
  56.1 2.0 %place.1 = (bf16[32,64,256]{2,1,0:T(8,128)(2,1)S(1)}, bf16[256,2048]{1,0:T(8,128)(2,1)S(1)}) custom-call(bf16[32,16,128]{2,1,0:T(8,128)(2,1)S(1)} %get-tuple-element.14.refs_0_, bf16[32,16,128]{2,1,0:T(8,128)(2,1)S(1)} %collective-permute-done.1.refs_1_, bf16[32,16,128]{2,1,0:T(8,128)(2,1)S(1)} %collective-permute-done.2.refs_2_, ...), custom_call_target="tpu_custom_call" | custom-call | tf_op jit(solution)/shard_map/place/pallas_call | solution.py:140
  58.2 6.3 %shrink.1 = bf16[32,64,128]{2,1,0:T(8,128)(2,1)S(1)} custom-call(bf16[32,128,256]{2,1,0:T(8,128)(2,1)S(1)} %all-to-all-done.x_ref, bf16[32,64,256]{2,1,0:T(8,128)(2,1)S(1)} %get-tuple-element.11.w_ref, bf16[32,48,128]{2,1,0:T(8,128)(2,1)S(1)} %all-to-all-done.1.r_ref), custom_call_target="tpu_custom_call" | custom-call | tf_op jit(solution)/shard_map/shrink/pallas_call | solution.py:178
  64.5 21.1 %all_to_all.25.part_ref = bf16[32,64,128]{2,1,0:T(8,128)(2,1)S(1)} all-to-all(bf16[32,64,128]{2,1,0:T(8,128)(2,1)S(1)} %shrink.1), channel_id=1, replica_groups=mesh['expert'=32,'tensor'=8] {'expert'}, dimensions={0} | all-to-all | bytes 1048576 | tf_op jit(solution)/shard_map/all_to_all | solution.py:294
  85.7 15.0 %all_to_all.26.s_ref = bf16[32,32,256]{2,1,0:T(8,128)(2,1)S(1)} all-to-all(bf16[32,32,256]{2,1,0:T(8,128)(2,1)S(1)} %combine.1), channel_id=1, replica_groups=mesh['expert'=32,'tensor'=8] {'expert'}, dimensions={0} | all-to-all | bytes 1048576 | tf_op jit(solution)/shard_map/all_to_all | solution.py:294
  100.7 5.1 %expand.1 = bf16[32,256,128]{2,1,0:T(8,128)(2,1)S(1)} custom-call(bf16[32,32,256]{2,1,0:T(8,128)(2,1)S(1)} %all_to_all.26.s_ref, bf16[32,48,128]{2,1,0:T(8,128)(2,1)S(1)} %all-to-all-done.1.r_ref, bf16[256,2048]{1,0:T(8,128)(2,1)S(1)} %get-tuple-element.12.w_ref), custom_call_target="tpu_custom_call" | custom-call | tf_op jit(solution)/shard_map/expand/pallas_call | solution.py:242
  105.8 31.6 %all_to_all.27.in_ref = bf16[32,256,128]{2,1,0:T(8,128)(2,1)S(1)} all-to-all(bf16[32,256,128]{2,1,0:T(8,128)(2,1)S(1)} %expand.1), channel_id=1, replica_groups=mesh['expert'=32,'tensor'=8] {'expert'}, dimensions={0} | all-to-all | bytes 4194304 | tf_op jit(solution)/shard_map/all_to_all | solution.py:294
  137.4 1.9 %unpack.1 = bf16[128,8192]{1,0:T(8,128)(2,1)} custom-call(bf16[32,256,128]{2,1,0:T(8,128)(2,1)S(1)} %all_to_all.27.in_ref), custom_call_target="tpu_custom_call" | custom-call | tf_op jit(solution)/shard_map/unpack/pallas_call | solution.py:279
  (21 shorter events, 1.5 us)
Async XLA Ops:
  2.3 18.9 %all-to-all-start.1 = ((bf16[32,48,128]{2,1,0:T(8,128)(2,1)}), bf16[32,48,128]{2,1,0:T(8,128)(2,1)S(1)}, u32[]{:S(2)}, u32[]{:S(2)}) async-start(bf16[32,48,128]{2,1,0:T(8,128)(2,1)} %pack_first.1), calls=%async_computation.1 | async-start | bytes 786432 | tf_op jit(solution)/shard_map/all_to_all | solution.py:294
  21.2 31.9 %all-to-all-start = ((bf16[32,128,256]{2,1,0:T(8,128)(2,1)}), bf16[32,128,256]{2,1,0:T(8,128)(2,1)S(1)}, u32[]{:S(2)}, u32[]{:S(2)}) async-start(bf16[32,128,256]{2,1,0:T(8,128)(2,1)} %pack.1), calls=%async_computation | async-start | bytes 4194304 | tf_op jit(solution)/shard_map/all_to_all | solution.py:294
  25.1 8.5 %collective-permute-start.1 = (bf16[32,16,128]{2,1,0:T(8,128)(2,1)S(1)}, bf16[32,16,128]{2,1,0:T(8,128)(2,1)S(1)}, u32[]{:S(2)}, u32[]{:S(2)}) collective-permute-start(bf16[32,16,128]{2,1,0:T(8,128)(2,1)S(1)} %get-tuple-element.14.refs_0_), channel_id=1, source_target_pairs={{0,7},{1,0},{2,1},{3,2},{4,3},{5,4},{6,5},{7,6},{8,15},{9,8},{10,9... | collective-permute-start | bytes 393224 | tf_op jit(solution)/shard_map/ppermute | solution.py:302
  30.7 6.3 %collective-permute-start.7 = (bf16[32,16,128]{2,1,0:T(8,128)(2,1)S(1)}, bf16[32,16,128]{2,1,0:T(8,128)(2,1)S(1)}, u32[]{:S(2)}, u32[]{:S(2)}) collective-permute-start(bf16[32,16,128]{2,1,0:T(8,128)(2,1)S(1)} %get-tuple-element.13.refs_8_), channel_id=1, source_target_pairs={{0,7},{1,0},{2,1},{3,2},{4,3},{5,4},{6,5},{7,6},{8,15},{9,8},{10,9... | collective-permute-start | bytes 393224 | tf_op jit(solution)/shard_map/ppermute | solution.py:302
  31.5 8.3 %collective-permute-start = (bf16[32,16,128]{2,1,0:T(8,128)(2,1)S(1)}, bf16[32,16,128]{2,1,0:T(8,128)(2,1)S(1)}, u32[]{:S(2)}, u32[]{:S(2)}) collective-permute-start(bf16[32,16,128]{2,1,0:T(8,128)(2,1)S(1)} %get-tuple-element.14.refs_0_), channel_id=1, source_target_pairs={{0,1},{1,2},{2,3},{3,4},{4,5},{5,6},{6,7},{7,0},{8,9},{9,10},{10,1... | collective-permute-start | bytes 393224 | tf_op jit(solution)/shard_map/ppermute | solution.py:304
  32.2 7.7 %collective-permute-start.11 = (bf16[32,16,128]{2,1,0:T(8,128)(2,1)S(1)}, bf16[32,16,128]{2,1,0:T(8,128)(2,1)S(1)}, u32[]{:S(2)}, u32[]{:S(2)}) collective-permute-start(bf16[32,16,128]{2,1,0:T(8,128)(2,1)S(1)} %get-tuple-element.13.refs_8_), channel_id=1, source_target_pairs={{0,1},{1,2},{2,3},{3,4},{4,5},{5,6},{6,7},{7,0},{8,9},{9,10},{10,1... | collective-permute-start | bytes 393224 | tf_op jit(solution)/shard_map/ppermute | solution.py:304
  33.6 6.3 %collective-permute-start.2 = (bf16[32,16,128]{2,1,0:T(8,128)(2,1)S(1)}, bf16[32,16,128]{2,1,0:T(8,128)(2,1)S(1)}, u32[]{:S(2)}, u32[]{:S(2)}) collective-permute-start(bf16[32,16,128]{2,1,0:T(8,128)(2,1)S(1)} %collective-permute-done.1.refs_1_), channel_id=1, source_target_pairs={{0,7},{1,0},{2,1},{3,2},{4,3},{5,4},{6,5},{7,6},{8,15},{9,8},{10,9... | collective-permute-start | bytes 393224 | tf_op jit(solution)/shard_map/ppermute | solution.py:302
  37.0 5.6 %collective-permute-start.8 = (bf16[32,16,128]{2,1,0:T(8,128)(2,1)S(1)}, bf16[32,16,128]{2,1,0:T(8,128)(2,1)S(1)}, u32[]{:S(2)}, u32[]{:S(2)}) collective-permute-start(bf16[32,16,128]{2,1,0:T(8,128)(2,1)S(1)} %collective-permute-done.7.refs_9_), channel_id=1, source_target_pairs={{0,7},{1,0},{2,1},{3,2},{4,3},{5,4},{6,5},{7,6},{8,15},{9,8},{10,9... | collective-permute-start | bytes 393224 | tf_op jit(solution)/shard_map/ppermute | solution.py:302
  39.8 6.2 %collective-permute-start.5 = (bf16[32,16,128]{2,1,0:T(8,128)(2,1)S(1)}, bf16[32,16,128]{2,1,0:T(8,128)(2,1)}, u32[]{:S(2)}, u32[]{:S(2)}) collective-permute-start(bf16[32,16,128]{2,1,0:T(8,128)(2,1)S(1)} %collective-permute-done.refs_7_), channel_id=1, source_target_pairs={{0,1},{1,2},{2,3},{3,4},{4,5},{5,6},{6,7},{7,0},{8,9},{9,10},{10,1... | collective-permute-start | bytes 393224 | tf_op jit(solution)/shard_map/ppermute | solution.py:304
  39.9 7.9 %collective-permute-start.12 = (bf16[32,16,128]{2,1,0:T(8,128)(2,1)S(1)}, bf16[32,16,128]{2,1,0:T(8,128)(2,1)}, u32[]{:S(2)}, u32[]{:S(2)}) collective-permute-start(bf16[32,16,128]{2,1,0:T(8,128)(2,1)S(1)} %collective-permute-done.11.refs_15_), channel_id=1, source_target_pairs={{0,1},{1,2},{2,3},{3,4},{4,5},{5,6},{6,7},{7,0},{8,9},{9,10},{10,1... | collective-permute-start | bytes 393224 | tf_op jit(solution)/shard_map/ppermute | solution.py:304
  39.9 7.9 %collective-permute-start.3 = (bf16[32,16,128]{2,1,0:T(8,128)(2,1)S(1)}, bf16[32,16,128]{2,1,0:T(8,128)(2,1)}, u32[]{:S(2)}, u32[]{:S(2)}) collective-permute-start(bf16[32,16,128]{2,1,0:T(8,128)(2,1)S(1)} %collective-permute-done.2.refs_2_), channel_id=1, source_target_pairs={{0,7},{1,0},{2,1},{3,2},{4,3},{5,4},{6,5},{7,6},{8,15},{9,8},{10,9... | collective-permute-start | bytes 393224 | tf_op jit(solution)/shard_map/ppermute | solution.py:302
  42.6 7.9 %collective-permute-start.9 = (bf16[32,16,128]{2,1,0:T(8,128)(2,1)S(1)}, bf16[32,16,128]{2,1,0:T(8,128)(2,1)}, u32[]{:S(2)}, u32[]{:S(2)}) collective-permute-start(bf16[32,16,128]{2,1,0:T(8,128)(2,1)S(1)} %collective-permute-done.8.refs_10_), channel_id=1, source_target_pairs={{0,7},{1,0},{2,1},{3,2},{4,3},{5,4},{6,5},{7,6},{8,15},{9,8},{10,9... | collective-permute-start | bytes 393224 | tf_op jit(solution)/shard_map/ppermute | solution.py:302
  46.0 7.2 %collective-permute-start.6 = (bf16[32,16,128]{2,1,0:T(8,128)(2,1)}, bf16[32,16,128]{2,1,0:T(8,128)(2,1)}, u32[]{:S(2)}, u32[]{:S(2)}) collective-permute-start(bf16[32,16,128]{2,1,0:T(8,128)(2,1)} %collective-permute-done.5.refs_6_), channel_id=1, source_target_pairs={{0,1},{1,2},{2,3},{3,4},{4,5},{5,6},{6,7},{7,0},{8,9},{9,10},{10,1... | collective-permute-start | bytes 393224 | tf_op jit(solution)/shard_map/ppermute | solution.py:304
  47.8 5.9 %collective-permute-start.13 = (bf16[32,16,128]{2,1,0:T(8,128)(2,1)}, bf16[32,16,128]{2,1,0:T(8,128)(2,1)}, u32[]{:S(2)}, u32[]{:S(2)}) collective-permute-start(bf16[32,16,128]{2,1,0:T(8,128)(2,1)} %collective-permute-done.12.refs_14_), channel_id=1, source_target_pairs={{0,1},{1,2},{2,3},{3,4},{4,5},{5,6},{6,7},{7,0},{8,9},{9,10},{10,1... | collective-permute-start | bytes 393224 | tf_op jit(solution)/shard_map/ppermute | solution.py:304
  47.8 5.9 %collective-permute-start.4 = (bf16[32,16,128]{2,1,0:T(8,128)(2,1)}, bf16[32,16,128]{2,1,0:T(8,128)(2,1)}, u32[]{:S(2)}, u32[]{:S(2)}) collective-permute-start(bf16[32,16,128]{2,1,0:T(8,128)(2,1)} %collective-permute-done.3.refs_3_), channel_id=1, source_target_pairs={{0,7},{1,0},{2,1},{3,2},{4,3},{5,4},{6,5},{7,6},{8,15},{9,8},{10,9... | collective-permute-start | bytes 393224 | tf_op jit(solution)/shard_map/ppermute | solution.py:302
  50.5 5.7 %collective-permute-start.10 = (bf16[32,16,128]{2,1,0:T(8,128)(2,1)}, bf16[32,16,128]{2,1,0:T(8,128)(2,1)}, u32[]{:S(2)}, u32[]{:S(2)}) collective-permute-start(bf16[32,16,128]{2,1,0:T(8,128)(2,1)} %collective-permute-done.9.refs_11_), channel_id=1, source_target_pairs={{0,7},{1,0},{2,1},{3,2},{4,3},{5,4},{6,5},{7,6},{8,15},{9,8},{10,9... | collective-permute-start | bytes 393224 | tf_op jit(solution)/shard_map/ppermute | solution.py:302
  58.2 27.4 %copy-start = (f32[128,2]{0,1:T(2,128)S(1)}, f32[128,2]{0,1:T(2,128)}, u32[]{:S(2)}) copy-start(f32[128,2]{0,1:T(2,128)} %param.7) | copy-start | bytes 3076

commit v7 on v6

--- a/solution.py
+++ b/solution.py
@@ -74,32 +74,41 @@
     )(weight, expand_weight, routes)
 
 
-def pack_kernel(peers, width, tokens_ref, out_ref, buf, sems):
+def pack_kernel(chips, width, tokens_ref, out_ref, buf, sems):
+    core = lax.rem(lax.axis_index("expert"), 2)
     copies = []
-    for p in range(peers):
-        copy = pltpu.make_async_copy(tokens_ref.at[:, pl.ds(p * width, width)], buf.at[p], sems.at[0, p])
-        copy.start()
-        copies.append(copy)
+    for p in range(chips):
+        pair = []
+        for h in range(2):
+            side = core if h == 0 else 1 - core
+            col = pl.multiple_of((2 * p + side) * width, LANES)
+            copy = pltpu.make_async_copy(
+                tokens_ref.at[:, pl.ds(col, width)], buf.at[p, :, pl.ds(h * width, width)], sems.at[h, p]
+            )
+            copy.start()
+            pair.append(copy)
+        copies.append(pair)
     sends = []
-    for p in range(peers):
-        copies[p].wait()
-        send = pltpu.make_async_copy(buf.at[p], out_ref.at[p], sems.at[1, p])
+    for p in range(chips):
+        for copy in copies[p]:
+            copy.wait()
+        send = pltpu.make_async_copy(buf.at[p], out_ref.at[p], sems.at[2, p])
         send.start()
         sends.append(send)
     for send in sends:
         send.wait()
 
 
-def pack(tokens, peers):
+def pack(tokens, chips):
     toks, d = tokens.shape
-    width = d // peers
-    shape = (peers, toks, width)
-    return pl.pallas_call(
-        functools.partial(pack_kernel, peers, width),
+    width = d // chips // 2
+    shape = (chips, toks, 2 * width)
+    return pl.pallas_call(
+        functools.partial(pack_kernel, chips, width),
         out_shape=jax.ShapeDtypeStruct(shape, tokens.dtype),
         in_specs=[HBM],
         out_specs=HBM,
-        scratch_shapes=[pltpu.VMEM(shape, tokens.dtype), pltpu.SemaphoreType.DMA((2, peers))],
+        scratch_shapes=[pltpu.VMEM(shape, tokens.dtype), pltpu.SemaphoreType.DMA((3, chips))],
         compiler_params=params(56),
         name="pack",
     )(tokens)
@@ -151,7 +160,8 @@
     )(*held, *more)
 
 
-def shrink_kernel(group, rank, x_ref, w_ref, r_ref, out_ref):
+def shrink_kernel(group, rank, x_ref, w_ref, r_ref, *refs):
+    *base_refs, out_ref = refs
     peers, wrows, width = w_ref.shape
     toks = x_ref.shape[1]
     chunk = max(1, 256 // wrows)
@@ -170,24 +180,35 @@
                     acc[b][k] = jnp.where(names[b][k : k + 1] == e, piece, acc[b][k])
     for b in range(group):
         for k in range(2):
-            out_ref[b, pl.ds(k * rank, rank), :] = acc[b][k].astype(out_ref.dtype)
-
-
-def shrink(tokens, weight, first, rank, group):
-    peers, toks, width = tokens.shape
+            part = acc[b][k]
+            for base in base_refs:
+                part = part + base[b, pl.ds(k * rank, rank), :]
+            out_ref[b, pl.ds(k * rank, rank), :] = part.astype(out_ref.dtype)
+
+
+def shrink(tokens, weight, names, half, base, rank, group, dtype):
+    chips, toks, width2 = tokens.shape
+    width = width2 // 2
+    sums = pl.BlockSpec((group, 2 * rank, toks), lambda i: (i, 0, 0))
     return pl.pallas_call(
         functools.partial(shrink_kernel, group, rank),
-        grid=(peers // group,),
-        out_shape=jax.ShapeDtypeStruct((peers, 2 * rank, toks), BF16),
+        grid=(chips // group,),
+        out_shape=jax.ShapeDtypeStruct((chips, 2 * rank, toks), dtype),
         in_specs=[
-            pl.BlockSpec((group, toks, width), lambda i: (i, 0, 0)),
+            pl.BlockSpec((group, toks, width), lambda i: (i, 0, half)),
             pl.BlockSpec(weight.shape, lambda i: (0, 0, 0)),
-            pl.BlockSpec((group, TILE, LANES), lambda i: (i, 2, 0)),
-        ],
-        out_specs=pl.BlockSpec((group, 2 * rank, toks), lambda i: (i, 0, 0)),
+            pl.BlockSpec((group, TILE, LANES), lambda i: (i, 0, 0)),
+        ]
+        + [sums] * len(base),
+        out_specs=sums,
         compiler_params=params(14),
+        cost_estimate=pl.CostEstimate(
+            flops=2 * chips * toks * width * weight.shape[0] * weight.shape[1],
+            bytes_accessed=2 * (chips * toks * width + weight.size),
+            transcendentals=0,
+        ),
         name="shrink",
-    )(tokens, weight, first)
+    )(tokens, weight, names, *base)
 
 
 def combine_kernel(peers, rank, part_ref, gate_ref, out_ref):
@@ -215,9 +236,10 @@
     )(part, gates)
 
 
-def expand_kernel(group, experts, s_ref, r_ref, w_ref, out_ref):
+def expand_kernel(group, experts, s_ref, r_ref, own_ref, other_ref, out_ref):
     rank = s_ref.shape[1]
     toks = s_ref.shape[2] // 2
+    feats = own_ref.shape[0]
     spread = []
     for b in range(group):
         s = s_ref[b]
@@ -230,39 +252,49 @@
             name = jnp.asarray(e, BF16)
             rows.append(jnp.where(r0 == name, s0, jnp.where(r1 == name, s1, zero)))
         spread.append(jnp.concatenate(rows, axis=0))
-    out = jnp.dot(w_ref[...], jnp.concatenate(spread, axis=1), preferred_element_type=F32)
-    for b in range(group):
-        out_ref[b] = out[:, b * toks : (b + 1) * toks].astype(BF16)
-
-
-def expand(vectors, first, weight, rank, group):
-    peers, _, toks2 = vectors.shape
+    spread = jnp.concatenate(spread, axis=1)
+    for h, w_ref in enumerate((own_ref, other_ref)):
+        out = jnp.dot(w_ref[...], spread, preferred_element_type=F32)
+        for b in range(group):
+            out_ref[b, pl.ds(h * feats, feats), :] = out[:, b * toks : (b + 1) * toks].astype(BF16)
+
+
+def expand(vectors, names, own, other, rank, group):
+    chips, _, toks2 = vectors.shape
     toks = toks2 // 2
-    feats, cols = weight.shape
+    feats, cols = own.shape
     return pl.pallas_call(
         functools.partial(expand_kernel, group, cols // rank),
-        grid=(peers // group,),
-        out_shape=jax.ShapeDtypeStruct((peers, feats, toks), BF16),
+        grid=(chips // group,),
+        out_shape=jax.ShapeDtypeStruct((chips, 2 * feats, toks), BF16),
         in_specs=[
             pl.BlockSpec((group, rank, toks2), lambda i: (i, 0, 0)),
-            pl.BlockSpec((group, TILE, LANES), lambda i: (i, 2, 0)),
-            pl.BlockSpec(weight.shape, lambda i: (0, 0)),
+            pl.BlockSpec((group, TILE, LANES), lambda i: (i, 0, 0)),
+            pl.BlockSpec(own.shape, lambda i: (0, 0)),
+            pl.BlockSpec(other.shape, lambda i: (0, 0)),
         ],
-        out_specs=pl.BlockSpec((group, feats, toks), lambda i: (i, 0, 0)),
-        compiler_params=params(20),
+        out_specs=pl.BlockSpec((group, 2 * feats, toks), lambda i: (i, 0, 0)),
+        compiler_params=params(24),
         name="expand",
-    )(vectors, first, weight)
+    )(vectors, names, own, other)
 
 
 def unpack_kernel(blocks, in_ref, out_ref, buf, sems):
-    peers, feats, toks = in_ref.shape
+    chips, feats2, toks = in_ref.shape
+    feats = feats2 // 2
     piece = feats // blocks
-    per = LANES // piece
-    cols = peers * piece
+    per = LANES // piece // 2
+    cols = 2 * chips * piece
+    core = lax.rem(lax.axis_index("expert"), 2)
     copies = []
     for z in range(blocks):
-        for q in range(peers // per):
-            parts = [in_ref[per * q + k, z * piece : (z + 1) * piece, :] for k in range(per)]
+        for q in range(chips // per):
+            parts = []
+            for k in range(per):
+                for side in range(2):
+                    half = core if side == 0 else 1 - core
+                    row = pl.multiple_of(half * feats + z * piece, piece)
+                    parts.append(in_ref[per * q + k, pl.ds(row, piece), :])
             buf[z, q] = jnp.concatenate(parts, axis=0).T
             copy = pltpu.make_async_copy(
                 buf.at[z, q], out_ref.at[:, pl.ds(z * cols + q * LANES, LANES)], sems.at[z, q]
@@ -274,11 +306,11 @@
 
 
 def unpack(buf, blocks):
-    peers, feats, toks = buf.shape
-    quads = peers * (feats // blocks) // LANES
+    chips, feats2, toks = buf.shape
+    quads = chips * (feats2 // blocks) // LANES
     return pl.pallas_call(
         functools.partial(unpack_kernel, blocks),
-        out_shape=jax.ShapeDtypeStruct((toks, peers * feats), buf.dtype),
+        out_shape=jax.ShapeDtypeStruct((toks, chips * feats2), buf.dtype),
         in_specs=[VM],
         out_specs=ANY,
         scratch_shapes=[
@@ -294,6 +326,16 @@
     return lax.all_to_all(x, "expert", split_axis=0, concat_axis=0, tiled=True)
 
 
+def swap_chips(x):
+    chips = x.shape[0]
+    groups = [[2 * q + core for q in range(chips)] for core in range(2)]
+    return lax.all_to_all(x, "expert", split_axis=0, concat_axis=0, axis_index_groups=groups, tiled=True)
+
+
+def sibling(x, peers):
+    return lax.ppermute(x, "expert", [(i, i ^ 1) for i in range(peers)])
+
+
 def ring(x, blocks):
     ahead = [(i, (i - 1) % blocks) for i in range(blocks)]
     behind = [(i, (i + 1) % blocks) for i in range(blocks)]
@@ -310,17 +352,22 @@
     peers = lax.axis_size("expert")
     blocks = lax.axis_size("tensor")
     rows = local * rank
-    group = min(8, peers)
+    chips = peers // 2
+    group = min(8, chips)
+    core = lax.rem(lax.axis_index("expert"), 2)
     first = swap(
         pack_first(shrink_weight.reshape(rows, -1), expand_weight.reshape(rows, -1), routes.T, peers, blocks)
     )
-    arrived = swap(pack(tokens, peers))
+    arrived = swap_chips(pack(tokens, chips))
+    names = first.reshape(chips, 2, 3 * TILE, LANES)[:, :, 2 * TILE :]
+    names = lax.dynamic_index_in_dim(names, core, 1, keepdims=False)
     downs, ups = ring(first[:, :TILE], blocks), ring(first[:, TILE : 2 * TILE], blocks)
-    arrived, last = lax.optimization_barrier((arrived, downs[-1]))
-    down, up = place(downs[:-1] + [last], ups, rows, features // peers)
-    partial = shrink(arrived, down, first, rank, group)
-    vectors = swap(combine(swap(partial), route_weight.T))
-    return unpack(swap(expand(vectors, first, up, rank, group)), blocks)
+    down, up = place(downs, ups, rows, features // peers)
+    other_down, other_up = sibling(down, peers), sibling(up, peers)
+    own = shrink(arrived, down, names, 0, [], rank, group, F32)
+    partial = shrink(arrived, other_down, names, 1, [own], rank, group, BF16)
+    vectors = swap_chips(combine(swap_chips(partial), route_weight.T))
+    return unpack(swap_chips(expand(vectors, names, up, other_up, rank, group)), blocks)
 
 
 def solution(mesh):

time: 140 us -> 133 us (0.950)
  the two profiles are of different devices: /device:TPU:1 before, /device:TPU:8 now
where the time goes in v7:
time: 133 us
  blocking collectives  44.3 us (33%)
  starting transfers between devices  43.5 us (33%)
  Pallas kernels  24.2 us (18%)
  waiting for transfers between devices  20.3 us (15%)
    all_to_all x2, blocking collectives, swap_chips(): lax.all_to_all(x, 'expert', split_axis=0, concat_axis=0, axis_index_group...  44.3 us
    ppermute x8, starting transfers between devices, ring(): held[step] = lax.ppermute(held[step - 1], 'tensor', ahead)  24.2 us
    all_to_all x2, starting transfers between devices, swap_chips(): lax.all_to_all(x, 'expert', split_axis=0, concat_axis=0, axis_index_group...  10.1 us
    pallas_call x2, Pallas kernels, shrink(): pl.pallas_call(functools.partial(shrink_kernel, group, rank), grid=(chips...  8.85 us
    all_to_all x1, starting transfers between devices, swap(): return lax.all_to_all(x, 'expert', split_axis=0, concat_axis=0, tiled=True)  7.55 us
    all_to_all x2, waiting for transfers between devices, swap_chips(): lax.all_to_all(x, 'expert', split_axis=0, concat_axis=0, axis_index_group...  6.98 us
    all_to_all x1, waiting for transfers between devices, swap(): return lax.all_to_all(x, 'expert', split_axis=0, concat_axis=0, tiled=True)  5.99 us
    pallas_call x1, Pallas kernels, expand(): pl.pallas_call(functools.partial(expand_kernel, group, cols // rank), gri...  5.93 us
  transfers between devices with their start and end apart: 19, of which 10 were waited for; matrix products, arithmetic and copies ran while one was open for 0% of the time, Pallas kernels for 11%

profile of v7, /device:TPU:8, one launch (start us, length us, event | category | flops | bytes accessed | tf_op | source)
XLA Modules:
  0.0 132.7 jit_solution(17375569305945024236)
XLA Ops:
  0.0 2.3 %pack_first.1 = bf16[32,48,128]{2,1,0:T(8,128)(2,1)} custom-call(bf16[64,8192]{1,0:T(8,128)(2,1)} %bitcast.11, bf16[64,1024]{1,0:T(8,128)(2,1)} %bitcast.12, s32[2,128]{1,0:T(2,128)} %bitcast.13), custom_call_target="tpu_custom_call" | custom-call | tf_op jit(solution)/shard_map/pack_first/pallas_call | solution.py:62
  2.3 7.5 %all-to-all-start.1 = ((bf16[32,48,128]{2,1,0:T(8,128)(2,1)}), bf16[32,48,128]{2,1,0:T(8,128)(2,1)S(1)}, u32[]{:S(2)}, u32[]{:S(2)}) async-start(bf16[32,48,128]{2,1,0:T(8,128)(2,1)} %pack_first.1), calls=%async_computation.1 | async-start | bytes 786432 | tf_op jit(solution)/shard_map/all_to_all | solution.py:326
  9.9 2.7 %pack.1 = bf16[16,128,512]{2,1,0:T(8,128)(2,1)} custom-call(bf16[128,8192]{1,0:T(8,128)(2,1)} %tokens_ref.1), custom_call_target="tpu_custom_call" | custom-call | tf_op jit(solution)/shard_map/pack/pallas_call | solution.py:106
  12.6 6.0 %all-to-all-done.1 = bf16[32,48,128]{2,1,0:T(8,128)(2,1)S(1)} async-done(((bf16[32,48,128]{2,1,0:T(8,128)(2,1)}), bf16[32,48,128]{2,1,0:T(8,128)(2,1)S(1)}, u32[]{:S(2)}, u32[]{:S(2)}) %all-to-all-start.1) | async-done | bytes 393248 | tf_op jit(solution)/shard_map/all_to_all | solution.py:326
  18.6 5.0 %all-to-all-start = ((bf16[16,128,512]{2,1,0:T(8,128)(2,1)}), bf16[16,128,512]{2,1,0:T(8,128)(2,1)S(1)}, u32[]{:S(2)}, u32[]{:S(2)}) async-start(bf16[16,128,512]{2,1,0:T(8,128)(2,1)} %pack.1), calls=%async_computation | async-start | bytes 4194304 | tf_op jit(solution)/shard_map/all_to_all | solution.py:332
  23.6 5.9 %collective-permute-start.7 = (bf16[32,16,128]{2,1,0:T(8,128)(2,1)S(1)}, bf16[32,16,128]{2,1,0:T(8,128)(2,1)S(1)}, u32[]{:S(2)}, u32[]{:S(2)}) collective-permute-start(bf16[32,16,128]{2,1,0:T(8,128)(2,1)S(1)} %get-tuple-element.9.refs_8_), channel_id=1, source_target_pairs={{0,7},{1,0},{2,1},{3,2},{4,3},{5,4},{6,5},{7,6},{8,15},{9,8},{10,9... | collective-permute-start | bytes 393224 | tf_op jit(solution)/shard_map/ppermute | solution.py:344
  31.6 1.8 %collective-permute-done.7.refs_9_ = bf16[32,16,128]{2,1,0:T(8,128)(2,1)S(1)} collective-permute-done((bf16[32,16,128]{2,1,0:T(8,128)(2,1)S(1)}, bf16[32,16,128]{2,1,0:T(8,128)(2,1)S(1)}, u32[]{:S(2)}, u32[]{:S(2)}) %collective-permute-start.7) | collective-permute-done | bytes 131104 | tf_op jit(solution)/shard_map/ppermute | solution.py:344
  33.4 3.7 %collective-permute-start.8 = (bf16[32,16,128]{2,1,0:T(8,128)(2,1)S(1)}, bf16[32,16,128]{2,1,0:T(8,128)(2,1)S(1)}, u32[]{:S(2)}, u32[]{:S(2)}) collective-permute-start(bf16[32,16,128]{2,1,0:T(8,128)(2,1)S(1)} %collective-permute-done.7.refs_9_), channel_id=1, source_target_pairs={{0,7},{1,0},{2,1},{3,2},{4,3},{5,4},{6,5},{7,6},{8,15},{9,8},{10,9... | collective-permute-start | bytes 393224 | tf_op jit(solution)/shard_map/ppermute | solution.py:344
  37.1 2.2 %collective-permute-start.1 = (bf16[32,16,128]{2,1,0:T(8,128)(2,1)S(1)}, bf16[32,16,128]{2,1,0:T(8,128)(2,1)S(1)}, u32[]{:S(2)}, u32[]{:S(2)}) collective-permute-start(bf16[32,16,128]{2,1,0:T(8,128)(2,1)S(1)} %collective-permute-done.refs_1_), channel_id=1, source_target_pairs={{0,7},{1,0},{2,1},{3,2},{4,3},{5,4},{6,5},{7,6},{8,15},{9,8},{10,9... | collective-permute-start | bytes 393224 | tf_op jit(solution)/shard_map/ppermute | solution.py:344
  40.2 3.7 %collective-permute-start.9 = (bf16[32,16,128]{2,1,0:T(8,128)(2,1)S(1)}, bf16[32,16,128]{2,1,0:T(8,128)(2,1)S(1)}, u32[]{:S(2)}, u32[]{:S(2)}) collective-permute-start(bf16[32,16,128]{2,1,0:T(8,128)(2,1)S(1)} %collective-permute-done.8.refs_10_), channel_id=1, source_target_pairs={{0,7},{1,0},{2,1},{3,2},{4,3},{5,4},{6,5},{7,6},{8,15},{9,8},{10,9... | collective-permute-start | bytes 393224 | tf_op jit(solution)/shard_map/ppermute | solution.py:344
  43.9 2.8 %collective-permute-start.2 = (bf16[32,16,128]{2,1,0:T(8,128)(2,1)S(1)}, bf16[32,16,128]{2,1,0:T(8,128)(2,1)S(1)}, u32[]{:S(2)}, u32[]{:S(2)}) collective-permute-start(bf16[32,16,128]{2,1,0:T(8,128)(2,1)S(1)} %collective-permute-done.1.refs_2_), channel_id=1, source_target_pairs={{0,7},{1,0},{2,1},{3,2},{4,3},{5,4},{6,5},{7,6},{8,15},{9,8},{10,9... | collective-permute-start | bytes 393224 | tf_op jit(solution)/shard_map/ppermute | solution.py:344
  48.0 3.2 %collective-permute-start.10 = (bf16[32,16,128]{2,1,0:T(8,128)(2,1)S(1)}, bf16[32,16,128]{2,1,0:T(8,128)(2,1)S(1)}, u32[]{:S(2)}, u32[]{:S(2)}) collective-permute-start(bf16[32,16,128]{2,1,0:T(8,128)(2,1)S(1)} %collective-permute-done.9.refs_11_), channel_id=1, source_target_pairs={{0,7},{1,0},{2,1},{3,2},{4,3},{5,4},{6,5},{7,6},{8,15},{9,8},{10,9... | collective-permute-start | bytes 393224 | tf_op jit(solution)/shard_map/ppermute | solution.py:344
  51.2 1.6 %collective-permute-start.3 = (bf16[32,16,128]{2,1,0:T(8,128)(2,1)S(1)}, bf16[32,16,128]{2,1,0:T(8,128)(2,1)S(1)}, u32[]{:S(2)}, u32[]{:S(2)}) collective-permute-start(bf16[32,16,128]{2,1,0:T(8,128)(2,1)S(1)} %collective-permute-done.2.refs_3_), channel_id=1, source_target_pairs={{0,7},{1,0},{2,1},{3,2},{4,3},{5,4},{6,5},{7,6},{8,15},{9,8},{10,9... | collective-permute-start | bytes 393224 | tf_op jit(solution)/shard_map/ppermute | solution.py:344
  53.0 1.4 %collective-permute-done.6.refs_5_ = bf16[32,16,128]{2,1,0:T(8,128)(2,1)S(1)} collective-permute-done((bf16[32,16,128]{2,1,0:T(8,128)(2,1)S(1)}, bf16[32,16,128]{2,1,0:T(8,128)(2,1)S(1)}, u32[]{:S(2)}, u32[]{:S(2)}) %collective-permute-start.6) | collective-permute-done | bytes 131104 | tf_op jit(solution)/shard_map/ppermute | solution.py:346
  54.5 1.7 %collective-permute-done.3.refs_4_ = bf16[32,16,128]{2,1,0:T(8,128)(2,1)S(1)} collective-permute-done((bf16[32,16,128]{2,1,0:T(8,128)(2,1)S(1)}, bf16[32,16,128]{2,1,0:T(8,128)(2,1)S(1)}, u32[]{:S(2)}, u32[]{:S(2)}) %collective-permute-start.3) | collective-permute-done | bytes 131104 | tf_op jit(solution)/shard_map/ppermute | solution.py:344
  56.2 1.7 %place.1 = (bf16[32,64,256]{2,1,0:T(8,128)(2,1)}, bf16[256,2048]{1,0:T(8,128)(2,1)S(1)}) custom-call(bf16[32,16,128]{2,1,0:T(8,128)(2,1)S(1)} %get-tuple-element.10.refs_0_, bf16[32,16,128]{2,1,0:T(8,128)(2,1)S(1)} %collective-permute-done.refs_1_, bf16[32,16,128]{2,1,0:T(8,128)(2,1)S(1)} %collective-permute-done.1.refs_2_, ...), custom_call_target="tpu_custom_call" | custom-call | tf_op jit(solution)/shard_map/place/pallas_call | solution.py:149
  58.6 4.4 %shrink.2.refs_0_ = f32[16,64,128]{2,1,0:T(8,128)S(1)} custom-call(bf16[16,128,512]{2,1,0:T(8,128)(2,1)S(1)} %all-to-all-done.x_ref, bf16[32,64,256]{2,1,0:T(8,128)(2,1)} %get-tuple-element.7.w_ref, bf16[16,16,128]{2,1,0:T(8,128)(2,1)S(1)} %dynamic-slice_bitcast_fusion.r_ref), custom_call_target="tpu_custom_call" | custom-call | flops 2147483648 | bytes 2097152 | tf_op jit(solution)/shard_map/shrink/pallas_call | solution.py:193
  63.0 4.4 %shrink.3 = bf16[16,64,128]{2,1,0:T(8,128)(2,1)S(1)} custom-call(bf16[16,128,512]{2,1,0:T(8,128)(2,1)S(1)} %all-to-all-done.x_ref, bf16[32,64,256]{2,1,0:T(8,128)(2,1)} %collective-permute-done.14.w_ref, bf16[16,16,128]{2,1,0:T(8,128)(2,1)S(1)} %dynamic-slice_bitcast_fusion.r_ref, f32[16,64,128]{2,1,0:T(8,128)S(1)} %shrink.2.refs_0_), custom_call_target="tpu_custom_call" | custom-call | flops 2147483648 | bytes 2097152 | tf_op jit(solution)/shard_map/shrink/pallas_call | solution.py:193
  67.5 14.4 %all_to_all.25.part_ref = bf16[16,64,128]{2,1,0:T(8,128)(2,1)S(1)} all-to-all(bf16[16,64,128]{2,1,0:T(8,128)(2,1)S(1)} %shrink.3), channel_id=1, replica_groups={{0,16,32,48,64,80,96,112,128,144,160,176,192,208,224,240},{8,24,40,56,7..., dimensions={0} | all-to-all | bytes 524288 | tf_op jit(solution)/shard_map/all_to_all | solution.py:332
  82.7 5.1 %all-to-all-start.3 = ((bf16[16,32,256]{2,1,0:T(8,128)(2,1)}), bf16[16,32,256]{2,1,0:T(8,128)(2,1)S(1)}, u32[]{:S(2)}, u32[]{:S(2)}) async-start(bf16[16,32,256]{2,1,0:T(8,128)(2,1)} %combine.1), calls=%async_computation.3 | async-start | bytes 524288 | tf_op jit(solution)/shard_map/all_to_all | solution.py:332
  87.7 7.0 %all-to-all-done.3.s_ref = bf16[16,32,256]{2,1,0:T(8,128)(2,1)S(1)} async-done(((bf16[16,32,256]{2,1,0:T(8,128)(2,1)}), bf16[16,32,256]{2,1,0:T(8,128)(2,1)S(1)}, u32[]{:S(2)}, u32[]{:S(2)}) %all-to-all-start.3) | async-done | bytes 262176 | tf_op jit(solution)/shard_map/all_to_all | solution.py:332
  94.7 5.9 %expand.1 = bf16[16,512,128]{2,1,0:T(8,128)(2,1)S(1)} custom-call(bf16[16,32,256]{2,1,0:T(8,128)(2,1)S(1)} %all-to-all-done.3.s_ref, bf16[16,16,128]{2,1,0:T(8,128)(2,1)S(1)} %dynamic-slice_bitcast_fusion.r_ref, bf16[256,2048]{1,0:T(8,128)(2,1)S(1)} %get-tuple-element.8.own_ref, bf16[256,2048]{1,0:T(8,128)(2,1)} %collective-permute-done.15.other_ref), custom_call_target="tpu_custom_call" | custom-call | tf_op jit(solution)/shard_map/expand/pallas_call | solution.py:266
  100.7 29.9 %all_to_all.26.in_ref = bf16[16,512,128]{2,1,0:T(8,128)(2,1)S(1)} all-to-all(bf16[16,512,128]{2,1,0:T(8,128)(2,1)S(1)} %expand.1), channel_id=1, replica_groups={{0,16,32,48,64,80,96,112,128,144,160,176,192,208,224,240},{8,24,40,56,7..., dimensions={0} | all-to-all | bytes 4194304 | tf_op jit(solution)/shard_map/all_to_all | solution.py:332
  130.6 1.9 %unpack.1 = bf16[128,8192]{1,0:T(8,128)(2,1)} custom-call(bf16[16,512,128]{2,1,0:T(8,128)(2,1)S(1)} %all_to_all.26.in_ref), custom_call_target="tpu_custom_call" | custom-call | tf_op jit(solution)/shard_map/unpack/pallas_call | solution.py:311
  (29 shorter events, 5.9 us)
Async XLA Ops:
  2.3 16.2 %all-to-all-start.1 = ((bf16[32,48,128]{2,1,0:T(8,128)(2,1)}), bf16[32,48,128]{2,1,0:T(8,128)(2,1)S(1)}, u32[]{:S(2)}, u32[]{:S(2)}) async-start(bf16[32,48,128]{2,1,0:T(8,128)(2,1)} %pack_first.1), calls=%async_computation.1 | async-start | bytes 786432 | tf_op jit(solution)/shard_map/all_to_all | solution.py:326
  18.6 40.0 %all-to-all-start = ((bf16[16,128,512]{2,1,0:T(8,128)(2,1)}), bf16[16,128,512]{2,1,0:T(8,128)(2,1)S(1)}, u32[]{:S(2)}, u32[]{:S(2)}) async-start(bf16[16,128,512]{2,1,0:T(8,128)(2,1)} %pack.1), calls=%async_computation | async-start | bytes 4194304 | tf_op jit(solution)/shard_map/all_to_all | solution.py:332
  23.6 9.8 %collective-permute-start.7 = (bf16[32,16,128]{2,1,0:T(8,128)(2,1)S(1)}, bf16[32,16,128]{2,1,0:T(8,128)(2,1)S(1)}, u32[]{:S(2)}, u32[]{:S(2)}) collective-permute-start(bf16[32,16,128]{2,1,0:T(8,128)(2,1)S(1)} %get-tuple-element.9.refs_8_), channel_id=1, source_target_pairs={{0,7},{1,0},{2,1},{3,2},{4,3},{5,4},{6,5},{7,6},{8,15},{9,8},{10,9... | collective-permute-start | bytes 393224 | tf_op jit(solution)/shard_map/ppermute | solution.py:344
  29.5 7.5 %collective-permute-start = (bf16[32,16,128]{2,1,0:T(8,128)(2,1)S(1)}, bf16[32,16,128]{2,1,0:T(8,128)(2,1)S(1)}, u32[]{:S(2)}, u32[]{:S(2)}) collective-permute-start(bf16[32,16,128]{2,1,0:T(8,128)(2,1)S(1)} %get-tuple-element.10.refs_0_), channel_id=1, source_target_pairs={{0,7},{1,0},{2,1},{3,2},{4,3},{5,4},{6,5},{7,6},{8,15},{9,8},{10,9... | collective-permute-start | bytes 393224 | tf_op jit(solution)/shard_map/ppermute | solution.py:344
  30.5 8.8 %collective-permute-start.11 = (bf16[32,16,128]{2,1,0:T(8,128)(2,1)S(1)}, bf16[32,16,128]{2,1,0:T(8,128)(2,1)S(1)}, u32[]{:S(2)}, u32[]{:S(2)}) collective-permute-start(bf16[32,16,128]{2,1,0:T(8,128)(2,1)S(1)} %get-tuple-element.9.refs_8_), channel_id=1, source_target_pairs={{0,1},{1,2},{2,3},{3,4},{4,5},{5,6},{6,7},{7,0},{8,9},{9,10},{10,1... | collective-permute-start | bytes 393224 | tf_op jit(solution)/shard_map/ppermute | solution.py:346
  31.6 8.2 %collective-permute-start.4 = (bf16[32,16,128]{2,1,0:T(8,128)(2,1)S(1)}, bf16[32,16,128]{2,1,0:T(8,128)(2,1)S(1)}, u32[]{:S(2)}, u32[]{:S(2)}) collective-permute-start(bf16[32,16,128]{2,1,0:T(8,128)(2,1)S(1)} %get-tuple-element.10.refs_0_), channel_id=1, source_target_pairs={{0,1},{1,2},{2,3},{3,4},{4,5},{5,6},{6,7},{7,0},{8,9},{9,10},{10,1... | collective-permute-start | bytes 393224 | tf_op jit(solution)/shard_map/ppermute | solution.py:346
  33.4 6.8 %collective-permute-start.8 = (bf16[32,16,128]{2,1,0:T(8,128)(2,1)S(1)}, bf16[32,16,128]{2,1,0:T(8,128)(2,1)S(1)}, u32[]{:S(2)}, u32[]{:S(2)}) collective-permute-start(bf16[32,16,128]{2,1,0:T(8,128)(2,1)S(1)} %collective-permute-done.7.refs_9_), channel_id=1, source_target_pairs={{0,7},{1,0},{2,1},{3,2},{4,3},{5,4},{6,5},{7,6},{8,15},{9,8},{10,9... | collective-permute-start | bytes 393224 | tf_op jit(solution)/shard_map/ppermute | solution.py:344
  37.1 6.8 %collective-permute-start.1 = (bf16[32,16,128]{2,1,0:T(8,128)(2,1)S(1)}, bf16[32,16,128]{2,1,0:T(8,128)(2,1)S(1)}, u32[]{:S(2)}, u32[]{:S(2)}) collective-permute-start(bf16[32,16,128]{2,1,0:T(8,128)(2,1)S(1)} %collective-permute-done.refs_1_), channel_id=1, source_target_pairs={{0,7},{1,0},{2,1},{3,2},{4,3},{5,4},{6,5},{7,6},{8,15},{9,8},{10,9... | collective-permute-start | bytes 393224 | tf_op jit(solution)/shard_map/ppermute | solution.py:344
  39.3 7.3 %collective-permute-start.12 = (bf16[32,16,128]{2,1,0:T(8,128)(2,1)S(1)}, bf16[32,16,128]{2,1,0:T(8,128)(2,1)S(1)}, u32[]{:S(2)}, u32[]{:S(2)}) collective-permute-start(bf16[32,16,128]{2,1,0:T(8,128)(2,1)S(1)} %collective-permute-done.11.refs_15_), channel_id=1, source_target_pairs={{0,1},{1,2},{2,3},{3,4},{4,5},{5,6},{6,7},{7,0},{8,9},{9,10},{10,1... | collective-permute-start | bytes 393224 | tf_op jit(solution)/shard_map/ppermute | solution.py:346
  39.7 8.2 %collective-permute-start.5 = (bf16[32,16,128]{2,1,0:T(8,128)(2,1)S(1)}, bf16[32,16,128]{2,1,0:T(8,128)(2,1)S(1)}, u32[]{:S(2)}, u32[]{:S(2)}) collective-permute-start(bf16[32,16,128]{2,1,0:T(8,128)(2,1)S(1)} %collective-permute-done.4.refs_7_), channel_id=1, source_target_pairs={{0,1},{1,2},{2,3},{3,4},{4,5},{5,6},{6,7},{7,0},{8,9},{9,10},{10,1... | collective-permute-start | bytes 393224 | tf_op jit(solution)/shard_map/ppermute | solution.py:346
  40.2 7.8 %collective-permute-start.9 = (bf16[32,16,128]{2,1,0:T(8,128)(2,1)S(1)}, bf16[32,16,128]{2,1,0:T(8,128)(2,1)S(1)}, u32[]{:S(2)}, u32[]{:S(2)}) collective-permute-start(bf16[32,16,128]{2,1,0:T(8,128)(2,1)S(1)} %collective-permute-done.8.refs_10_), channel_id=1, source_target_pairs={{0,7},{1,0},{2,1},{3,2},{4,3},{5,4},{6,5},{7,6},{8,15},{9,8},{10,9... | collective-permute-start | bytes 393224 | tf_op jit(solution)/shard_map/ppermute | solution.py:344
  43.9 7.4 %collective-permute-start.2 = (bf16[32,16,128]{2,1,0:T(8,128)(2,1)S(1)}, bf16[32,16,128]{2,1,0:T(8,128)(2,1)S(1)}, u32[]{:S(2)}, u32[]{:S(2)}) collective-permute-start(bf16[32,16,128]{2,1,0:T(8,128)(2,1)S(1)} %collective-permute-done.1.refs_2_), channel_id=1, source_target_pairs={{0,7},{1,0},{2,1},{3,2},{4,3},{5,4},{6,5},{7,6},{8,15},{9,8},{10,9... | collective-permute-start | bytes 393224 | tf_op jit(solution)/shard_map/ppermute | solution.py:344
  46.6 6.4 %collective-permute-start.13 = (bf16[32,16,128]{2,1,0:T(8,128)(2,1)S(1)}, bf16[32,16,128]{2,1,0:T(8,128)(2,1)S(1)}, u32[]{:S(2)}, u32[]{:S(2)}) collective-permute-start(bf16[32,16,128]{2,1,0:T(8,128)(2,1)S(1)} %collective-permute-done.12.refs_14_), channel_id=1, source_target_pairs={{0,1},{1,2},{2,3},{3,4},{4,5},{5,6},{6,7},{7,0},{8,9},{9,10},{10,1... | collective-permute-start | bytes 393224 | tf_op jit(solution)/shard_map/ppermute | solution.py:346
  48.0 6.4 %collective-permute-start.6 = (bf16[32,16,128]{2,1,0:T(8,128)(2,1)S(1)}, bf16[32,16,128]{2,1,0:T(8,128)(2,1)S(1)}, u32[]{:S(2)}, u32[]{:S(2)}) collective-permute-start(bf16[32,16,128]{2,1,0:T(8,128)(2,1)S(1)} %collective-permute-done.5.refs_6_), channel_id=1, source_target_pairs={{0,1},{1,2},{2,3},{3,4},{4,5},{5,6},{6,7},{7,0},{8,9},{9,10},{10,1... | collective-permute-start | bytes 393224 | tf_op jit(solution)/shard_map/ppermute | solution.py:346
  48.0 6.5 %collective-permute-start.10 = (bf16[32,16,128]{2,1,0:T(8,128)(2,1)S(1)}, bf16[32,16,128]{2,1,0:T(8,128)(2,1)S(1)}, u32[]{:S(2)}, u32[]{:S(2)}) collective-permute-start(bf16[32,16,128]{2,1,0:T(8,128)(2,1)S(1)} %collective-permute-done.9.refs_11_), channel_id=1, source_target_pairs={{0,7},{1,0},{2,1},{3,2},{4,3},{5,4},{6,5},{7,6},{8,15},{9,8},{10,9... | collective-permute-start | bytes 393224 | tf_op jit(solution)/shard_map/ppermute | solution.py:344
  51.2 5.0 %collective-permute-start.3 = (bf16[32,16,128]{2,1,0:T(8,128)(2,1)S(1)}, bf16[32,16,128]{2,1,0:T(8,128)(2,1)S(1)}, u32[]{:S(2)}, u32[]{:S(2)}) collective-permute-start(bf16[32,16,128]{2,1,0:T(8,128)(2,1)S(1)} %collective-permute-done.2.refs_3_), channel_id=1, source_target_pairs={{0,7},{1,0},{2,1},{3,2},{4,3},{5,4},{6,5},{7,6},{8,15},{9,8},{10,9... | collective-permute-start | bytes 393224 | tf_op jit(solution)/shard_map/ppermute | solution.py:344
  58.0 5.1 %collective-permute-start.14 = (bf16[32,64,256]{2,1,0:T(8,128)(2,1)}, bf16[32,64,256]{2,1,0:T(8,128)(2,1)}, u32[]{:S(2)}, u32[]{:S(2)}) collective-permute-start(bf16[32,64,256]{2,1,0:T(8,128)(2,1)} %get-tuple-element.7.w_ref), channel_id=1, source_target_pairs={{0,8},{8,0},{16,24},{24,16},{32,40},{40,32},{48,56},{56,48},{64,72... | collective-permute-start | bytes 3145736 | tf_op jit(solution)/shard_map/ppermute | solution.py:336
  58.1 29.7 %collective-permute-start.15 = (bf16[256,2048]{1,0:T(8,128)(2,1)S(1)}, bf16[256,2048]{1,0:T(8,128)(2,1)}, u32[]{:S(2)}, u32[]{:S(2)}) collective-permute-start(bf16[256,2048]{1,0:T(8,128)(2,1)S(1)} %get-tuple-element.8.own_ref), channel_id=1, source_target_pairs={{0,8},{8,0},{16,24},{24,16},{32,40},{40,32},{48,56},{56,48},{64,72... | collective-permute-start | bytes 3145736 | tf_op jit(solution)/shard_map/ppermute | solution.py:336
  63.0 18.9 %copy-start = (f32[128,2]{0,1:T(2,128)S(1)}, f32[128,2]{0,1:T(2,128)}, u32[]{:S(2)}) copy-start(f32[128,2]{0,1:T(2,128)} %param.7) | copy-start | bytes 3076
  82.7 12.1 %all-to-all-start.3 = ((bf16[16,32,256]{2,1,0:T(8,128)(2,1)}), bf16[16,32,256]{2,1,0:T(8,128)(2,1)S(1)}, u32[]{:S(2)}, u32[]{:S(2)}) async-start(bf16[16,32,256]{2,1,0:T(8,128)(2,1)} %combine.1), calls=%async_computation.3 | async-start | bytes 524288 | tf_op jit(solution)/shard_map/all_to_all | solution.py:332

commit v8 on v7

--- a/solution.py
+++ b/solution.py
@@ -336,14 +336,12 @@
     return lax.ppermute(x, "expert", [(i, i ^ 1) for i in range(peers)])
 
 
-def ring(x, blocks):
-    ahead = [(i, (i - 1) % blocks) for i in range(blocks)]
-    behind = [(i, (i + 1) % blocks) for i in range(blocks)]
+def ring(x, blocks, turn):
     held = {0: x}
     for step in range(1, blocks // 2 + 1):
-        held[step] = lax.ppermute(held[step - 1], "tensor", ahead)
-        if 2 * step < blocks:
-            held[blocks - step] = lax.ppermute(held[(blocks - step + 1) % blocks], "tensor", behind)
+        for way in (turn, -turn) if 2 * step < blocks else (turn,):
+            pairs = [(i, (i - way) % blocks) for i in range(blocks)]
+            held[way * step % blocks] = lax.ppermute(held[way * (step - 1) % blocks], "tensor", pairs)
     return [held[k] for k in range(blocks)]
 
 
@@ -361,7 +359,7 @@
     arrived = swap_chips(pack(tokens, chips))
     names = first.reshape(chips, 2, 3 * TILE, LANES)[:, :, 2 * TILE :]
     names = lax.dynamic_index_in_dim(names, core, 1, keepdims=False)
-    downs, ups = ring(first[:, :TILE], blocks), ring(first[:, TILE : 2 * TILE], blocks)
+    downs, ups = ring(first[:, :TILE], blocks, 1), ring(first[:, TILE : 2 * TILE], blocks, -1)
     down, up = place(downs, ups, rows, features // peers)
     other_down, other_up = sibling(down, peers), sibling(up, peers)
     own = shrink(arrived, down, names, 0, [], rank, group, F32)

time: 133 us -> 132 us (level); the launches traced: 133 us -> 130 us
  waiting for transfers between devices: 20.3 us -> 16.7 us
    ppermute x14, waiting for transfers between devices: 7.33 us -> 3.75 us  [ring(): lax.ppermute(held[way * (step - 1) % blocks], 'tensor', pairs)]
  transfers between devices with their start and end apart: 19 -> 19, of which waited for: 10 -> 6; matrix products, arithmetic and copies ran while one was open for 0% -> 0% of each run, Pallas kernels for 11% -> 11%
where the time goes in v8:
time: 132 us; the launch traced here: 130 us
  blocking collectives  44.5 us (34%)
  starting transfers between devices  44.1 us (33%)
  Pallas kernels  24.2 us (18%)
  waiting for transfers between devices  16.7 us (13%)
    all_to_all x2, blocking collectives, swap_chips(): lax.all_to_all(x, 'expert', split_axis=0, concat_axis=0, axis_index_group...  44.5 us
    ppermute x14, starting transfers between devices, ring(): lax.ppermute(held[way * (step - 1) % blocks], 'tensor', pairs)  25.8 us
    all_to_all x2, starting transfers between devices, swap_chips(): lax.all_to_all(x, 'expert', split_axis=0, concat_axis=0, axis_index_group...  10.1 us
    pallas_call x2, Pallas kernels, shrink(): pl.pallas_call(functools.partial(shrink_kernel, group, rank), grid=(chips...  8.85 us
    all_to_all x1, starting transfers between devices, swap(): return lax.all_to_all(x, 'expert', split_axis=0, concat_axis=0, tiled=True)  7.55 us
    all_to_all x2, waiting for transfers between devices, swap_chips(): lax.all_to_all(x, 'expert', split_axis=0, concat_axis=0, axis_index_group...  6.98 us
    all_to_all x1, waiting for transfers between devices, swap(): return lax.all_to_all(x, 'expert', split_axis=0, concat_axis=0, tiled=True)  5.99 us
    pallas_call x1, Pallas kernels, expand(): pl.pallas_call(functools.partial(expand_kernel, group, cols // rank), gri...  5.93 us
  transfers between devices with their start and end apart: 19, of which 6 were waited for; matrix products, arithmetic and copies ran while one was open for 0% of the time, Pallas kernels for 11%

profile of v8, /device:TPU:8, one launch (start us, length us, event | category | flops | bytes accessed | tf_op | source)
XLA Modules:
  0.0 129.8 jit_solution(12733041338820527657)
XLA Ops:
  0.0 2.3 %pack_first.1 = bf16[32,48,128]{2,1,0:T(8,128)(2,1)} custom-call(bf16[64,8192]{1,0:T(8,128)(2,1)} %bitcast.11, bf16[64,1024]{1,0:T(8,128)(2,1)} %bitcast.12, s32[2,128]{1,0:T(2,128)} %bitcast.13), custom_call_target="tpu_custom_call" | custom-call | tf_op jit(solution)/shard_map/pack_first/pallas_call | solution.py:62
  2.3 7.5 %all-to-all-start.1 = ((bf16[32,48,128]{2,1,0:T(8,128)(2,1)}), bf16[32,48,128]{2,1,0:T(8,128)(2,1)S(1)}, u32[]{:S(2)}, u32[]{:S(2)}) async-start(bf16[32,48,128]{2,1,0:T(8,128)(2,1)} %pack_first.1), calls=%async_computation.1 | async-start | bytes 786432 | tf_op jit(solution)/shard_map/all_to_all | solution.py:326
  9.9 2.7 %pack.1 = bf16[16,128,512]{2,1,0:T(8,128)(2,1)} custom-call(bf16[128,8192]{1,0:T(8,128)(2,1)} %tokens_ref.1), custom_call_target="tpu_custom_call" | custom-call | tf_op jit(solution)/shard_map/pack/pallas_call | solution.py:106
  12.6 6.0 %all-to-all-done.1 = bf16[32,48,128]{2,1,0:T(8,128)(2,1)S(1)} async-done(((bf16[32,48,128]{2,1,0:T(8,128)(2,1)}), bf16[32,48,128]{2,1,0:T(8,128)(2,1)S(1)}, u32[]{:S(2)}, u32[]{:S(2)}) %all-to-all-start.1) | async-done | bytes 393248 | tf_op jit(solution)/shard_map/all_to_all | solution.py:326
  18.6 5.0 %all-to-all-start = ((bf16[16,128,512]{2,1,0:T(8,128)(2,1)}), bf16[16,128,512]{2,1,0:T(8,128)(2,1)S(1)}, u32[]{:S(2)}, u32[]{:S(2)}) async-start(bf16[16,128,512]{2,1,0:T(8,128)(2,1)} %pack.1), calls=%async_computation | async-start | bytes 4194304 | tf_op jit(solution)/shard_map/all_to_all | solution.py:332
  23.6 2.0 %collective-permute-start.10 = (bf16[32,16,128]{2,1,0:T(8,128)(2,1)S(1)}, bf16[32,16,128]{2,1,0:T(8,128)(2,1)S(1)}, u32[]{:S(2)}, u32[]{:S(2)}) collective-permute-start(bf16[32,16,128]{2,1,0:T(8,128)(2,1)S(1)} %get-tuple-element.9.refs_8_), channel_id=1, source_target_pairs={{0,1},{1,2},{2,3},{3,4},{4,5},{5,6},{6,7},{7,0},{8,9},{9,10},{10,1... | collective-permute-start | bytes 393224 | tf_op jit(solution)/shard_map/ppermute | solution.py:344
  25.6 4.0 %collective-permute-start = (bf16[32,16,128]{2,1,0:T(8,128)(2,1)S(1)}, bf16[32,16,128]{2,1,0:T(8,128)(2,1)S(1)}, u32[]{:S(2)}, u32[]{:S(2)}) collective-permute-start(bf16[32,16,128]{2,1,0:T(8,128)(2,1)S(1)} %get-tuple-element.10.refs_0_), channel_id=1, source_target_pairs={{0,7},{1,0},{2,1},{3,2},{4,3},{5,4},{6,5},{7,6},{8,15},{9,8},{10,9... | collective-permute-start | bytes 393224 | tf_op jit(solution)/shard_map/ppermute | solution.py:344
  29.6 3.2 %collective-permute-start.7 = (bf16[32,16,128]{2,1,0:T(8,128)(2,1)S(1)}, bf16[32,16,128]{2,1,0:T(8,128)(2,1)S(1)}, u32[]{:S(2)}, u32[]{:S(2)}) collective-permute-start(bf16[32,16,128]{2,1,0:T(8,128)(2,1)S(1)} %get-tuple-element.9.refs_8_), channel_id=1, source_target_pairs={{0,7},{1,0},{2,1},{3,2},{4,3},{5,4},{6,5},{7,6},{8,15},{9,8},{10,9... | collective-permute-start | bytes 393224 | tf_op jit(solution)/shard_map/ppermute | solution.py:344
  33.5 3.2 %collective-permute-start.1 = (bf16[32,16,128]{2,1,0:T(8,128)(2,1)S(1)}, bf16[32,16,128]{2,1,0:T(8,128)(2,1)S(1)}, u32[]{:S(2)}, u32[]{:S(2)}) collective-permute-start(bf16[32,16,128]{2,1,0:T(8,128)(2,1)S(1)} %collective-permute-done.refs_1_), channel_id=1, source_target_pairs={{0,7},{1,0},{2,1},{3,2},{4,3},{5,4},{6,5},{7,6},{8,15},{9,8},{10,9... | collective-permute-start | bytes 393224 | tf_op jit(solution)/shard_map/ppermute | solution.py:344
  36.8 3.2 %collective-permute-start.8 = (bf16[32,16,128]{2,1,0:T(8,128)(2,1)S(1)}, bf16[32,16,128]{2,1,0:T(8,128)(2,1)S(1)}, u32[]{:S(2)}, u32[]{:S(2)}) collective-permute-start(bf16[32,16,128]{2,1,0:T(8,128)(2,1)S(1)} %collective-permute-done.7.refs_9_), channel_id=1, source_target_pairs={{0,7},{1,0},{2,1},{3,2},{4,3},{5,4},{6,5},{7,6},{8,15},{9,8},{10,9... | collective-permute-start | bytes 393224 | tf_op jit(solution)/shard_map/ppermute | solution.py:344
  40.1 3.2 %collective-permute-start.2 = (bf16[32,16,128]{2,1,0:T(8,128)(2,1)S(1)}, bf16[32,16,128]{2,1,0:T(8,128)(2,1)S(1)}, u32[]{:S(2)}, u32[]{:S(2)}) collective-permute-start(bf16[32,16,128]{2,1,0:T(8,128)(2,1)S(1)} %collective-permute-done.1.refs_2_), channel_id=1, source_target_pairs={{0,7},{1,0},{2,1},{3,2},{4,3},{5,4},{6,5},{7,6},{8,15},{9,8},{10,9... | collective-permute-start | bytes 393224 | tf_op jit(solution)/shard_map/ppermute | solution.py:344
  43.3 3.3 %collective-permute-start.9 = (bf16[32,16,128]{2,1,0:T(8,128)(2,1)S(1)}, bf16[32,16,128]{2,1,0:T(8,128)(2,1)S(1)}, u32[]{:S(2)}, u32[]{:S(2)}) collective-permute-start(bf16[32,16,128]{2,1,0:T(8,128)(2,1)S(1)} %collective-permute-done.8.refs_10_), channel_id=1, source_target_pairs={{0,7},{1,0},{2,1},{3,2},{4,3},{5,4},{6,5},{7,6},{8,15},{9,8},{10,9... | collective-permute-start | bytes 393224 | tf_op jit(solution)/shard_map/ppermute | solution.py:344
  47.1 3.6 %collective-permute-start.3 = (bf16[32,16,128]{2,1,0:T(8,128)(2,1)S(1)}, bf16[32,16,128]{2,1,0:T(8,128)(2,1)S(1)}, u32[]{:S(2)}, u32[]{:S(2)}) collective-permute-start(bf16[32,16,128]{2,1,0:T(8,128)(2,1)S(1)} %collective-permute-done.2.refs_3_), channel_id=1, source_target_pairs={{0,7},{1,0},{2,1},{3,2},{4,3},{5,4},{6,5},{7,6},{8,15},{9,8},{10,9... | collective-permute-start | bytes 393224 | tf_op jit(solution)/shard_map/ppermute | solution.py:344
  50.7 2.5 %collective-permute-done.13.refs_12_ = bf16[32,16,128]{2,1,0:T(8,128)(2,1)S(1)} collective-permute-done((bf16[32,16,128]{2,1,0:T(8,128)(2,1)S(1)}, bf16[32,16,128]{2,1,0:T(8,128)(2,1)S(1)}, u32[]{:S(2)}, u32[]{:S(2)}) %collective-permute-start.13) | collective-permute-done | bytes 131104 | tf_op jit(solution)/shard_map/ppermute | solution.py:344
  53.2 1.8 %place.1 = (bf16[32,64,256]{2,1,0:T(8,128)(2,1)}, bf16[256,2048]{1,0:T(8,128)(2,1)S(1)}) custom-call(bf16[32,16,128]{2,1,0:T(8,128)(2,1)S(1)} %get-tuple-element.10.refs_0_, bf16[32,16,128]{2,1,0:T(8,128)(2,1)S(1)} %collective-permute-done.refs_1_, bf16[32,16,128]{2,1,0:T(8,128)(2,1)S(1)} %collective-permute-done.1.refs_2_, ...), custom_call_target="tpu_custom_call" | custom-call | tf_op jit(solution)/shard_map/place/pallas_call | solution.py:149
  55.6 4.4 %shrink.2.refs_0_ = f32[16,64,128]{2,1,0:T(8,128)S(1)} custom-call(bf16[16,128,512]{2,1,0:T(8,128)(2,1)S(1)} %all-to-all-done.x_ref, bf16[32,64,256]{2,1,0:T(8,128)(2,1)} %get-tuple-element.7.w_ref, bf16[16,16,128]{2,1,0:T(8,128)(2,1)S(1)} %dynamic-slice_bitcast_fusion.r_ref), custom_call_target="tpu_custom_call" | custom-call | flops 2147483648 | bytes 2097152 | tf_op jit(solution)/shard_map/shrink/pallas_call | solution.py:193
  60.1 4.4 %shrink.3 = bf16[16,64,128]{2,1,0:T(8,128)(2,1)S(1)} custom-call(bf16[16,128,512]{2,1,0:T(8,128)(2,1)S(1)} %all-to-all-done.x_ref, bf16[32,64,256]{2,1,0:T(8,128)(2,1)} %collective-permute-done.14.w_ref, bf16[16,16,128]{2,1,0:T(8,128)(2,1)S(1)} %dynamic-slice_bitcast_fusion.r_ref, f32[16,64,128]{2,1,0:T(8,128)S(1)} %shrink.2.refs_0_), custom_call_target="tpu_custom_call" | custom-call | flops 2147483648 | bytes 2097152 | tf_op jit(solution)/shard_map/shrink/pallas_call | solution.py:193
  64.5 14.5 %all_to_all.25.part_ref = bf16[16,64,128]{2,1,0:T(8,128)(2,1)S(1)} all-to-all(bf16[16,64,128]{2,1,0:T(8,128)(2,1)S(1)} %shrink.3), channel_id=1, replica_groups={{0,16,32,48,64,80,96,112,128,144,160,176,192,208,224,240},{8,24,40,56,7..., dimensions={0} | all-to-all | bytes 524288 | tf_op jit(solution)/shard_map/all_to_all | solution.py:332
  79.1 0.8 combine.1
  79.8 5.1 %all-to-all-start.3 = ((bf16[16,32,256]{2,1,0:T(8,128)(2,1)}), bf16[16,32,256]{2,1,0:T(8,128)(2,1)S(1)}, u32[]{:S(2)}, u32[]{:S(2)}) async-start(bf16[16,32,256]{2,1,0:T(8,128)(2,1)} %combine.1), calls=%async_computation.3 | async-start | bytes 524288 | tf_op jit(solution)/shard_map/all_to_all | solution.py:332
  84.9 7.0 %all-to-all-done.3.s_ref = bf16[16,32,256]{2,1,0:T(8,128)(2,1)S(1)} async-done(((bf16[16,32,256]{2,1,0:T(8,128)(2,1)}), bf16[16,32,256]{2,1,0:T(8,128)(2,1)S(1)}, u32[]{:S(2)}, u32[]{:S(2)}) %all-to-all-start.3) | async-done | bytes 262176 | tf_op jit(solution)/shard_map/all_to_all | solution.py:332
  91.9 5.9 %expand.1 = bf16[16,512,128]{2,1,0:T(8,128)(2,1)S(1)} custom-call(bf16[16,32,256]{2,1,0:T(8,128)(2,1)S(1)} %all-to-all-done.3.s_ref, bf16[16,16,128]{2,1,0:T(8,128)(2,1)S(1)} %dynamic-slice_bitcast_fusion.r_ref, bf16[256,2048]{1,0:T(8,128)(2,1)S(1)} %get-tuple-element.8.own_ref, bf16[256,2048]{1,0:T(8,128)(2,1)} %collective-permute-done.15.other_ref), custom_call_target="tpu_custom_call" | custom-call | tf_op jit(solution)/shard_map/expand/pallas_call | solution.py:266
  97.8 29.9 %all_to_all.26.in_ref = bf16[16,512,128]{2,1,0:T(8,128)(2,1)S(1)} all-to-all(bf16[16,512,128]{2,1,0:T(8,128)(2,1)S(1)} %expand.1), channel_id=1, replica_groups={{0,16,32,48,64,80,96,112,128,144,160,176,192,208,224,240},{8,24,40,56,7..., dimensions={0} | all-to-all | bytes 4194304 | tf_op jit(solution)/shard_map/all_to_all | solution.py:332
  127.7 1.9 %unpack.1 = bf16[128,8192]{1,0:T(8,128)(2,1)} custom-call(bf16[16,512,128]{2,1,0:T(8,128)(2,1)S(1)} %all_to_all.26.in_ref), custom_call_target="tpu_custom_call" | custom-call | tf_op jit(solution)/shard_map/unpack/pallas_call | solution.py:311
  (29 shorter events, 1.9 us)
Async XLA Ops:
  2.3 16.2 %all-to-all-start.1 = ((bf16[32,48,128]{2,1,0:T(8,128)(2,1)}), bf16[32,48,128]{2,1,0:T(8,128)(2,1)S(1)}, u32[]{:S(2)}, u32[]{:S(2)}) async-start(bf16[32,48,128]{2,1,0:T(8,128)(2,1)} %pack_first.1), calls=%async_computation.1 | async-start | bytes 786432 | tf_op jit(solution)/shard_map/all_to_all | solution.py:326
  18.6 37.1 %all-to-all-start = ((bf16[16,128,512]{2,1,0:T(8,128)(2,1)}), bf16[16,128,512]{2,1,0:T(8,128)(2,1)S(1)}, u32[]{:S(2)}, u32[]{:S(2)}) async-start(bf16[16,128,512]{2,1,0:T(8,128)(2,1)} %pack.1), calls=%async_computation | async-start | bytes 4194304 | tf_op jit(solution)/shard_map/all_to_all | solution.py:332
  23.6 9.9 %collective-permute-start.10 = (bf16[32,16,128]{2,1,0:T(8,128)(2,1)S(1)}, bf16[32,16,128]{2,1,0:T(8,128)(2,1)S(1)}, u32[]{:S(2)}, u32[]{:S(2)}) collective-permute-start(bf16[32,16,128]{2,1,0:T(8,128)(2,1)S(1)} %get-tuple-element.9.refs_8_), channel_id=1, source_target_pairs={{0,1},{1,2},{2,3},{3,4},{4,5},{5,6},{6,7},{7,0},{8,9},{9,10},{10,1... | collective-permute-start | bytes 393224 | tf_op jit(solution)/shard_map/ppermute | solution.py:344
  25.6 7.9 %collective-permute-start = (bf16[32,16,128]{2,1,0:T(8,128)(2,1)S(1)}, bf16[32,16,128]{2,1,0:T(8,128)(2,1)S(1)}, u32[]{:S(2)}, u32[]{:S(2)}) collective-permute-start(bf16[32,16,128]{2,1,0:T(8,128)(2,1)S(1)} %get-tuple-element.10.refs_0_), channel_id=1, source_target_pairs={{0,7},{1,0},{2,1},{3,2},{4,3},{5,4},{6,5},{7,6},{8,15},{9,8},{10,9... | collective-permute-start | bytes 393224 | tf_op jit(solution)/shard_map/ppermute | solution.py:344
  29.6 7.2 %collective-permute-start.4 = (bf16[32,16,128]{2,1,0:T(8,128)(2,1)S(1)}, bf16[32,16,128]{2,1,0:T(8,128)(2,1)S(1)}, u32[]{:S(2)}, u32[]{:S(2)}) collective-permute-start(bf16[32,16,128]{2,1,0:T(8,128)(2,1)S(1)} %get-tuple-element.10.refs_0_), channel_id=1, source_target_pairs={{0,1},{1,2},{2,3},{3,4},{4,5},{5,6},{6,7},{7,0},{8,9},{9,10},{10,1... | collective-permute-start | bytes 393224 | tf_op jit(solution)/shard_map/ppermute | solution.py:344
  29.6 7.2 %collective-permute-start.7 = (bf16[32,16,128]{2,1,0:T(8,128)(2,1)S(1)}, bf16[32,16,128]{2,1,0:T(8,128)(2,1)S(1)}, u32[]{:S(2)}, u32[]{:S(2)}) collective-permute-start(bf16[32,16,128]{2,1,0:T(8,128)(2,1)S(1)} %get-tuple-element.9.refs_8_), channel_id=1, source_target_pairs={{0,7},{1,0},{2,1},{3,2},{4,3},{5,4},{6,5},{7,6},{8,15},{9,8},{10,9... | collective-permute-start | bytes 393224 | tf_op jit(solution)/shard_map/ppermute | solution.py:344
  33.5 6.5 %collective-permute-start.11 = (bf16[32,16,128]{2,1,0:T(8,128)(2,1)S(1)}, bf16[32,16,128]{2,1,0:T(8,128)(2,1)S(1)}, u32[]{:S(2)}, u32[]{:S(2)}) collective-permute-start(bf16[32,16,128]{2,1,0:T(8,128)(2,1)S(1)} %collective-permute-done.10.refs_15_), channel_id=1, source_target_pairs={{0,1},{1,2},{2,3},{3,4},{4,5},{5,6},{6,7},{7,0},{8,9},{9,10},{10,1... | collective-permute-start | bytes 393224 | tf_op jit(solution)/shard_map/ppermute | solution.py:344
  33.5 6.5 %collective-permute-start.1 = (bf16[32,16,128]{2,1,0:T(8,128)(2,1)S(1)}, bf16[32,16,128]{2,1,0:T(8,128)(2,1)S(1)}, u32[]{:S(2)}, u32[]{:S(2)}) collective-permute-start(bf16[32,16,128]{2,1,0:T(8,128)(2,1)S(1)} %collective-permute-done.refs_1_), channel_id=1, source_target_pairs={{0,7},{1,0},{2,1},{3,2},{4,3},{5,4},{6,5},{7,6},{8,15},{9,8},{10,9... | collective-permute-start | bytes 393224 | tf_op jit(solution)/shard_map/ppermute | solution.py:344
  36.8 6.5 %collective-permute-start.5 = (bf16[32,16,128]{2,1,0:T(8,128)(2,1)S(1)}, bf16[32,16,128]{2,1,0:T(8,128)(2,1)S(1)}, u32[]{:S(2)}, u32[]{:S(2)}) collective-permute-start(bf16[32,16,128]{2,1,0:T(8,128)(2,1)S(1)} %collective-permute-done.4.refs_7_), channel_id=1, source_target_pairs={{0,1},{1,2},{2,3},{3,4},{4,5},{5,6},{6,7},{7,0},{8,9},{9,10},{10,1... | collective-permute-start | bytes 393224 | tf_op jit(solution)/shard_map/ppermute | solution.py:344
  36.8 6.5 %collective-permute-start.8 = (bf16[32,16,128]{2,1,0:T(8,128)(2,1)S(1)}, bf16[32,16,128]{2,1,0:T(8,128)(2,1)S(1)}, u32[]{:S(2)}, u32[]{:S(2)}) collective-permute-start(bf16[32,16,128]{2,1,0:T(8,128)(2,1)S(1)} %collective-permute-done.7.refs_9_), channel_id=1, source_target_pairs={{0,7},{1,0},{2,1},{3,2},{4,3},{5,4},{6,5},{7,6},{8,15},{9,8},{10,9... | collective-permute-start | bytes 393224 | tf_op jit(solution)/shard_map/ppermute | solution.py:344
  40.1 7.0 %collective-permute-start.12 = (bf16[32,16,128]{2,1,0:T(8,128)(2,1)S(1)}, bf16[32,16,128]{2,1,0:T(8,128)(2,1)S(1)}, u32[]{:S(2)}, u32[]{:S(2)}) collective-permute-start(bf16[32,16,128]{2,1,0:T(8,128)(2,1)S(1)} %collective-permute-done.11.refs_14_), channel_id=1, source_target_pairs={{0,1},{1,2},{2,3},{3,4},{4,5},{5,6},{6,7},{7,0},{8,9},{9,10},{10,1... | collective-permute-start | bytes 393224 | tf_op jit(solution)/shard_map/ppermute | solution.py:344
  40.1 7.0 %collective-permute-start.2 = (bf16[32,16,128]{2,1,0:T(8,128)(2,1)S(1)}, bf16[32,16,128]{2,1,0:T(8,128)(2,1)S(1)}, u32[]{:S(2)}, u32[]{:S(2)}) collective-permute-start(bf16[32,16,128]{2,1,0:T(8,128)(2,1)S(1)} %collective-permute-done.1.refs_2_), channel_id=1, source_target_pairs={{0,7},{1,0},{2,1},{3,2},{4,3},{5,4},{6,5},{7,6},{8,15},{9,8},{10,9... | collective-permute-start | bytes 393224 | tf_op jit(solution)/shard_map/ppermute | solution.py:344
  43.3 7.4 %collective-permute-start.6 = (bf16[32,16,128]{2,1,0:T(8,128)(2,1)S(1)}, bf16[32,16,128]{2,1,0:T(8,128)(2,1)S(1)}, u32[]{:S(2)}, u32[]{:S(2)}) collective-permute-start(bf16[32,16,128]{2,1,0:T(8,128)(2,1)S(1)} %collective-permute-done.5.refs_6_), channel_id=1, source_target_pairs={{0,1},{1,2},{2,3},{3,4},{4,5},{5,6},{6,7},{7,0},{8,9},{9,10},{10,1... | collective-permute-start | bytes 393224 | tf_op jit(solution)/shard_map/ppermute | solution.py:344
  43.3 7.4 %collective-permute-start.9 = (bf16[32,16,128]{2,1,0:T(8,128)(2,1)S(1)}, bf16[32,16,128]{2,1,0:T(8,128)(2,1)S(1)}, u32[]{:S(2)}, u32[]{:S(2)}) collective-permute-start(bf16[32,16,128]{2,1,0:T(8,128)(2,1)S(1)} %collective-permute-done.8.refs_10_), channel_id=1, source_target_pairs={{0,7},{1,0},{2,1},{3,2},{4,3},{5,4},{6,5},{7,6},{8,15},{9,8},{10,9... | collective-permute-start | bytes 393224 | tf_op jit(solution)/shard_map/ppermute | solution.py:344
  47.0 6.2 %collective-permute-start.13 = (bf16[32,16,128]{2,1,0:T(8,128)(2,1)S(1)}, bf16[32,16,128]{2,1,0:T(8,128)(2,1)S(1)}, u32[]{:S(2)}, u32[]{:S(2)}) collective-permute-start(bf16[32,16,128]{2,1,0:T(8,128)(2,1)S(1)} %collective-permute-done.12.refs_13_), channel_id=1, source_target_pairs={{0,1},{1,2},{2,3},{3,4},{4,5},{5,6},{6,7},{7,0},{8,9},{9,10},{10,1... | collective-permute-start | bytes 393224 | tf_op jit(solution)/shard_map/ppermute | solution.py:344
  47.1 6.2 %collective-permute-start.3 = (bf16[32,16,128]{2,1,0:T(8,128)(2,1)S(1)}, bf16[32,16,128]{2,1,0:T(8,128)(2,1)S(1)}, u32[]{:S(2)}, u32[]{:S(2)}) collective-permute-start(bf16[32,16,128]{2,1,0:T(8,128)(2,1)S(1)} %collective-permute-done.2.refs_3_), channel_id=1, source_target_pairs={{0,7},{1,0},{2,1},{3,2},{4,3},{5,4},{6,5},{7,6},{8,15},{9,8},{10,9... | collective-permute-start | bytes 393224 | tf_op jit(solution)/shard_map/ppermute | solution.py:344
  55.0 5.1 %collective-permute-start.14 = (bf16[32,64,256]{2,1,0:T(8,128)(2,1)}, bf16[32,64,256]{2,1,0:T(8,128)(2,1)}, u32[]{:S(2)}, u32[]{:S(2)}) collective-permute-start(bf16[32,64,256]{2,1,0:T(8,128)(2,1)} %get-tuple-element.7.w_ref), channel_id=1, source_target_pairs={{0,8},{8,0},{16,24},{24,16},{32,40},{40,32},{48,56},{56,48},{64,72... | collective-permute-start | bytes 3145736 | tf_op jit(solution)/shard_map/ppermute | solution.py:336
  55.1 29.8 %collective-permute-start.15 = (bf16[256,2048]{1,0:T(8,128)(2,1)S(1)}, bf16[256,2048]{1,0:T(8,128)(2,1)}, u32[]{:S(2)}, u32[]{:S(2)}) collective-permute-start(bf16[256,2048]{1,0:T(8,128)(2,1)S(1)} %get-tuple-element.8.own_ref), channel_id=1, source_target_pairs={{0,8},{8,0},{16,24},{24,16},{32,40},{40,32},{48,56},{56,48},{64,72... | collective-permute-start | bytes 3145736 | tf_op jit(solution)/shard_map/ppermute | solution.py:336
  60.0 19.0 %copy-start = (f32[128,2]{0,1:T(2,128)S(1)}, f32[128,2]{0,1:T(2,128)}, u32[]{:S(2)}) copy-start(f32[128,2]{0,1:T(2,128)} %param.7) | copy-start | bytes 3076
  79.8 12.0 %all-to-all-start.3 = ((bf16[16,32,256]{2,1,0:T(8,128)(2,1)}), bf16[16,32,256]{2,1,0:T(8,128)(2,1)S(1)}, u32[]{:S(2)}, u32[]{:S(2)}) async-start(bf16[16,32,256]{2,1,0:T(8,128)(2,1)} %combine.1), calls=%async_computation.3 | async-start | bytes 524288 | tf_op jit(solution)/shard_map/all_to_all | solution.py:332
